TPU v7x, 32 devices: a whole 2x2x4 slice. The times are simulated.
32 devices in a mesh: seq: 8 (over y, x, core), res: 4 (over z).
Axes of the slice: x: 2, y: 2, z: 4, core: 2. Of those that a mesh axis runs over, the one named last changes fastest.
Arguments:
- alignment_embedding: bfloat16 [32, 256, 256], P('seq', 'res'), may hold values from -6 to 6
- coupling_embedding: bfloat16 [256, 256, 128], P('seq', 'res'), may hold values from -6 to 6
- vertex_embedding: float32 [256, 64], replicated, may hold values from -6 to 6
- atom_locations: float32 [3, 256], replicated, may hold values from -6 to 6
- chain_existence_flags: int32 [32], replicated, may hold values from 0 to 1
- closest_aminos: int32 [256, 64], P('seq'), may hold values from 0 to 255, all different within a row
- softmax_mixer_scale_factor: float32 [256], replicated, may hold values from 0.1 to 1.9
- attender_stacked_matrix: bfloat16 [256, 1024], replicated, may hold values from -0.375 to 0.375
- softmax_mixer_exit_matrix: bfloat16 [256, 256], replicated, may hold values from -1.5 to 1.5
- tensor_mean_scale_factor: float32 [256], replicated, may hold values from 0.1 to 1.9
- tensor_mean_entry_matrix: bfloat16 [256, 64], replicated, may hold values from -0.375 to 0.375
- tensor_mean_exit_matrix: bfloat16 [1024, 128], replicated, may hold values from -0.5 to 0.5
- outbound_entry_scale: float32 [128], replicated, may hold values from 0.1 to 1.9
- outbound_entry_matrix: bfloat16 [128, 640], replicated, may hold values from -0.5 to 0.5
- outbound_exit_scale: float32 [128], replicated, may hold values from 0.1 to 1.9
- outbound_exit_matrix: bfloat16 [128, 128], replicated, may hold values from -0.5 to 0.5
- inbound_entry_scale: float32 [128], replicated, may hold values from 0.1 to 1.9
- inbound_entry_matrix: bfloat16 [128, 640], replicated, may hold values from -0.5 to 0.5
- inbound_exit_scale: float32 [128], replicated, may hold values from 0.1 to 1.9
- inbound_exit_matrix: bfloat16 [128, 128], replicated, may hold values from -0.5 to 0.5
- vertex_mapping_matrix: bfloat16 [64, 128], replicated, may hold values from -0.75 to 0.75
- bond_mapping_matrix: bfloat16 [128, 64], replicated, may hold values from -0.5 to 0.5
- distance_basis_matrix: float32 [64], replicated, may hold values from -3 to 3
- signal_matrix: bfloat16 [64, 64], replicated, may hold values from -0.75 to 0.75
- signal_location_matrix: float32 [64], replicated, may hold values from -1.5 to 1.5
- vertex_change_matrix: bfloat16 [64, 64], replicated, may hold values from -0.75 to 0.75
- alignment_adjoint: bfloat16 [32, 256, 256], P('seq', 'res'), may hold values from -6 to 6
- coupling_adjoint: bfloat16 [256, 256, 128], P('seq', 'res'), may hold values from -6 to 6
- vertex_adjoint: float32 [256, 64], P('seq'), may hold values from -6 to 6
- location_adjoint: float32 [3, 256], P(None, 'seq'), may hold values from -6 to 6
Outputs:
- msa_out: bfloat16 [32, 256, 256], P('seq', 'res')
- pair_out: bfloat16 [256, 256, 128], P('seq', 'res')
- single_out: float32 [256, 64], P('seq')
- coords_out: float32 [3, 256], P(None, 'seq')
- alignment_sensitivity: float32 [32, 256, 256], P('seq', 'res')
- pair_grad: float32 [256, 256, 128], P('seq', 'res')
- single_grad: float32 [256, 64], P('seq')
- coords_grad: float32 [3, 256], P(None, 'seq')
- msa_gain_grad: float32 [256], replicated
- w_qkvg_grad: float32 [256, 1024], replicated
- w_attn_out_grad: float32 [256, 256], replicated
- opm_gain_grad: float32 [256], replicated
- w_opm_in_grad: float32 [256, 64], replicated
- w_opm_out_grad: float32 [1024, 128], replicated
- tri_gain_grad: float32 [128], replicated
- w_tri_in_grad: float32 [128, 640], replicated
- tri_out_gain_grad: float32 [128], replicated
- w_tri_out_grad: float32 [128, 128], replicated
- inc_gain_grad: float32 [128], replicated
- w_inc_in_grad: float32 [128, 640], replicated
- inc_out_gain_grad: float32 [128], replicated
- w_inc_out_grad: float32 [128, 128], replicated
- w_node_grad: float32 [64, 128], replicated
- w_edge_grad: float32 [128, 64], replicated
- dist_weight_grad: float32 [64], replicated
- w_msg_grad: float32 [64, 64], replicated
- coord_weight_grad: float32 [64], replicated
- w_update_grad: float32 [64, 64], replicated
Inputs may be any that keep to these rules, and one draw needn't show every extreme that they name: `closest_aminos`: each row names 64 different residues.
All inputs are finite; a program needn't handle non-finite values.
Results may differ from a plain program's by a relative error of at most 0.03.
Values may be sent and summed in bfloat16 or wider, within the bound.
A program may use at most 192 MiB of HBM per device.

v0:
```python
import jax
import jax.numpy as jnp
from jax import lax
from jax.sharding import PartitionSpec as P

HEADS = 8


EPS = 1e-05
HIGH = lax.Precision.HIGHEST


def spread_2(value, axis, source):
    kept = jnp.where(lax.axis_index(axis) == source, value, 0).astype(value.dtype)
    return lax.psum(kept, axis)


def standardize_lines(value, gain):
    row_mean = jnp.mean(value, -1, keepdims=True)
    centred = value - row_mean
    spread = jnp.mean(centred * centred, -1, keepdims=True)
    return centred * lax.rsqrt(spread + EPS) * gain


def tensor_mean_answer(left, right):
    return jnp.einsum("...c,cd->...d", left, right, preferred_element_type=jnp.float32)


def product_back(grad, right):
    return jnp.einsum("...d,cd->...c", grad, right, preferred_element_type=jnp.float32)


def weight_back(left, grad):
    flat_left = left.reshape(-1, left.shape[-1])
    flat_grad = grad.reshape(-1, grad.shape[-1])
    return jnp.einsum("nc,nd->cd", flat_left, flat_grad, preferred_element_type=jnp.float32)


def attn_scores(query, keys, allowed, scale):
    raw_scores = (
        jnp.einsum("qlhd,klhd->lhqk", query, keys, preferred_element_type=jnp.float32) * scale
    )
    return jnp.where(allowed, raw_scores, -1e30)


def tri_gates(tri_lin):
    quarter = tri_lin.shape[-1] // 4
    left_part = jax.nn.sigmoid(tri_lin[..., quarter : 2 * quarter]) * tri_lin[..., :quarter]
    right_part = (
        jax.nn.sigmoid(tri_lin[..., 3 * quarter :]) * tri_lin[..., 2 * quarter : 3 * quarter]
    )
    return (left_part, right_part)


def edge_front(own_rows, other_near, edge_lin, diff, distance_basis_matrix):
    radial = jnp.log(1.0 + jnp.sum(diff * diff, 0))
    return jax.nn.silu(
        own_rows[:, None, :] + other_near + edge_lin + radial[..., None] * distance_basis_matrix
    )


def edge_finish(msg_lin, signal_location_matrix, diff):
    message = jax.nn.silu(msg_lin)
    turn = jnp.tanh(jnp.einsum("ikc,c->ik", message, signal_location_matrix, precision=HIGH))
    return (jnp.mean(message, 1), jnp.mean(diff * turn[None], 2))


def gather_rows(value):
    return lax.all_gather(value, "seq", axis=0, tiled=True)


def across_res(value):
    return lax.psum(value.astype(jnp.bfloat16), "res").astype(jnp.float32)


def owners_sum(value):
    return lax.psum_scatter(value, "seq", scatter_dimension=0, tiled=True)


def place_home(rows_part, col_width, offset, keep_home):
    empty = jnp.zeros((rows_part.shape[0], col_width, rows_part.shape[2]), jnp.float32)
    return lax.dynamic_update_slice_in_dim(empty, rows_part, offset, 1) * keep_home


def sum_flat(parts):
    flat = jnp.concatenate([jnp.ravel(member) for member in parts])
    summed = lax.psum(flat, ("seq", "res"))
    pieces = []
    offset = 0
    for member in parts:
        pieces.append(summed[offset : offset + member.size].reshape(member.shape))
        offset = offset + member.size
    return pieces


def shards(
    alignment_embedding,
    coupling_embedding,
    vertex_embedding,
    atom_locations,
    chain_existence_flags,
    closest_aminos,
    softmax_mixer_scale_factor,
    attender_stacked_matrix,
    softmax_mixer_exit_matrix,
    tensor_mean_scale_factor,
    tensor_mean_entry_matrix,
    tensor_mean_exit_matrix,
    outbound_entry_scale,
    outbound_entry_matrix,
    outbound_exit_scale,
    outbound_exit_matrix,
    inbound_entry_scale,
    inbound_entry_matrix,
    inbound_exit_scale,
    inbound_exit_matrix,
    vertex_mapping_matrix,
    bond_mapping_matrix,
    distance_basis_matrix,
    signal_matrix,
    signal_location_matrix,
    vertex_change_matrix,
    alignment_adjoint,
    coupling_adjoint,
    vertex_adjoint,
    location_adjoint,
):
    seq_index = lax.axis_index("seq")
    res_index = lax.axis_index("res")
    n_seq = lax.axis_size("seq")
    n_res = lax.axis_size("res")
    chain_shard_piece, vertical_shard_piece, breadth_overall = alignment_embedding.shape
    rows_dev = coupling_embedding.shape[0]
    span_overall, node_width = vertex_embedding.shape
    block_tally = chain_existence_flags.shape[0]
    head_size = breadth_overall // HEADS
    scale = head_size ** (-0.5)
    opm_width = tensor_mean_entry_matrix.shape[1] // 2
    tri_width = outbound_exit_matrix.shape[0]
    chain_exists = (chain_existence_flags > 0).astype(jnp.float32)
    line_indicator_entries = lax.dynamic_slice_in_dim(
        chain_exists, seq_index * chain_shard_piece, chain_shard_piece
    )
    first_res = (res_index == 0).astype(jnp.float32)
    home = seq_index * rows_dev // vertical_shard_piece
    offset = seq_index * rows_dev - home * vertical_shard_piece
    keep_home = (home == res_index).astype(jnp.float32)
    alignment_real_lines = alignment_embedding.astype(jnp.float32)
    standardized_lines, standardize_reverse_alpha = jax.vjp(
        standardize_lines, alignment_real_lines, softmax_mixer_scale_factor
    )
    normed_b = standardized_lines.astype(jnp.bfloat16)
    projected = tensor_mean_answer(normed_b, attender_stacked_matrix)
    query = projected[..., :breadth_overall].astype(jnp.bfloat16)
    keyval = projected[..., breadth_overall : 3 * breadth_overall].astype(jnp.bfloat16)
    attn_gate = jax.nn.sigmoid(projected[..., 3 * breadth_overall :])
    all_keyval = lax.all_gather(keyval, "seq", axis=0, tiled=True)
    query4 = query.reshape(chain_shard_piece, vertical_shard_piece, HEADS, head_size)
    keys4 = all_keyval[..., :breadth_overall].reshape(
        block_tally, vertical_shard_piece, HEADS, head_size
    )
    values4 = all_keyval[..., breadth_overall:].reshape(
        block_tally, vertical_shard_piece, HEADS, head_size
    )
    allowed = chain_exists[None, None, None, :] > 0
    scores = attn_scores(query4, keys4, allowed, scale)
    score_peak = jnp.max(scores, -1, keepdims=True)
    exp_scores = jnp.exp(scores - score_peak)
    exp_total = jnp.sum(exp_scores, -1, keepdims=True)
    log_total = score_peak + jnp.log(exp_total)
    probs_b = (exp_scores / exp_total).astype(jnp.bfloat16)
    attended = jnp.einsum(
        "lhqk,klhd->qlhd", probs_b, values4, preferred_element_type=jnp.float32
    ).reshape(chain_shard_piece, vertical_shard_piece, breadth_overall)
    sigmoid_scaled_lines = (attn_gate * attended).astype(jnp.bfloat16)
    alignment_later = alignment_real_lines + tensor_mean_answer(
        sigmoid_scaled_lines, softmax_mixer_exit_matrix
    )
    standardized_lines2, standardize_reverse_beta = jax.vjp(
        standardize_lines, alignment_later, tensor_mean_scale_factor
    )
    normed2_b = standardized_lines2.astype(jnp.bfloat16)
    outer_in = (
        tensor_mean_answer(normed2_b, tensor_mean_entry_matrix)
        * line_indicator_entries[:, None, None]
    ).astype(jnp.bfloat16)
    everyone = lax.all_gather(outer_in, ("seq", "res"), axis=0, tiled=True)
    blocks = everyone.reshape(n_seq, n_res, chain_shard_piece, vertical_shard_piece, 2 * opm_width)
    home_block = lax.dynamic_index_in_dim(blocks, home, 1, keepdims=False)
    left_rows = lax.dynamic_slice_in_dim(home_block, offset, rows_dev, 2)[..., :opm_width]
    left_rows = left_rows.reshape(block_tally, rows_dev, opm_width)
    right_cols = lax.dynamic_index_in_dim(blocks, res_index, 1, keepdims=False)[..., opm_width:]
    right_cols = right_cols.reshape(block_tally, vertical_shard_piece, opm_width)
    outer_b = jnp.einsum("sic,sjd->ijcd", left_rows, right_cols, preferred_element_type=jnp.float32)
    outer_b = outer_b.reshape(rows_dev, vertical_shard_piece, opm_width * opm_width).astype(
        jnp.bfloat16
    )
    count = jnp.sum(chain_exists)
    pair1 = (
        coupling_embedding.astype(jnp.float32)
        + tensor_mean_answer(outer_b, tensor_mean_exit_matrix) / count
    )
    normed3, norm_back3 = jax.vjp(standardize_lines, pair1, outbound_entry_scale)
    normed3_b = normed3.astype(jnp.bfloat16)
    tri = tensor_mean_answer(normed3_b, outbound_entry_matrix)
    (left_t, right_t), gates_back = jax.vjp(tri_gates, tri[..., : 4 * tri_width])
    left_b = left_t.astype(jnp.bfloat16)
    right_b = right_t.astype(jnp.bfloat16)
    right_all = gather_rows(right_b)
    partial_tri = jnp.einsum("ikc,jkc->ijc", left_b, right_all, preferred_element_type=jnp.float32)
    triangle = lax.psum_scatter(
        partial_tri.astype(jnp.bfloat16), "res", scatter_dimension=1, tiled=True
    ).astype(jnp.float32)
    normed4, norm_back4 = jax.vjp(standardize_lines, triangle, outbound_exit_scale)
    normed4_b = normed4.astype(jnp.bfloat16)
    update = tensor_mean_answer(normed4_b, outbound_exit_matrix)
    out_gate = jax.nn.sigmoid(tri[..., 4 * tri_width :])
    pair2 = pair1 + out_gate * update
    normed5, norm_back5 = jax.vjp(standardize_lines, pair2, inbound_entry_scale)
    normed5_b = normed5.astype(jnp.bfloat16)
    tri2 = tensor_mean_answer(normed5_b, inbound_entry_matrix)
    (left_i, right_i), gates_back2 = jax.vjp(tri_gates, tri2[..., : 4 * tri_width])
    both_local = jnp.concatenate([left_i.astype(jnp.bfloat16), right_i.astype(jnp.bfloat16)], -1)
    both_all = gather_rows(both_local)
    right_all2 = both_all[..., tri_width:]
    left_cand = lax.dynamic_slice_in_dim(both_all[..., :tri_width], offset, rows_dev, 1)
    left_sel = spread_2(left_cand, "res", home)
    triangle2 = jnp.einsum("kic,kjc->ijc", left_sel, right_all2, preferred_element_type=jnp.float32)
    normed6, norm_back6 = jax.vjp(standardize_lines, triangle2, inbound_exit_scale)
    normed6_b = normed6.astype(jnp.bfloat16)
    update2 = tensor_mean_answer(normed6_b, inbound_exit_matrix)
    out_gate2 = jax.nn.sigmoid(tri2[..., 4 * tri_width :])
    coupling_later3 = pair2 + out_gate2 * update2
    pair3_b = coupling_later3.astype(jnp.bfloat16)
    rows_all = lax.all_gather(pair3_b, "res", axis=1, tiled=True)
    nbr_hot = closest_aminos[:, :, None] == jnp.arange(span_overall, dtype=jnp.int32)[None, None, :]
    hot_float = nbr_hot.astype(jnp.float32)
    edges_b = jnp.einsum(
        "ikl,ilc->ikc", nbr_hot.astype(jnp.bfloat16), rows_all, preferred_element_type=jnp.float32
    ).astype(jnp.bfloat16)
    single_b = vertex_embedding.astype(jnp.bfloat16)
    node_proj = tensor_mean_answer(single_b, vertex_mapping_matrix)
    own_rows = lax.dynamic_slice_in_dim(node_proj[:, :node_width], seq_index * rows_dev, rows_dev)
    other_near = jnp.einsum("ikl,lc->ikc", hot_float, node_proj[:, node_width:], precision=HIGH)
    coords_own = lax.dynamic_slice_in_dim(atom_locations, seq_index * rows_dev, rows_dev, 1)
    coords_near = jnp.einsum("ikl,xl->xik", hot_float, atom_locations, precision=HIGH)
    diff = coords_own[:, :, None] - coords_near
    edge_lin = tensor_mean_answer(edges_b, bond_mapping_matrix)
    hidden, front_back = jax.vjp(
        edge_front, own_rows, other_near, edge_lin, diff, distance_basis_matrix
    )
    hidden_b = hidden.astype(jnp.bfloat16)
    msg_lin = tensor_mean_answer(hidden_b, signal_matrix)
    (mean_msg, shift), finish_back = jax.vjp(edge_finish, msg_lin, signal_location_matrix, diff)
    mean_b = mean_msg.astype(jnp.bfloat16)
    single_rows = lax.dynamic_slice_in_dim(vertex_embedding, seq_index * rows_dev, rows_dev)
    single_out = single_rows + tensor_mean_answer(mean_b, vertex_change_matrix)
    coords_out = coords_own + shift
    d_update_b = vertex_adjoint.astype(jnp.bfloat16)
    g_update = weight_back(mean_b, d_update_b)
    d_mean = product_back(d_update_b, vertex_change_matrix)
    d_msg_lin, g_coord, d_diff_finish = finish_back((d_mean, location_adjoint))
    d_msg_b = d_msg_lin.astype(jnp.bfloat16)
    g_msg = weight_back(hidden_b, d_msg_b)
    d_hidden = product_back(d_msg_b, signal_matrix)
    d_own, d_other_near, d_edge_lin, d_diff_front, g_dist = front_back(d_hidden)
    d_edge_b = d_edge_lin.astype(jnp.bfloat16)
    g_edge = weight_back(edges_b, d_edge_b)
    d_edges = product_back(d_edge_b, bond_mapping_matrix)
    d_rows = jnp.einsum("ikl,ikc->ilc", hot_float, d_edges, precision=HIGH)
    d_pair3 = coupling_adjoint.astype(jnp.float32) + lax.dynamic_slice_in_dim(
        d_rows, res_index * vertical_shard_piece, vertical_shard_piece, 1
    )
    d_diff = d_diff_front + d_diff_finish
    d_coords_own = jnp.sum(d_diff, 2)
    d_coords_near = jnp.einsum("ikl,xik->xl", hot_float, -d_diff, precision=HIGH)
    d_other_all = jnp.einsum("ikl,ikc->lc", hot_float, d_other_near, precision=HIGH)
    d_other_rows, d_near_rows = (
        lax.psum_scatter(d_other_all, "seq", scatter_dimension=0, tiled=True),
        lax.psum_scatter(d_coords_near, "seq", scatter_dimension=1, tiled=True),
    )
    d_node_b = jnp.concatenate([d_own, d_other_rows], -1).astype(jnp.bfloat16)
    g_node = weight_back(
        lax.dynamic_slice_in_dim(single_b, seq_index * rows_dev, rows_dev), d_node_b
    )
    single_grad = vertex_adjoint + product_back(d_node_b, vertex_mapping_matrix)
    coords_grad = location_adjoint + d_coords_own + d_near_rows
    layer_two = [
        g_node * first_res,
        g_edge * first_res,
        g_dist * first_res,
        g_msg * first_res,
        g_coord * first_res,
        g_update * first_res,
    ]
    d_inc_b = (d_pair3 * out_gate2).astype(jnp.bfloat16)
    d_gate_out2 = d_pair3 * update2 * out_gate2 * (1.0 - out_gate2)
    g_inc_out = weight_back(normed6_b, d_inc_b)
    d_normed6 = product_back(d_inc_b, inbound_exit_matrix)
    d_triangle2, g_inc_out_gain = norm_back6(d_normed6)
    d_tri2_b = d_triangle2.astype(jnp.bfloat16)
    d_left_sel = jnp.einsum(
        "ijc,kjc->kic", d_tri2_b, right_all2, preferred_element_type=jnp.float32
    )
    d_right_all2 = jnp.einsum(
        "ijc,kic->kjc", d_tri2_b, left_sel, preferred_element_type=jnp.float32
    )
    d_left_total = across_res(d_left_sel)
    d_both2 = owners_sum(
        jnp.concatenate(
            [place_home(d_left_total, vertical_shard_piece, offset, keep_home), d_right_all2], -1
        )
    )
    (d_gates2,) = gates_back2((d_both2[..., :tri_width], d_both2[..., tri_width:]))
    d_tri2_in_b = jnp.concatenate([d_gates2, d_gate_out2], -1).astype(jnp.bfloat16)
    g_inc_in = weight_back(normed5_b, d_tri2_in_b)
    d_normed5 = product_back(d_tri2_in_b, inbound_entry_matrix)
    d_pair2_norm, g_inc_gain = norm_back5(d_normed5)
    d_pair2 = d_pair3 + d_pair2_norm
    d_tri_out_b = (d_pair2 * out_gate).astype(jnp.bfloat16)
    d_gate_out = d_pair2 * update * out_gate * (1.0 - out_gate)
    g_tri_out = weight_back(normed4_b, d_tri_out_b)
    d_normed4 = product_back(d_tri_out_b, outbound_exit_matrix)
    d_triangle, g_tri_out_gain = norm_back4(d_normed4)
    d_triangle_b = d_triangle.astype(jnp.bfloat16)
    d_tri_all = lax.all_gather(d_triangle_b, "res", axis=1, tiled=True)
    d_left = jnp.einsum("ijc,jkc->ikc", d_tri_all, right_all, preferred_element_type=jnp.float32)
    d_right_part = jnp.einsum("ijc,ikc->jkc", d_tri_all, left_b, preferred_element_type=jnp.float32)
    d_right = owners_sum(d_right_part)
    (d_gates_in,) = gates_back((d_left, d_right))
    d_tri_b = jnp.concatenate([d_gates_in, d_gate_out], -1).astype(jnp.bfloat16)
    g_tri_in = weight_back(normed3_b, d_tri_b)
    d_normed3 = product_back(d_tri_b, outbound_entry_matrix)
    d_pair1_norm, g_tri_gain = norm_back3(d_normed3)
    pair_grad = d_pair2 + d_pair1_norm
    d_opm_b = (pair_grad / count).astype(jnp.bfloat16)
    g_opm_out = weight_back(outer_b, d_opm_b)
    d_outer = product_back(d_opm_b, tensor_mean_exit_matrix).astype(jnp.bfloat16)
    d_outer = d_outer.reshape(rows_dev, vertical_shard_piece, opm_width, opm_width)
    d_left_rows = jnp.einsum(
        "ijcd,sjd->sic", d_outer, right_cols, preferred_element_type=jnp.float32
    )
    d_right_cols = jnp.einsum(
        "ijcd,sic->sjd", d_outer, left_rows, preferred_element_type=jnp.float32
    )
    d_left_sum = across_res(d_left_rows)
    d_outer_in = owners_sum(
        jnp.concatenate(
            [place_home(d_left_sum, vertical_shard_piece, offset, keep_home), d_right_cols], -1
        )
    )
    d_outer_in_b = (d_outer_in * line_indicator_entries[:, None, None]).astype(jnp.bfloat16)
    g_opm_in = weight_back(normed2_b, d_outer_in_b)
    standardized_sens2 = product_back(d_outer_in_b, tensor_mean_entry_matrix)
    alignment_standard_sens, tensor_mean_scale_sens = standardize_reverse_beta(standardized_sens2)
    alignment_later_sens = alignment_adjoint.astype(jnp.float32) + alignment_standard_sens
    softmax_mixer_sens_lines = alignment_later_sens.astype(jnp.bfloat16)
    g_attn_out = weight_back(sigmoid_scaled_lines, softmax_mixer_sens_lines)
    d_gated = product_back(softmax_mixer_sens_lines, softmax_mixer_exit_matrix)
    d_attended_b = (d_gated * attn_gate).astype(jnp.bfloat16)
    d_gate_lin = d_gated * attended * attn_gate * (1.0 - attn_gate)
    probs_full = jnp.exp(attn_scores(query4, keys4, allowed, scale) - log_total)
    d_attended4 = d_attended_b.reshape(chain_shard_piece, vertical_shard_piece, HEADS, head_size)
    d_probs = jnp.einsum(
        "qlhd,klhd->lhqk", d_attended4, values4, preferred_element_type=jnp.float32
    )
    softmax_total = jnp.sum(probs_full * d_probs, -1, keepdims=True)
    d_scores_b = (probs_full * (d_probs - softmax_total) * scale).astype(jnp.bfloat16)
    d_query = jnp.einsum(
        "lhqk,klhd->qlhd", d_scores_b, keys4, preferred_element_type=jnp.float32
    ).reshape(chain_shard_piece, vertical_shard_piece, breadth_overall)
    d_keys = jnp.einsum("lhqk,qlhd->klhd", d_scores_b, query4, preferred_element_type=jnp.float32)
    d_values = jnp.einsum(
        "lhqk,qlhd->klhd",
        probs_full.astype(jnp.bfloat16),
        d_attended4,
        preferred_element_type=jnp.float32,
    )
    d_keyval = jnp.concatenate(
        [
            d_keys.reshape(block_tally, vertical_shard_piece, breadth_overall),
            d_values.reshape(block_tally, vertical_shard_piece, breadth_overall),
        ],
        -1,
    )
    d_keyval_own = lax.psum_scatter(d_keyval, "seq", scatter_dimension=0, tiled=True)
    d_proj_b = jnp.concatenate([d_query, d_keyval_own, d_gate_lin], -1).astype(jnp.bfloat16)
    g_qkvg = weight_back(normed_b, d_proj_b)
    standardized_sens = product_back(d_proj_b, attender_stacked_matrix)
    alignment_early_sens, alignment_scale_sens = standardize_reverse_alpha(standardized_sens)
    alignment_sensitivity = alignment_later_sens + alignment_early_sens
    layer_one = [
        alignment_scale_sens,
        g_qkvg,
        g_attn_out,
        tensor_mean_scale_sens,
        g_opm_in,
        g_opm_out,
        g_tri_gain,
        g_tri_in,
        g_tri_out_gain,
        g_tri_out,
        g_inc_gain,
        g_inc_in,
        g_inc_out_gain,
        g_inc_out,
    ]
    summed_all = sum_flat(layer_one + layer_two)
    layer_one = summed_all[:14]
    layer_two = summed_all[14:]
    return (
        alignment_later.astype(jnp.bfloat16),
        pair3_b,
        single_out,
        coords_out,
        alignment_sensitivity,
        pair_grad,
        single_grad,
        coords_grad,
        layer_one[0],
        layer_one[1],
        layer_one[2],
        layer_one[3],
        layer_one[4],
        layer_one[5],
        layer_one[6],
        layer_one[7],
        layer_one[8],
        layer_one[9],
        layer_one[10],
        layer_one[11],
        layer_one[12],
        layer_one[13],
        layer_two[0],
        layer_two[1],
        layer_two[2],
        layer_two[3],
        layer_two[4],
        layer_two[5],
    )


def solution(mesh):
    return jax.shard_map(
        shards,
        mesh=mesh,
        in_specs=(
            P("seq", "res", None),
            P("seq", "res", None),
            P(),
            P(),
            P(),
            P("seq", None),
            P(),
            P(),
            P(),
            P(),
            P(),
            P(),
            P(),
            P(),
            P(),
            P(),
            P(),
            P(),
            P(),
            P(),
            P(),
            P(),
            P(),
            P(),
            P(),
            P(),
            P("seq", "res", None),
            P("seq", "res", None),
            P("seq", None),
            P(None, "seq"),
        ),
        out_specs=(
            P("seq", "res", None),
            P("seq", "res", None),
            P("seq", None),
            P(None, "seq"),
            P("seq", "res", None),
            P("seq", "res", None),
            P("seq", None),
            P(None, "seq"),
            P(),
            P(),
            P(),
            P(),
            P(),
            P(),
            P(),
            P(),
            P(),
            P(),
            P(),
            P(),
            P(),
            P(),
            P(),
            P(),
            P(),
            P(),
            P(),
            P(),
        ),
        check_vma=False,
    )
```

profile of v0, /device:TPU:1, one launch (start us, length us, event | category | flops | bytes accessed | tf_op | source)
XLA Modules:
  0.0 1361.0 jit_solution(7006177612727944377)
XLA Ops:
  14.2 29.4 %all-gather.7.cloned.1.call-done = bf16[32,64,512]{2,1,0:T(8,128)(2,1)} async-done(((bf16[4,64,512]{2,1,0:T(8,128)(2,1)}), bf16[32,64,512]{2,1,0:T(8,128)(2,1)}) %all-gather.7.cloned.1.call-update) | async-done | bytes 2097168 | tf_op jit(solution)/shard_map/all_gather | solution.py:157
  48.7 6.8 copy.170
  57.6 6.9 copy.171
  78.2 55.5 %all-gather.9.cloned.1.call-done = bf16[128,64,64]{2,1,0:T(8,128)(2,1)} async-done(((bf16[4,64,64]{2,1,0:T(8,128)(2,1)}), bf16[128,64,64]{2,1,0:T(8,128)(2,1)}) %all-gather.9.cloned.1.call-update) | async-done | bytes 1048592 | tf_op jit(solution)/shard_map/all_gather | solution.py:187
  142.8 16.7 %copy.176 = bf16[32,64,32,32]{1,3,2,0:T(8,128)(2,1)} copy(bf16[32,64,32,32]{1,2,0,3:T(8,128)(2,1)} %fusion.5) | data formatting | bytes 8388608 | tf_op jit(solution)/shard_map/convert_element_type | solution.py:195
  159.4 6.6 fusion.221
  173.2 34.1 %all-gather.11.cloned.1.call-done = bf16[256,64,128]{2,1,0:T(8,128)(2,1)} async-done(((bf16[32,64,128]{2,1,0:T(8,128)(2,1)}), bf16[256,64,128]{2,1,0:T(8,128)(2,1)}) %all-gather.11.cloned.1.call-update) | async-done | bytes 4194320 | tf_op jit(solution)/shard_map/all_gather | solution.py:69
  207.3 12.9 copy.178
  220.3 7.7 convert_bitcast_fusion.1
  233.6 43.0 %reduce-scatter.10.cloned.1.call-done = bf16[32,64,128]{2,0,1:T(8,128)(2,1)} async-done(((bf16[32,256,128]{2,0,1:T(8,128)(2,1)}), bf16[32,64,128]{2,0,1:T(8,128)(2,1)}) %reduce-scatter.10.cloned.1.call-update) | async-done | bytes 524304 | tf_op jit(solution)/shard_map/reduce_scatter | solution.py:211
  289.2 54.4 %all-gather.13.cloned.1.call-done = bf16[256,64,256]{2,1,0:T(8,128)(2,1)} async-done(((bf16[32,64,256]{2,1,0:T(8,128)(2,1)}), bf16[256,64,256]{2,1,0:T(8,128)(2,1)}) %all-gather.13.cloned.1.call-update) | async-done | bytes 8388624 | tf_op jit(solution)/shard_map/all_gather | solution.py:69
  356.7 7.6 copy.253
  364.3 78.6 %all-reduce.13.cloned.1.call-done = bf16[256,32,128]{0,1,2:T(8,128)(2,1)} async-done(((bf16[256,32,128]{0,1,2:T(8,128)(2,1)}), bf16[256,32,128]{0,1,2:T(8,128)(2,1)}) %all-reduce.13.cloned.1.call-update) | async-done | bytes 2097168 | tf_op jit(solution)/shard_map/psum | solution.py:15
  463.0 36.3 %all-gather.15.cloned.1.call-done = bf16[32,256,128]{2,1,0:T(8,128)(2,1)} async-done(((bf16[32,64,128]{2,1,0:T(8,128)(2,1)}), bf16[32,256,128]{2,1,0:T(8,128)(2,1)}) %all-gather.15.cloned.1.call-update) | async-done | bytes 2097168 | tf_op jit(solution)/shard_map/all_gather | solution.py:235
  547.2 9.3 copy.193
  556.5 69.8 %all-reduce.15.cloned.1.call-done = bf16[256,32,128]{2,1,0:T(8,128)(2,1)} async-done(((bf16[256,32,128]{2,1,0:T(8,128)(2,1)}), bf16[256,32,128]{2,1,0:T(8,128)(2,1)}) %all-reduce.15.cloned.1.call-update) | async-done | bytes 2097168 | tf_op jit(solution)/shard_map/psum | solution.py:73
  630.3 9.8 pad_maximum_fusion
  640.2 115.0 %reduce-scatter.12.cloned.1.call-done = f32[32,64,256]{2,1,0:T(8,128)} async-done(((f32[256,64,256]{2,1,0:T(8,128)}), f32[32,64,256]{2,1,0:T(8,128)}) %reduce-scatter.12.cloned.1.call-update) | async-done | bytes 2097168 | tf_op jit(solution)/shard_map/reduce_scatter | solution.py:77
  772.3 46.1 %all-gather.17.cloned.1.call-done = bf16[32,256,128]{2,0,1:T(8,128)(2,1)} async-done(((bf16[32,64,128]{2,0,1:T(8,128)(2,1)}), bf16[32,256,128]{2,0,1:T(8,128)(2,1)}) %all-gather.17.cloned.1.call-update) | async-done | bytes 2097168 | tf_op jit(solution)/shard_map/all_gather | solution.py:326
  828.1 8.9 copy.197
  843.5 7.5 fusion.225
  853.9 53.2 %reduce-scatter.14.cloned.1.call-done = f32[32,64,128]{2,1,0:T(8,128)} async-done(((f32[256,64,128]{2,1,0:T(8,128)}), f32[32,64,128]{2,1,0:T(8,128)}) %reduce-scatter.14.cloned.1.call-update) | async-done | bytes 1048592 | tf_op jit(solution)/shard_map/reduce_scatter | solution.py:77
  922.5 8.4 copy.201
  930.9 9.8 fusion.30
  941.9 8.3 fusion.33
  951.6 24.2 %all-reduce.17.cloned.1.call-done = bf16[32,32,32]{2,1,0:T(8,128)(2,1)} async-done(((bf16[32,32,32]{2,1,0:T(8,128)(2,1)}), bf16[32,32,32]{2,1,0:T(8,128)(2,1)}) %all-reduce.17.cloned.1.call-update) | async-done | bytes 65552 | tf_op jit(solution)/shard_map/psum | solution.py:73
  984.9 31.4 %reduce-scatter.16.cloned.1.call-done = f32[4,64,64]{2,1,0:T(8,128)} async-done(((f32[32,64,64]{2,1,0:T(8,128)}), f32[4,64,64]{2,1,0:T(8,128)}) %reduce-scatter.16.cloned.1.call-update) | async-done | bytes 65552 | tf_op jit(solution)/shard_map/reduce_scatter | solution.py:77
  1033.6 28.6 %fusion.90 = f32[64,8,32,32]{3,2,1,0:T(8,128)} fusion(bf16[4,64,8,32]{3,0,2,1:T(4,128)(2,1)} %copy-done.22, f32[64,8,4,32]{3,2,1,0:T(4,128)} %fusion.224, f32[64,8,4,32]{3,2,1,0:T(4,128)S(1)} %copy-done.14, f32[64,8,4]{2,1,0:T(8,128)} %log_add_fusion), kind=kOutput, calls=%fused_computation.182 | convolution fusion | flops 4655135 | bytes 2760704 | tf_op jit(solution)/shard_map/lhqk,qlhd->klhd/dot_general | solution.py:372
  1122.2 6.7 convolution_bitcast_fusion
  1130.2 26.0 %fusion.36 = bf16[4,64,8,32]{3,0,2,1:T(4,128)(2,1)} fusion(bf16[32,64,8,32]{3,0,2,1:T(8,128)(2,1)} %copy.170, f32[64,8,4,32]{3,2,1,0:T(4,128)} %fusion.224, f32[64,8,4,32]{3,2,1,0:T(4,128)S(1)} %copy-done.15, f32[64,8,4]{2,1,0:T(8,128)S(1)} %copy-done.36), kind=kOutput, calls=%fused_computation.73 | convolution fusion | flops 4720671 | bytes 1712128 | tf_op jit(solution)/shard_map/lhqk,klhd->qlhd/dot_general | solution.py:369
  1162.9 35.9 %concatenate.39 = f32[697472]{0:T(1024)} concatenate(f32[256]{0:T(256)} %get-tuple-element.97, f32[262144]{0:T(1024)S(1)} %bitcast.288, f32[65536]{0:T(1024)S(1)} %bitcast.298, f32[256]{0:T(256)} %get-tuple-element.95, f32[16384]{0:T(1024)} %reshape.461, f32[131072]{0:T(1024)S(1)} %copy-done.63, f32[128]{0:T(128)} %get-tuple-element.88, f32[81920]{0:T(1024)S(1)} %reshape.463, ...), dimensions={0} | concatenate | bytes 5579776 | tf_op jit(solution)/shard_map/concatenate | solution.py:86
  1204.5 130.4 %all-reduce.19.cloned.1.call-done = f32[697472]{0:T(1024)} async-done(((f32[697472]{0:T(1024)}), f32[697472]{0:T(1024)}) %all-reduce.19.cloned.1.call-update) | async-done | bytes 2789904 | tf_op jit(solution)/shard_map/psum | solution.py:87
  (576 shorter events, 318.9 us)
Async XLA Ops:
  7.2 36.3 %all-gather.7.cloned.1.call-start = ((), (), s32[]{:S(2)}) async-start(), calls=%async_computation.7 | async-start | bytes 2359296 | tf_op jit(solution)/shard_map/all_gather | solution.py:157
  13.0 120.7 %all-gather.9.cloned.1.call-start = ((), (), s32[]{:S(2)}) async-start(), calls=%async_computation.8 | async-start | bytes 2162688 | tf_op jit(solution)/shard_map/all_gather | solution.py:187
  14.0 50.4 %copy-start.22 = (bf16[4,64,8,32]{3,0,2,1:T(4,128)(2,1)}, bf16[4,64,8,32]{3,0,2,1:T(4,128)(2,1)S(1)}, u32[]{:S(2)}) copy-start(bf16[4,64,8,32]{3,0,2,1:T(4,128)(2,1)S(1)} %copy.169) | copy-start | bytes 393220
  14.2 61.5 %copy-start.151 = (f32[4]{0:T(128)}, f32[4]{0:T(128)S(1)}, u32[]{:S(2)}) copy-start(f32[4]{0:T(128)S(1)} %dynamic_slice.31) | copy-start | bytes 52
  73.6 60.1 %copy-start.54 = (f32[4,64,256]{2,1,0:T(8,128)}, f32[4,64,256]{2,1,0:T(8,128)S(1)}, u32[]{:S(2)}) copy-start(f32[4,64,256]{2,1,0:T(8,128)S(1)} %copy.173) | copy-start | bytes 786436
  75.4 58.3 %copy-start.94 = (f32[4,64]{1,0:T(4,128)}, f32[4,64]{1,0:T(4,128)S(1)}, u32[]{:S(2)}) copy-start(f32[4,64]{1,0:T(4,128)S(1)} %broadcast_multiply_fusion.7) | copy-start | bytes 3076
  75.6 58.1 %copy-start.136 = (f32[4,64]{1,0:T(4,128)}, f32[4,64]{1,0:T(4,128)S(1)}, u32[]{:S(2)}) copy-start(f32[4,64]{1,0:T(4,128)S(1)} %multiply_reduce_fusion.14) | copy-start | bytes 3076
  76.1 57.6 %copy-start.117 = (f32[4,64]{1,0:T(4,128)}, f32[4,64]{1,0:T(4,128)S(1)}, u32[]{:S(2)}) copy-start(f32[4,64]{1,0:T(4,128)S(1)} %fusion.182) | copy-start | bytes 3076
  77.1 130.2 %all-gather.11.cloned.1.call-start = ((), (), s32[]{:S(2)}) async-start(), calls=%async_computation.9 | async-start | bytes 4718592 | tf_op jit(solution)/shard_map/all_gather | solution.py:69
  166.1 113.7 %copy-start.7 = (f32[32,64,128]{2,1,0:T(8,128)}, f32[32,64,128]{2,1,0:T(8,128)S(1)}, u32[]{:S(2)}) copy-start(f32[32,64,128]{2,1,0:T(8,128)S(1)} %get-tuple-element.165) | copy-start | bytes 3145732
  166.8 749.5 %copy-start.67 = (f32[32,64]{1,0:T(8,128)}, f32[32,64]{1,0:T(8,128)S(1)}, u32[]{:S(2)}) copy-start(f32[32,64]{1,0:T(8,128)S(1)} %fusion.173) | copy-start | bytes 24580
  171.6 105.0 %reduce-scatter.10.cloned.1.call-start = ((), (), s32[]{:S(2)}) async-start(), calls=%async_computation.10 | async-start | bytes 2621440 | tf_op jit(solution)/shard_map/reduce_scatter | solution.py:211
  227.9 51.8 %copy-start.123 = (bf16[128,128]{1,0:T(8,128)(2,1)S(1)}, bf16[128,128]{1,0:T(8,128)(2,1)}, u32[]{:S(2)}) copy-start(bf16[128,128]{1,0:T(8,128)(2,1)} %param.45) | copy-start | bytes 98308
  227.9 51.8 %copy-start.149 = (f32[128]{0:T(128)S(1)}, f32[128]{0:T(128)}, u32[]{:S(2)}) copy-start(f32[128]{0:T(128)} %param.44) | copy-start | bytes 1540
  233.2 110.4 %all-gather.13.cloned.1.call-start = ((), (), s32[]{:S(2)}) async-start(), calls=%async_computation.11 | async-start | bytes 9437184 | tf_op jit(solution)/shard_map/all_gather | solution.py:69
  278.0 491.8 %copy-start.65 = (f32[32,64]{1,0:T(8,128)}, f32[32,64]{1,0:T(8,128)S(1)}, u32[]{:S(2)}) copy-start(f32[32,64]{1,0:T(8,128)S(1)} %broadcast_multiply_fusion.4) | copy-start | bytes 24580
  283.1 480.4 %copy-start.64 = (f32[32,64]{1,0:T(8,128)}, f32[32,64]{1,0:T(8,128)S(1)}, u32[]{:S(2)}) copy-start(f32[32,64]{1,0:T(8,128)S(1)} %broadcast_multiply_fusion.3) | copy-start | bytes 24580
  284.1 479.4 %copy-start.68 = (f32[32,64]{1,0:T(8,128)}, f32[32,64]{1,0:T(8,128)S(1)}, u32[]{:S(2)}) copy-start(f32[32,64]{1,0:T(8,128)S(1)} %fusion.175) | copy-start | bytes 24580
  289.1 153.8 %all-reduce.13.cloned.1.call-start = ((), (), s32[]{:S(2)}) async-start(), calls=%async_computation.12 | async-start | bytes 4194304 | tf_op jit(solution)/shard_map/psum | solution.py:15
  356.7 142.6 %all-gather.15.cloned.1.call-start = ((), (), s32[]{:S(2)}) async-start(), calls=%async_computation.13 | async-start | bytes 2621440 | tf_op jit(solution)/shard_map/all_gather | solution.py:235
  364.3 83.1 %copy-start.154 = (f32[128]{0:T(128)S(1)}, f32[128]{0:T(128)}, u32[]{:S(2)}) copy-start(f32[128]{0:T(128)} %param.48) | copy-start | bytes 1540
  454.2 172.1 %all-reduce.15.cloned.1.call-start = ((), (), s32[]{:S(2)}) async-start(), calls=%async_computation.14 | async-start | bytes 4194304 | tf_op jit(solution)/shard_map/psum | solution.py:73
  540.9 214.3 %reduce-scatter.12.cloned.1.call-start = ((), (), s32[]{:S(2)}) async-start(), calls=%async_computation.15 | async-start | bytes 18874368 | tf_op jit(solution)/shard_map/reduce_scatter | solution.py:77
  640.1 178.2 %all-gather.17.cloned.1.call-start = ((), (), s32[]{:S(2)}) async-start(), calls=%async_computation.16 | async-start | bytes 2621440 | tf_op jit(solution)/shard_map/all_gather | solution.py:326
  772.2 134.9 %reduce-scatter.14.cloned.1.call-start = ((), (), s32[]{:S(2)}) async-start(), calls=%async_computation.17 | async-start | bytes 9437184 | tf_op jit(solution)/shard_map/reduce_scatter | solution.py:77
  837.0 138.7 %all-reduce.17.cloned.1.call-start = ((), (), s32[]{:S(2)}) async-start(), calls=%async_computation.18 | async-start | bytes 524288 | tf_op jit(solution)/shard_map/psum | solution.py:73
  851.0 56.1 %copy-start.18 = (f32[32,64,128]{2,1,0:T(8,128)S(1)}, f32[32,64,128]{2,1,0:T(8,128)}, u32[]{:S(2)}) copy-start(f32[32,64,128]{2,1,0:T(8,128)} %get-tuple-element.106) | copy-start | bytes 3145732
  941.6 74.7 %reduce-scatter.16.cloned.1.call-start = ((), (), s32[]{:S(2)}) async-start(), calls=%async_computation.19 | async-start | bytes 1179648 | tf_op jit(solution)/shard_map/reduce_scatter | solution.py:77
  978.4 129.1 %reduce-scatter.20.cloned.1.call-start = ((), (), s32[]{:S(2)}) async-start(), calls=%async_computation.21 | async-start | bytes 147456 | tf_op jit(solution)/shard_map/reduce_scatter | solution.py:279
  984.4 174.8 %reduce-scatter.18.cloned.1.call-start = ((), (), s32[]{:S(2)}) async-start(), calls=%async_computation.20 | async-start | bytes 4718592 | tf_op jit(solution)/shard_map/reduce_scatter | solution.py:386
  1080.1 121.3 %reduce-scatter.22.cloned.1.call-start = ((), (), s32[]{:S(2)}) async-start(), calls=%async_computation.23 | async-start | bytes 147456
  1107.3 227.7 %all-reduce.19.cloned.1.call-start = ((), (), s32[]{:S(2)}) async-start(), calls=%async_computation.22 | async-start | bytes 5586944 | tf_op jit(solution)/shard_map/psum | solution.py:87
  (151 other events, 1264.8 us)
Sparse Core Ops, SparseCore 0:
  13.1 30.3 all-gather.6
  77.2 56.4 all-gather.8
  171.7 35.5 all-gather.10
  233.3 43.2 reduce-scatter.9
  289.2 54.3 all-gather.12
  356.8 86.0 all-reduce.12
  454.3 44.8 all-gather.14
  541.0 85.2 all-reduce.14
  640.2 114.8 reduce-scatter.11
  772.4 45.9 all-gather.16
  837.1 69.9 reduce-scatter.13
  941.7 33.9 all-reduce.16
  979.2 37.0 reduce-scatter.15
  1020.0 33.1 reduce-scatter.19
  1080.2 51.4 reduce-scatter.17
  1134.8 33.0 reduce-scatter.21
  1199.1 135.7 all-reduce.18
where the time goes:
time: 1370 us; the launch traced here: 1360 us
  waiting for transfers between devices  802 us (59%)
  local copies, waits for them, and re-layouts  246 us (18%)
  matrix products  219 us (16%)
  other arithmetic  75.2 us (5%)
  between operations  16.4 us (1%)
    reduce_scatter x3, waiting for transfers between devices, owners_sum(): return lax.psum_scatter(value, 'seq', scatter_dimension=0, tiled=True)  200 us
    psum x1, waiting for transfers between devices, sum_flat(): summed = lax.psum(flat, ('seq', 'res'))  130 us
    psum x2, waiting for transfers between devices, across_res(): return lax.psum(value.astype(jnp.bfloat16), 'res').astype(jnp.float32)  94 us
    all_gather x2, waiting for transfers between devices, gather_rows(): return lax.all_gather(value, 'seq', axis=0, tiled=True)  88.5 us
    psum x1, waiting for transfers between devices, spread_2(): return lax.psum(kept, axis)  78.6 us
    all_gather x1, waiting for transfers between devices, shards(): everyone = lax.all_gather(outer_in, ('seq', 'res'), axis=0, tiled=True)  55.5 us
    all_gather x1, waiting for transfers between devices, shards(): d_tri_all = lax.all_gather(d_triangle_b, 'res', axis=1, tiled=True)  46.1 us
    unnamed x347, local copies, waits for them, and re-layouts  43.8 us
  transfers between devices with their start and end apart: 17, of which 14 were waited for; matrix products, arithmetic and copies ran while one was open for 18% of the time, Pallas kernels for 0%

commit v1 on v0

--- a/solution.py
+++ b/solution.py
@@ -1,6 +1,11 @@
+import functools
+from types import SimpleNamespace
+
 import jax
 import jax.numpy as jnp
 from jax import lax
+from jax.experimental import pallas as pl
+from jax.experimental.pallas import tpu as pltpu
 from jax.sharding import PartitionSpec as P
 
 HEADS = 8
@@ -440,9 +445,1280 @@
     )
 
 
+F32 = jnp.float32
+BF16 = jnp.bfloat16
+MESH = pl.DeviceIdType.MESH
+LANES = 128
+CHUNK = 256
+
+
+def dot_nn(a, b):
+    return jnp.dot(a, b, preferred_element_type=F32)
+
+
+def dot_nt(a, b):
+    return lax.dot_general(a, b, (((1,), (1,)), ((), ())), preferred_element_type=F32)
+
+
+def dot_tn(a, b):
+    return lax.dot_general(a, b, (((0,), (0,)), ((), ())), preferred_element_type=F32)
+
+
+def split_terms(value, terms):
+    parts = []
+    for _ in range(terms):
+        part = value.astype(BF16)
+        parts.append(part)
+        value = value - part.astype(F32)
+    return parts
+
+
+def pick_nn(value, hot, terms):
+    return sum(dot_nn(part, hot) for part in split_terms(value, terms))
+
+
+def pick_nt(value, hot, terms):
+    return sum(dot_nt(part, hot) for part in split_terms(value, terms))
+
+
+def iota(shape, axis):
+    return lax.broadcasted_iota(jnp.int32, shape, axis)
+
+
+def hot_bf16(cond):
+    return jnp.where(cond, 1.0, 0.0).astype(BF16)
+
+
+def sigmoid(value):
+    return 0.5 * jnp.tanh(0.5 * value) + 0.5
+
+
+def norm(value, axis):
+    centred = value - jnp.mean(value, axis, keepdims=True)
+    rstd = lax.rsqrt(jnp.mean(centred * centred, axis, keepdims=True) + EPS)
+    return centred * rstd, rstd
+
+
+def norm_back(grad, gain, hat, rstd, axis):
+    scaled = grad * gain
+    first = jnp.mean(scaled, axis, keepdims=True)
+    second = jnp.mean(scaled * hat, axis, keepdims=True)
+    return rstd * (scaled - first - hat * second)
+
+
+def column(row):
+    size = row.shape[1]
+    eye = iota((size, size), 0) == iota((size, size), 1)
+    return jnp.sum(jnp.where(eye, row, 0.0), 1, keepdims=True)
+
+
+def lane_group(ref, j):
+    return jnp.concatenate(
+        [ref[pl.ds(2 * j + q, LANES, stride=16), :] for q in range(2)], axis=1
+    )
+
+
+def lane_ungroup(ref, j, value):
+    for q in range(2):
+        ref[pl.ds(2 * j + q, LANES, stride=16), :] = value[:, q * LANES : (q + 1) * LANES]
+
+
+def chunk_at(j):
+    return pl.ds(pl.multiple_of(j * CHUNK, CHUNK), CHUNK)
+
+
+def all_peers(D, t):
+    return lax.rem(D.s + t // D.nr, D.ns), lax.rem(D.r + t % D.nr, D.nr)
+
+
+def seq_peers(D, t):
+    return lax.rem(D.s + t, D.ns), D.r
+
+
+def res_peers(D, t):
+    return D.s, lax.rem(D.r + t, D.nr)
+
+
+def remote(src, dst, sems, slot, peer):
+    return pltpu.make_async_remote_copy(
+        src_ref=src,
+        dst_ref=dst,
+        send_sem=sems[0].at[slot],
+        recv_sem=sems[1].at[slot],
+        device_id=peer,
+        device_id_type=MESH,
+    )
+
+
+def swap(D, src_at, dst_at, sems, count, peers, index, me):
+    def copy(t):
+        peer = peers(D, t)
+        return remote(src_at(index(*peer)), dst_at(me), sems, t, peer)
+
+    @pl.loop(1, count)
+    def _(t):
+        copy(t).start()
+
+    return copy
+
+
+def swap_wait(copy, count):
+    @pl.loop(1, count)
+    def _(t):
+        copy(t).wait()
+
+
+def swap_all(R, D, src, dst, sems):
+    n = D.ns * D.nr
+    me = D.s * D.nr + D.r
+    copy = swap(
+        D,
+        lambda i: src.at[i],
+        lambda i: dst.at[i],
+        sems,
+        n,
+        all_peers,
+        lambda ps, pr: ps * D.nr + pr,
+        me,
+    )
+    dst[me] = src[me]
+    swap_wait(copy, n)
+
+
+def p_pack(R, D):
+    for q in range(4):
+        rows = R.x[q].astype(F32)
+        adjoint = R.adj_a[q].astype(F32)
+        for d in range(8):
+            both = jnp.concatenate([rows[8 * d : 8 * d + 8], adjoint[8 * d : 8 * d + 8]], 0)
+            R.xsend[d, q] = both.astype(BF16)
+
+
+def p_spread(R, D, sems):
+    copy = swap(
+        D,
+        lambda i: R.xsend.at[i],
+        lambda i: R.xrecv.at[i],
+        sems,
+        D.ns,
+        seq_peers,
+        lambda ps, pr: ps,
+        D.s,
+    )
+    R.xrecv[D.s] = R.xsend[D.s]
+    swap_wait(copy, D.ns)
+    for d in range(8):
+        for q in range(4):
+            both = R.xrecv[d, q].astype(F32)
+            rows = pl.ds(4 * d + q, 8, stride=32)
+            for half, stages in ((0, (R.sp0, R.sp2)), (1, (R.sp1, R.sp3))):
+                lanes = slice(LANES * half, LANES * half + LANES)
+                stages[0][rows, :] = both[:8, lanes]
+                stages[1][rows, :] = both[8:, lanes]
+    R.xc[...] = jnp.concatenate([R.sp0[...], R.sp1[...]], 1)
+    R.ac[...] = jnp.concatenate([R.sp2[...], R.sp3[...]], 1)
+
+
+def flag_column(flags):
+    here = iota((256, 32), 0) % 32 == iota((256, 32), 1)
+    return jnp.sum(jnp.where(here, flags, 0.0), 1, keepdims=True)
+
+
+def head_probs(keys, query, flag_rows, head):
+    lanes = iota((1, 256), 1) // 32
+    mine = hot_bf16(lanes == head)
+    scores = dot_nt(keys, query * mine) * (32 ** (-0.5))
+    same = iota((256, 256), 0) // 32 == iota((256, 256), 1) // 32
+    scores = jnp.where(same, jnp.where(flag_rows > 0, scores, -1e30), -3e38)
+    weights = jnp.exp(scores - jnp.max(scores, 0, keepdims=True))
+    return weights / jnp.sum(weights, 0, keepdims=True)
+
+
+def p_attention(R, D):
+    flag_rows = flag_column(R.fl[...].astype(F32))
+    hat, _ = norm(R.xc[...], -1)
+    normed = (hat * R.g1[...]).astype(BF16)
+    projected = dot_nn(normed, R.w_qkvg[...])
+    R.qkv[...] = projected[:, :768].astype(BF16)
+    R.gl[...] = projected[:, 768:]
+    R.att[...] = jnp.zeros((256, 256), F32)
+
+    @pl.loop(0, 8)
+    def _(head):
+        probs = head_probs(R.qkv[:, 256:512], R.qkv[:, :256], flag_rows, head).astype(BF16)
+        lanes = iota((1, 256), 1) // 32
+        R.att[...] += jnp.where(lanes == head, dot_tn(probs, R.qkv[:, 512:768]), 0.0)
+
+    gated = (sigmoid(R.gl[...]) * R.att[...]).astype(BF16)
+    later = R.xc[...] + dot_nn(gated, R.w_ao[...])
+    R.msan[...] = later
+    hat2, _ = norm(later, -1)
+    normed2 = (hat2 * R.g2[...]).astype(BF16)
+    outer_in = (dot_nt(normed2, R.w_oit[...]) * (flag_rows > 0).astype(F32)).astype(BF16)
+    wide = jnp.concatenate([outer_in.astype(F32), jnp.zeros((256, 64), F32)], 1)
+    R.lsend[...] = wide.T[:32].astype(BF16)
+    spread = hot_bf16(iota((64, 1024), 0) == 32 + iota((64, 1024), 1) // 32)
+    kept = iota((256, 1024), 0) % 32 == iota((256, 1024), 1) % 32
+    rows = jnp.where(kept, dot_nn(outer_in, spread), 0.0).astype(BF16)
+    R.rsend[...] = dot_nn(hot_bf16(iota((8, 256), 0) == iota((8, 256), 1) // 32), rows)
+
+
+def p_outer_exchange(R, D, sems):
+    owner = 2 * D.r + D.s // 4
+    slot = D.s % 4
+
+    def left(k):
+        return remote(R.lsend, R.lall.at[slot], sems, k, (owner, k))
+
+    for k in range(4):
+        mine = (owner == D.s) & (D.r == k)
+
+        @pl.when(jnp.logical_not(mine))
+        def _():
+            pltpu.make_async_remote_copy(
+                src_ref=R.lsend,
+                dst_ref=R.lall.at[slot],
+                send_sem=sems[0].at[k],
+                recv_sem=sems[1].at[slot],
+                device_id=(owner, k),
+                device_id_type=MESH,
+            ).start()
+
+        @pl.when(mine)
+        def _():
+            R.lall[slot] = R.lsend[...]
+
+    here = pl.ds(pl.multiple_of(8 * D.s, 8), 8)
+
+    def right(t):
+        return remote(R.rsend, R.rall.at[here], sems, 4 + t, seq_peers(D, t))
+
+    @pl.loop(1, 8)
+    def _(t):
+        right(t).start()
+
+    R.rall[here, :] = R.rsend[...]
+
+    for k in range(4):
+        mine = (owner == D.s) & (D.r == k)
+        theirs = (4 * (D.s % 2) + k == D.s) & (D.s // 2 == D.r)
+        token = pltpu.make_async_remote_copy(
+            src_ref=R.lsend,
+            dst_ref=R.lall.at[k],
+            send_sem=sems[0].at[k],
+            recv_sem=sems[1].at[k],
+            device_id=(owner, k),
+            device_id_type=MESH,
+        )
+
+        @pl.when(jnp.logical_not(mine))
+        def _():
+            token.wait_send()
+
+        @pl.when(jnp.logical_not(theirs))
+        def _():
+            token.wait_recv()
+
+    @pl.loop(1, 8)
+    def _(t):
+        right(t).wait()
+
+
+def stage_outer_weight(R):
+    R.st0[0:1024, :] = R.w_oo[...].astype(F32)
+
+
+def outer_weight(R, d):
+    return R.st0[pl.ds(d, 32, stride=32), :].astype(BF16)
+
+
+def count_of(R):
+    return jnp.sum(R.fl[...].astype(F32), 1, keepdims=True)
+
+
+def p_outer(R, D):
+    stage_outer_weight(R)
+    for q in range(4):
+        wide = jnp.concatenate([R.lall[q].astype(F32), jnp.zeros((96, 256), F32)], 0)
+        R.l2[256 * q : 256 * q + 256, :] = wide.T[:, :32].astype(BF16)
+
+    @pl.loop(0, 32)
+    def _(d):
+        part = dot_nn(R.l2[...], outer_weight(R, d)).astype(BF16)
+        at = pl.ds(pl.multiple_of(32 * d, 32), 32)
+        for i in range(32):
+            R.zb[i, at, :] = part[32 * i : 32 * i + 32]
+
+    inverse = 1.0 / count_of(R)
+
+    @pl.loop(0, 16)
+    def _(m):
+        right = R.rall[...].astype(BF16)
+        halves = []
+        for h in range(2):
+            i = 16 * h + m
+            halves.append(dot_nn(right, R.zb[i]) * inverse + R.pe[i].astype(F32))
+        R.pair1[:, pl.ds(pl.multiple_of(m * LANES, LANES), LANES)] = jnp.concatenate(halves, 0).T
+
+
+def entry_chunk(R, pair, gain, w_t, nb, j):
+    hat, _ = norm(pair, 0)
+    nb_here = (hat * gain).astype(BF16)
+    nb[:, chunk_at(j)] = nb_here
+    for k, stage in ((0, R.st0), (1, R.st1)):
+        linear = dot_nn(w_t[256 * k : 256 * k + 256, :], nb_here)
+        lane_ungroup(stage, j, sigmoid(linear[128:]) * linear[:128])
+
+
+def pack_both(R, send):
+    @pl.loop(0, 32)
+    def _(d):
+        at = pl.ds(pl.multiple_of(64 * d, 64), 64)
+        send[d, 0:64, :] = R.st0[at, :].astype(BF16)
+        send[d, 64:128, :] = R.st1[at, :].astype(BF16)
+
+
+def p_entry1(R, D):
+    R.w1t[...] = R.w_ti[...].astype(F32).T.astype(BF16)
+    gain = column(R.g3[...])
+
+    @pl.loop(0, 8)
+    def _(j):
+        entry_chunk(R, R.pair1[:, chunk_at(j)], gain, R.w1t, R.nb3, j)
+
+    pack_both(R, R.lrs)
+
+
+def gather_mats(recv, mats, first, rows, at):
+    @pl.loop(0, 8)
+    def _(s):
+        top = pl.ds(pl.multiple_of(32 * s, 32), 16)
+        low = pl.ds(pl.multiple_of(32 * s + 16, 16), 16)
+        for c in range(4):
+            off = first + 16 * c
+            for p in range(2):
+                a = recv[4 * s + 2 * p, off : off + 16, :]
+                b = recv[4 * s + 2 * p + 1, off : off + 16, :]
+                lanes = slice(LANES * p, LANES * p + LANES)
+                mats[at + c, top, lanes] = jnp.concatenate([a[:, :64], b[:, :64]], 1)
+                mats[at + c, low, lanes] = jnp.concatenate([a[:, 64:], b[:, 64:]], 1)
+
+
+def scatter_mat(mat, send, off):
+    @pl.loop(0, 8)
+    def _(s):
+        for p in range(2):
+            lanes = slice(LANES * p, LANES * p + LANES)
+            a = mat[pl.ds(pl.multiple_of(32 * s, 32), 16), lanes]
+            b = mat[pl.ds(pl.multiple_of(32 * s + 16, 16), 16), lanes]
+            send[4 * s + 2 * p, off : off + 16, :] = jnp.concatenate([a[:, :64], b[:, :64]], 1)
+            send[4 * s + 2 * p + 1, off : off + 16, :] = jnp.concatenate([a[:, 64:], b[:, 64:]], 1)
+
+
+def tri_forward(R, mats, send, product):
+    for c in range(4):
+        R.tm[...] = product(mats[c], mats[4 + c]).astype(BF16)
+        scatter_mat(R.tm, send, 16 * c)
+
+
+def tri_backward(R, recv, mats, send, products):
+    gather_mats(recv, R.dm, 0, 64, 0)
+    for c in range(4):
+        for k in range(2):
+            R.tm[...] = products[k](mats[c], mats[4 + c], R.dm[c]).astype(BF16)
+            scatter_mat(R.tm, send, 64 * k + 16 * c)
+
+
+def p_tri1(R, D, sems):
+    swap_all(R, D, R.lrs, R.lr1r, sems[0:2])
+    gather_mats(R.lr1r, R.mats1, 0, 64, 0)
+    gather_mats(R.lr1r, R.mats1, 64, 64, 4)
+    tri_forward(R, R.mats1, R.ts, dot_nt)
+    swap_all(R, D, R.ts, R.t1r, sems[2:4])
+
+
+def stage_single(recv, stage):
+    @pl.loop(0, 32)
+    def _(d):
+        stage[pl.ds(pl.multiple_of(64 * d, 64), 64), :] = recv[d].astype(F32)
+
+
+def stage_both(recv, first, second):
+    @pl.loop(0, 32)
+    def _(d):
+        at = pl.ds(pl.multiple_of(64 * d, 64), 64)
+        first[at, :] = recv[d, 0:64, :].astype(F32)
+        second[at, :] = recv[d, 64:128, :].astype(F32)
+
+
+def p_middle(R, D):
+    stage_single(R.t1r, R.st2)
+    R.w2t[...] = R.w_ii[...].astype(F32).T.astype(BF16)
+    R.wo1t[...] = R.w_to[...].astype(F32).T.astype(BF16)
+    gain4 = column(R.g4[...])
+    gain5 = column(R.g5[...])
+
+    @pl.loop(0, 8)
+    def _(j):
+        hat, _ = norm(lane_group(R.st2, j), 0)
+        nb4 = (hat * gain4).astype(BF16)
+        R.nb4[:, chunk_at(j)] = nb4
+        update = dot_nn(R.wo1t[...], nb4)
+        gate = sigmoid(dot_nn(R.w1t[512:, :], R.nb3[:, chunk_at(j)]))
+        pair2 = R.pair1[:, chunk_at(j)] + gate * update
+        R.pair2[:, chunk_at(j)] = pair2
+        entry_chunk(R, pair2, gain5, R.w2t, R.nb5, j)
+
+    pack_both(R, R.lrs)
+
+
+def p_tri2(R, D, sems):
+    swap_all(R, D, R.lrs, R.lr2r, sems[0:2])
+    gather_mats(R.lr2r, R.mats2, 0, 64, 0)
+    gather_mats(R.lr2r, R.mats2, 64, 64, 4)
+    tri_forward(R, R.mats2, R.ts, dot_tn)
+    swap_all(R, D, R.ts, R.t2r, sems[2:4])
+
+
+def p_turn(R, D):
+    stage_single(R.t2r, R.st2)
+    R.wo2t[...] = R.w_io[...].astype(F32).T.astype(BF16)
+    gain6 = column(R.g6[...])
+    dist = column(R.w_ds[...])
+    turn_weight = column(R.w_sl[...])
+    inv_k = 1.0 / R.ca.shape[1]
+    R.at8[...] = jnp.zeros((8, 256), F32)
+    R.at8[0:3, :] = R.at[...]
+    R.la8[...] = jnp.zeros((8, 32), F32)
+    R.la8[0:3, :] = R.adj_l[...]
+    node = dot_tn(R.vet[...].astype(BF16), R.w_nd[...])
+    R.nodet[...] = node.T
+    R.dmean[...] = dot_nt(R.w_up[...], R.adj_v[...].astype(BF16))
+    near = hot_bf16(iota((256, CHUNK), 0) == 64 * D.r + iota((256, CHUNK), 1) % 64)
+    R.nbase[...] = pick_nn(R.nodet[64:, :], near, 2)
+    R.cbase[...] = pick_nn(R.at8[...], near, 3)
+    for acc in (R.s_mean, R.s_own, R.s_other):
+        acc[...] = jnp.zeros(acc.shape, F32)
+    R.s_xyz[...] = jnp.zeros((16, 256), F32)
+    R.a_g6[...] = jnp.zeros((128, CHUNK), F32)
+    R.a_dist[...] = jnp.zeros((64, CHUNK), F32)
+    R.a_coord[...] = jnp.zeros((64, CHUNK), F32)
+    R.nb_f[...] = R.ca[...].astype(F32)
+
+    @pl.loop(0, 8)
+    def _(j):
+        here = chunk_at(j)
+        hat, rstd = norm(lane_group(R.st2, j), 0)
+        nb6 = (hat * gain6).astype(BF16)
+        R.nb6[:, here] = nb6
+        update2 = dot_nn(R.wo2t[...], nb6)
+        gate2 = sigmoid(dot_nn(R.w2t[512:, :], R.nb5[:, here]))
+        pair3 = R.pair2[:, here] + gate2 * update2
+        po_b = pair3.astype(BF16)
+        R.po[:, here] = po_b
+        lane = iota((1, CHUNK), 1)
+        local_row = 16 * ((lane % LANES) // 64) + 2 * j + lane // LANES
+        mine = hot_bf16(iota((32, CHUNK), 0) == local_row)
+        row = hot_bf16(iota((256, CHUNK), 0) == 32 * D.s + local_row)
+        named = dot_tn(R.nb_f[...].astype(BF16), mine)
+        target = (64 * D.r + lane % 64).astype(F32)
+        mask = jnp.max(jnp.where(named == target, 1.0, 0.0), 0, keepdims=True) * inv_k
+        diff = pick_nn(R.at8[...], row, 3) - R.cbase[...]
+        square = 1.0 + jnp.sum(diff * diff, 0, keepdims=True)
+        radial = jnp.log(square)
+        edge = dot_nn(R.w_edt[...], po_b)
+        pre = pick_nn(R.nodet[0:64, :], row, 2) + R.nbase[...] + edge + radial * dist
+        sig_pre = sigmoid(pre)
+        hidden = (pre * sig_pre).astype(BF16)
+        R.hid[:, here] = hidden
+        msg = dot_tn(R.w_ms[...], hidden)
+        sig_msg = sigmoid(msg)
+        message = msg * sig_msg
+        turn = jnp.tanh(jnp.sum(message * turn_weight, 0, keepdims=True))
+        R.s_mean[...] += pick_nt(message * mask, row, 2)
+        locadj = pick_nn(R.la8[...], mine, 3)
+        d_turn = jnp.sum(locadj * diff, 0, keepdims=True) * mask * (1.0 - turn * turn)
+        d_message = pick_nn(R.dmean[...], mine, 2) * mask + turn_weight * d_turn
+        R.a_coord[...] += message * d_turn
+        d_msg = (d_message * sig_msg * (1.0 + msg * (1.0 - sig_msg))).astype(BF16)
+        R.dmsg[:, here] = d_msg
+        d_pre = dot_nn(R.w_ms[...], d_msg) * sig_pre * (1.0 + pre * (1.0 - sig_pre))
+        R.a_dist[...] += d_pre * radial
+        d_edge = d_pre.astype(BF16)
+        R.dedge[:, here] = d_edge
+        R.s_own[...] += pick_nt(d_pre, row, 2)
+        R.s_other[...] += pick_nt(d_pre, near, 2)
+        d_radial = jnp.sum(d_pre * dist, 0, keepdims=True)
+        d_diff = (2.0 * d_radial / square) * diff + locadj * (turn * mask)
+        R.s_xyz[0:8, :] += pick_nt(diff * (turn * mask), row, 2)
+        R.s_xyz[8:16, :] += pick_nt(d_diff, row, 2) - pick_nt(d_diff, near, 2)
+        d_po = dot_tn(R.w_edt[...], d_edge)
+        adjoint = []
+        for q in range(2):
+            m = 2 * j + q
+            both = jnp.concatenate([R.adj_c[m], R.adj_c[16 + m]], 0).astype(F32)
+            adjoint.append(both.T)
+            out = pair3[:, q * LANES : (q + 1) * LANES].T.astype(BF16)
+            R.pair_out[m] = out[:64]
+            R.pair_out[16 + m] = out[64:]
+        d_pair3 = jnp.concatenate(adjoint, 1) + d_po
+        R.dpair[:, here] = d_pair3
+        d_up = (d_pair3 * gate2).astype(BF16)
+        R.dup2[:, here] = d_up
+        R.dtri2[512:, here] = (d_pair3 * update2 * gate2 * (1.0 - gate2)).astype(BF16)
+        d_nb = dot_nn(R.w_io[...], d_up)
+        R.a_g6[...] += d_nb * hat
+        lane_ungroup(R.st0, j, norm_back(d_nb, gain6, hat, rstd, 0))
+
+    R.g_io[...] = dot_nt(R.nb6[...], R.dup2[...])
+    R.g_ed[...] = dot_nt(R.dedge[...], R.po[...])
+    R.g_ms[...] = dot_nt(R.hid[...], R.dmsg[...])
+    R.gg6[...] = jnp.sum(R.a_g6[...], 1, keepdims=True)
+    R.g_ds[...] = jnp.sum(R.a_dist[...], 1, keepdims=True)
+    R.g_sl[...] = jnp.sum(R.a_coord[...], 1, keepdims=True)
+    pack_single(R, R.ts)
+
+
+def pack_single(R, send):
+    @pl.loop(0, 32)
+    def _(d):
+        send[d] = R.st0[pl.ds(pl.multiple_of(64 * d, 64), 64), :].astype(BF16)
+
+
+def p_back2(R, D, sems):
+    swap_all(R, D, R.ts, R.dt2r, sems[0:2])
+    tri_backward(
+        R,
+        R.dt2r,
+        R.mats2,
+        R.lrs,
+        (lambda a, b, d: dot_nt(b, d), lambda a, b, d: dot_nn(a, d)),
+    )
+    swap_all(R, D, R.lrs, R.dlr2r, sems[2:4])
+
+
+def gates_back(R, d_tri, w_t, nb_here, j):
+    here = chunk_at(j)
+    for k, stage in ((0, R.st0), (1, R.st1)):
+        grad = lane_group(stage, j)
+        linear = dot_nn(w_t[256 * k : 256 * k + 256, :], nb_here)
+        gate = sigmoid(linear[128:])
+        d_first = grad * gate
+        d_tri[256 * k : 256 * k + 128, here] = d_first.astype(BF16)
+        d_tri[256 * k + 128 : 256 * k + 256, here] = (
+            d_first * linear[:128] * (1.0 - gate)
+        ).astype(BF16)
+
+
+def p_between(R, D):
+    stage_both(R.dlr2r, R.st0, R.st1)
+    stage_single(R.t1r, R.st2)
+    gain4 = column(R.g4[...])
+    gain5 = column(R.g5[...])
+    R.a_g4[...] = jnp.zeros((128, CHUNK), F32)
+    R.a_g5[...] = jnp.zeros((128, CHUNK), F32)
+
+    @pl.loop(0, 8)
+    def _(j):
+        here = chunk_at(j)
+        gates_back(R, R.dtri2, R.w2t, R.nb5[:, here], j)
+        d_nb5 = dot_nn(R.w_ii[...], R.dtri2[:, here])
+        hat5, rstd5 = norm(R.pair2[:, here], 0)
+        R.a_g5[...] += d_nb5 * hat5
+        d_pair2 = R.dpair[:, here] + norm_back(d_nb5, gain5, hat5, rstd5, 0)
+        R.dpair[:, here] = d_pair2
+        gate = sigmoid(dot_nn(R.w1t[512:, :], R.nb3[:, here]))
+        update = dot_nn(R.wo1t[...], R.nb4[:, here])
+        d_up = (d_pair2 * gate).astype(BF16)
+        R.dup1[:, here] = d_up
+        R.dtri1[512:, here] = (d_pair2 * update * gate * (1.0 - gate)).astype(BF16)
+        d_nb4 = dot_nn(R.w_to[...], d_up)
+        hat4, rstd4 = norm(lane_group(R.st2, j), 0)
+        R.a_g4[...] += d_nb4 * hat4
+        lane_ungroup(R.st3, j, norm_back(d_nb4, gain4, hat4, rstd4, 0))
+
+    R.g_ii[...] = dot_nt(R.nb5[...], R.dtri2[...])
+    R.g_to[...] = dot_nt(R.nb4[...], R.dup1[...])
+    R.gg5[...] = jnp.sum(R.a_g5[...], 1, keepdims=True)
+    R.gg4[...] = jnp.sum(R.a_g4[...], 1, keepdims=True)
+
+    @pl.loop(0, 32)
+    def _(d):
+        R.ts[d] = R.st3[pl.ds(pl.multiple_of(64 * d, 64), 64), :].astype(BF16)
+
+
+def p_back1(R, D, sems):
+    swap_all(R, D, R.ts, R.dt1r, sems[0:2])
+    tri_backward(
+        R,
+        R.dt1r,
+        R.mats1,
+        R.lrs,
+        (lambda a, b, d: dot_nn(d, b), lambda a, b, d: dot_tn(d, a)),
+    )
+    swap_all(R, D, R.lrs, R.dlr1r, sems[2:4])
+
+
+def p_pair_end(R, D):
+    stage_both(R.dlr1r, R.st0, R.st1)
+    gain3 = column(R.g3[...])
+    R.a_g3[...] = jnp.zeros((128, CHUNK), F32)
+    inverse = 1.0 / count_of(R)
+
+    @pl.loop(0, 8)
+    def _(j):
+        here = chunk_at(j)
+        gates_back(R, R.dtri1, R.w1t, R.nb3[:, here], j)
+        d_nb3 = dot_nn(R.w_ti[...], R.dtri1[:, here])
+        hat3, rstd3 = norm(R.pair1[:, here], 0)
+        R.a_g3[...] += d_nb3 * hat3
+        d_pair1 = R.dpair[:, here] + norm_back(d_nb3, gain3, hat3, rstd3, 0)
+        for q in range(2):
+            m = 2 * j + q
+            out = d_pair1[:, q * LANES : (q + 1) * LANES].T
+            R.pair_grad[m] = out[:64]
+            R.pair_grad[16 + m] = out[64:]
+            small = (out * inverse).astype(BF16)
+            R.dopm[m] = small[:64]
+            R.dopm[16 + m] = small[64:]
+
+    R.g_ti[...] = dot_nt(R.nb3[...], R.dtri1[...])
+    R.gg3[...] = jnp.sum(R.a_g3[...], 1, keepdims=True)
+
+
+def p_outer_back(R, D):
+    stage_outer_weight(R)
+    R.rt[...] = R.rall[...].T.astype(BF16)
+    R.dright[...] = jnp.zeros((64, 1024), F32)
+    R.dleft[...] = jnp.zeros((32, 1024), F32)
+    for q in range(4):
+
+        @pl.loop(0, 8)
+        def _(k):
+            i = 8 * q + k
+            grad = R.dopm[i]
+            R.yb[k] = dot_nn(R.rt[...], grad).astype(BF16)
+            R.dright[...] += dot_nt(grad, R.zb[i])
+
+        @pl.loop(0, 32)
+        def _(d):
+            at = pl.ds(pl.multiple_of(32 * d, 32), 32)
+            rows = R.yb[:, at, :].reshape(256, LANES)
+            lanes = slice(256 * q, 256 * q + 256)
+            R.dleft[:, lanes] += dot_nt(outer_weight(R, d), rows)
+            total = dot_nn(R.lall[q], rows)
+            here = pl.ds(d, 32, stride=32)
+            if q:
+                total += R.st1[here, :]
+            R.st1[here, :] = total
+
+    R.g_oo[...] = R.st1[0:1024, :]
+    for q in range(4):
+        R.dls[q] = R.dleft[:, 256 * q : 256 * q + 256].astype(BF16)
+
+
+def p_outer_return(R, D, sems):
+    column_res = D.s // 2
+    owner = 2 * D.r + D.s // 4
+
+    def left(q, slot):
+        return pltpu.make_async_remote_copy(
+            src_ref=R.dls.at[q],
+            dst_ref=R.dlr.at[slot],
+            send_sem=sems[0].at[q],
+            recv_sem=sems[1].at[slot],
+            device_id=(4 * (D.s % 2) + q, column_res),
+            device_id_type=MESH,
+        )
+
+    for q in range(4):
+        mine = (4 * (D.s % 2) + q == D.s) & (column_res == D.r)
+
+        @pl.when(jnp.logical_not(mine))
+        def _():
+            left(q, D.r).start()
+
+        @pl.when(mine)
+        def _():
+            R.dlr[D.r] = R.dls[q]
+
+    def right(t):
+        peer = seq_peers(D, t)
+        at = pl.ds(pl.multiple_of(8 * peer[0], 8), 8)
+        return remote(R.dright.at[at], R.drr.at[D.s], sems, 4 + t, peer)
+
+    @pl.loop(1, 8)
+    def _(t):
+        right(t).start()
+
+    R.drr[D.s] = R.dright[pl.ds(pl.multiple_of(8 * D.s, 8), 8), :]
+
+    for q in range(4):
+        mine = (4 * (D.s % 2) + q == D.s) & (column_res == D.r)
+        theirs = (owner == D.s) & (D.r == q)
+
+        @pl.when(jnp.logical_not(mine))
+        def _():
+            left(q, q).wait_send()
+
+        @pl.when(jnp.logical_not(theirs))
+        def _():
+            left(q, q).wait_recv()
+
+    @pl.loop(1, 8)
+    def _(t):
+        right(t).wait()
+
+
+def p_attention_back(R, D):
+    flag_rows = flag_column(R.fl[...].astype(F32))
+    live = (flag_rows > 0).astype(F32)
+    left = R.dlr[0].astype(F32)
+    for k in range(1, 4):
+        left += R.dlr[k].astype(F32)
+    right = R.drr[0]
+    for k in range(1, 8):
+        right += R.drr[k]
+    wide = jnp.concatenate([left, jnp.zeros((96, 256), F32)], 0).T
+    spread = dot_nn(
+        hot_bf16(iota((256, 8), 0) // 32 == iota((256, 8), 1)), right.astype(BF16)
+    )
+    kept = iota((256, 1024), 0) % 32 == iota((256, 1024), 1) % 32
+    spread = jnp.where(kept, spread, 0.0).astype(BF16)
+    back = hot_bf16(32 + iota((1024, LANES), 0) // 32 == iota((1024, LANES), 1))
+    d_in = ((wide + dot_nn(spread, back)) * live).astype(BF16)[:, :64]
+    hat2, rstd2 = norm(R.msan[...], -1)
+    normed2 = (hat2 * R.g2[...]).astype(BF16)
+    R.g_oi[...] = dot_tn(d_in, normed2)
+    d_normed2 = dot_nn(d_in, R.w_oit[...])
+    R.gg2[...] = jnp.sum(d_normed2 * hat2, 0, keepdims=True)
+    d_later = R.ac[...] + norm_back(d_normed2, R.g2[...], hat2, rstd2, -1)
+    R.dlater[...] = d_later
+    d_exit = d_later.astype(BF16)
+    gate = sigmoid(R.gl[...])
+    gated = (gate * R.att[...]).astype(BF16)
+    R.g_ao[...] = dot_tn(gated, d_exit)
+    d_gated = dot_nt(d_exit, R.w_ao[...])
+    R.datt[...] = (d_gated * gate).astype(BF16)
+    R.dproj[:, 768:] = (d_gated * R.att[...] * gate * (1.0 - gate)).astype(BF16)
+    R.dqkv[...] = jnp.zeros((256, 768), F32)
+
+    @pl.loop(0, 8)
+    def _(head):
+        lanes = iota((1, 256), 1) // 32
+        mine = lanes == head
+        hot = hot_bf16(mine)
+        query = R.qkv[:, 0:256]
+        keys = R.qkv[:, 256:512]
+        probs = head_probs(keys, query, flag_rows, head)
+        d_att = R.datt[...]
+        d_probs = dot_nt(R.qkv[:, 512:768], d_att * hot)
+        total = jnp.sum(probs * d_probs, 0, keepdims=True)
+        d_scores = (probs * (d_probs - total) * (32 ** (-0.5))).astype(BF16)
+        R.dqkv[:, 0:256] += jnp.where(mine, dot_tn(d_scores, keys), 0.0)
+        R.dqkv[:, 256:512] += jnp.where(mine, dot_nn(d_scores, query), 0.0)
+        R.dqkv[:, 512:768] += jnp.where(mine, dot_nn(probs.astype(BF16), d_att), 0.0)
+
+    R.dproj[:, :768] = R.dqkv[...].astype(BF16)
+    hat, rstd = norm(R.xc[...], -1)
+    normed = (hat * R.g1[...]).astype(BF16)
+    R.g_qkvg[...] = dot_tn(normed, R.dproj[...])
+    d_normed = dot_nt(R.dproj[...], R.w_qkvg[...])
+    R.gg1[...] = jnp.sum(d_normed * hat, 0, keepdims=True)
+    R.dlater[...] += norm_back(d_normed, R.g1[...], hat, rstd, -1)
+
+    R.sp0[...] = R.msan[:, :LANES]
+    R.sp1[...] = R.msan[:, LANES:]
+    R.sp2[...] = R.dlater[:, :LANES]
+    R.sp3[...] = R.dlater[:, LANES:]
+    for d in range(8):
+        for q in range(4):
+            rows = pl.ds(4 * d + q, 8, stride=32)
+            value = jnp.concatenate([R.sp0[rows, :], R.sp1[rows, :]], 1)
+            grad = jnp.concatenate([R.sp2[rows, :], R.sp3[rows, :]], 1)
+            R.osend[d, q] = jnp.concatenate([value, grad], 0).astype(BF16)
+
+
+def p_collect(R, D, sems):
+    copy = swap(
+        D,
+        lambda i: R.osend.at[i],
+        lambda i: R.orecv.at[i],
+        sems,
+        D.ns,
+        seq_peers,
+        lambda ps, pr: ps,
+        D.s,
+    )
+    R.orecv[D.s] = R.osend[D.s]
+    swap_wait(copy, D.ns)
+    for q in range(4):
+        blocks = [R.orecv[d, q].astype(F32) for d in range(8)]
+        R.msa_out[q] = jnp.concatenate([b[:8] for b in blocks], 0).astype(BF16)
+        R.msa_grad[q] = jnp.concatenate([b[8:] for b in blocks], 0)
+
+
+def payload_layout():
+    layout = []
+    start = 0
+    shapes = dict(
+        g_qkvg=(256, 1024),
+        g_ao=(256, 256),
+        g_oo=(1024, 128),
+        g_ti=(128, 640),
+        g_ii=(128, 640),
+        g_to=(128, 128),
+        g_io=(128, 128),
+        s_mean=(64, 256),
+        s_own=(64, 256),
+        s_other=(64, 256),
+        s_vadj=(64, 256),
+        s_xyz=(16, 256),
+        g_oi=(64, 256),
+        g_ed=(64, 128),
+        g_ms=(64, 64),
+        small=(128, 128),
+    )
+    for name, (rows, cols) in shapes.items():
+        for lane in range(0, cols, LANES):
+            layout.append((name, start, rows, lane, min(LANES, cols - lane)))
+            start += rows
+    return layout, -(-start // 512) * 512
+
+
+def p_sum_pack(R, D):
+    rows = iota((32, 256), 0)
+    place = hot_bf16(iota((32, 256), 1) == 32 * D.s + rows)
+    first = jnp.where(D.r == 0, 1.0, 0.0)
+    R.s_vadj[...] = dot_tn(R.adj_v[...].astype(BF16), place) * first
+    R.small[...] = jnp.zeros((128, LANES), F32)
+    for k, name in enumerate(("gg3", "gg4", "gg5", "gg6", "g_ds", "g_sl")):
+        value = getattr(R, name)
+        R.small[0 : value.shape[0], k : k + 1] = value[...]
+    for k, name in enumerate(("gg1", "gg2")):
+        value = getattr(R, name)
+        for half in range(2):
+            R.small[:, 8 + 2 * k + half : 9 + 2 * k + half] = column(
+                value[:, LANES * half : LANES * half + LANES]
+            )
+    layout, total = payload_layout()
+    for name, start, count, lane, width in layout:
+        R.pay[start : start + count, 0:width] = getattr(R, name)[:, lane : lane + width].astype(
+            BF16
+        )
+    last = layout[-1]
+    end = last[1] + last[2]
+    if end < total:
+        R.pay[end:total, :] = jnp.zeros((total - end, LANES), BF16)
+
+
+def p_sum(R, D, sems):
+    eighth = R.pay.shape[0] // 8
+    part = eighth // 4
+
+    def rows(ref, index, size):
+        return ref.at[pl.ds(pl.multiple_of(index * size, size), size)]
+
+    copy = swap(
+        D,
+        lambda i: rows(R.pay, i, eighth),
+        lambda i: R.sum_a.at[i],
+        sems[0:2],
+        D.ns,
+        seq_peers,
+        lambda ps, pr: ps,
+        D.s,
+    )
+    swap_wait(copy, D.ns)
+    R.sum_a[D.s] = R.pay[pl.ds(pl.multiple_of(D.s * eighth, eighth), eighth), :]
+    total = R.sum_a[0].astype(F32)
+    for k in range(1, 8):
+        total += R.sum_a[k].astype(F32)
+    R.sum_b[...] = total.astype(BF16)
+    copy = swap(
+        D,
+        lambda i: rows(R.sum_b, i, part),
+        lambda i: R.sum_c.at[i],
+        sems[2:4],
+        D.nr,
+        res_peers,
+        lambda ps, pr: pr,
+        D.r,
+    )
+    swap_wait(copy, D.nr)
+    R.sum_c[D.r] = R.sum_b[pl.ds(pl.multiple_of(D.r * part, part), part), :]
+    total = R.sum_c[0].astype(F32)
+    for k in range(1, 4):
+        total += R.sum_c[k].astype(F32)
+    R.sum_d[...] = total.astype(BF16)
+    mine = pl.ds(pl.multiple_of(D.s * eighth + D.r * part, part), part)
+    R.full[mine, :] = R.sum_d[...]
+    copy = swap(
+        D,
+        lambda i: R.sum_d,
+        lambda i: R.full.at[mine],
+        sems[4:6],
+        D.nr,
+        res_peers,
+        lambda ps, pr: pr,
+        D.r,
+    )
+    swap_wait(copy, D.nr)
+    copy = swap(
+        D,
+        lambda i: rows(R.full, D.s, eighth),
+        lambda i: rows(R.full, i, eighth),
+        sems[6:8],
+        D.ns,
+        seq_peers,
+        lambda ps, pr: ps,
+        D.s,
+    )
+    swap_wait(copy, D.ns)
+
+
+def p_finish(R, D):
+    layout, _ = payload_layout()
+    held = {}
+    for name, start, count, lane, width in layout:
+        value = R.full[start : start + count, 0:width].astype(F32)
+        if name.startswith("g_"):
+            getattr(R, "o_" + name)[:, lane : lane + width] = value
+        else:
+            held.setdefault(name, []).append(value)
+    held = {name: jnp.concatenate(parts, 1) for name, parts in held.items()}
+    small = held["small"].T
+    for k, name in enumerate(("gg3", "gg4", "gg5", "gg6")):
+        getattr(R, "o_" + name)[...] = small[k : k + 1, :]
+    R.o_g_ds[...] = small[4:5, :64]
+    R.o_g_sl[...] = small[5:6, :64]
+    for k, name in enumerate(("gg1", "gg2")):
+        for half in range(2):
+            at = 8 + 2 * k + half
+            getattr(R, "o_" + name)[:, LANES * half : LANES * half + LANES] = small[at : at + 1]
+    mean_b = held["s_mean"].astype(BF16)
+    R.o_g_up[...] = dot_nt(mean_b, held["s_vadj"].astype(BF16))
+    d_node = jnp.concatenate([held["s_own"], held["s_other"]], 0).astype(BF16)
+    R.o_g_nd[...] = dot_nt(R.vet[...].astype(BF16), d_node)
+    step = dot_tn(R.w_up[...], mean_b)
+    grad = dot_nn(R.w_nd[...], d_node)
+    R.rows_f[...] = jnp.concatenate([step + R.vet[...], grad], 0).T
+    here = pl.ds(pl.multiple_of(32 * D.s, 32), 32)
+    mine = R.rows_f[here, :]
+    R.single_out[...] = mine[:, :64]
+    R.single_grad[...] = R.adj_v[...] + mine[:, 64:]
+    R.xyz[...] = jnp.zeros((128, 256), F32)
+    R.xyz[0:16, :] = held["s_xyz"]
+    R.xyz[16:19, :] = R.at[...]
+    R.rows_g[...] = R.xyz[...].T
+    turned = R.rows_g[here, :]
+    back = jnp.concatenate([turned, jnp.zeros((96, 128), F32)], 0).T
+    R.coords_out[...] = back[16:19, 0:32] + back[0:3, 0:32]
+    R.coords_grad[...] = R.adj_l[...] + back[8:11, 0:32]
+
+
+KEPT = dict(
+    xsend=((8, 4, 16, 256), BF16),
+    xrecv=((8, 4, 16, 256), BF16),
+    xc=((256, 256), F32),
+    ac=((256, 256), F32),
+    sp0=((256, 128), F32),
+    sp1=((256, 128), F32),
+    sp2=((256, 128), F32),
+    sp3=((256, 128), F32),
+    qkv=((256, 768), BF16),
+    gl=((256, 256), F32),
+    att=((256, 256), F32),
+    msan=((256, 256), F32),
+    lsend=((32, 256), BF16),
+    rsend=((8, 1024), F32),
+    lall=((4, 32, 256), BF16),
+    rall=((64, 1024), F32),
+    st0=((2048, 128), F32),
+    st1=((2048, 128), F32),
+    st2=((2048, 128), F32),
+    st3=((2048, 128), F32),
+    l2=((1024, 32), BF16),
+    zb=((32, 1024, 128), BF16),
+    yb=((8, 1024, 128), BF16),
+    pair1=((128, 2048), F32),
+    pair2=((128, 2048), F32),
+    dpair=((128, 2048), F32),
+    w1t=((640, 128), BF16),
+    w2t=((640, 128), BF16),
+    wo1t=((128, 128), BF16),
+    wo2t=((128, 128), BF16),
+    nb3=((128, 2048), BF16),
+    nb4=((128, 2048), BF16),
+    nb5=((128, 2048), BF16),
+    nb6=((128, 2048), BF16),
+    po=((128, 2048), BF16),
+    hid=((64, 2048), BF16),
+    dmsg=((64, 2048), BF16),
+    dedge=((64, 2048), BF16),
+    dup1=((128, 2048), BF16),
+    dup2=((128, 2048), BF16),
+    dtri1=((640, 2048), BF16),
+    dtri2=((640, 2048), BF16),
+    mats1=((8, 256, 256), BF16),
+    mats2=((8, 256, 256), BF16),
+    dm=((4, 256, 256), BF16),
+    tm=((256, 256), BF16),
+    lrs=((32, 128, 128), BF16),
+    lr1r=((32, 128, 128), BF16),
+    lr2r=((32, 128, 128), BF16),
+    dlr1r=((32, 128, 128), BF16),
+    dlr2r=((32, 128, 128), BF16),
+    ts=((32, 64, 128), BF16),
+    t1r=((32, 64, 128), BF16),
+    t2r=((32, 64, 128), BF16),
+    dt1r=((32, 64, 128), BF16),
+    dt2r=((32, 64, 128), BF16),
+    at8=((8, 256), F32),
+    la8=((8, 32), F32),
+    nodet=((128, 256), F32),
+    dmean=((64, 32), F32),
+    nbase=((64, 256), F32),
+    cbase=((8, 256), F32),
+    nb_f=((32, 64), F32),
+    s_mean=((64, 256), F32),
+    s_own=((64, 256), F32),
+    s_other=((64, 256), F32),
+    s_vadj=((64, 256), F32),
+    s_xyz=((16, 256), F32),
+    a_g3=((128, 256), F32),
+    a_g4=((128, 256), F32),
+    a_g5=((128, 256), F32),
+    a_g6=((128, 256), F32),
+    a_dist=((64, 256), F32),
+    a_coord=((64, 256), F32),
+    gg3=((128, 1), F32),
+    gg4=((128, 1), F32),
+    gg5=((128, 1), F32),
+    gg6=((128, 1), F32),
+    gg1=((1, 256), F32),
+    gg2=((1, 256), F32),
+    g_ds=((64, 1), F32),
+    g_sl=((64, 1), F32),
+    g_io=((128, 128), F32),
+    g_to=((128, 128), F32),
+    g_ti=((128, 640), F32),
+    g_ii=((128, 640), F32),
+    g_ed=((64, 128), F32),
+    g_ms=((64, 64), F32),
+    g_oo=((1024, 128), F32),
+    g_oi=((64, 256), F32),
+    g_ao=((256, 256), F32),
+    g_qkvg=((256, 1024), F32),
+    small=((128, 128), F32),
+    dopm=((32, 64, 128), BF16),
+    rt=((1024, 64), BF16),
+    dright=((64, 1024), F32),
+    dleft=((32, 1024), F32),
+    dls=((4, 32, 256), BF16),
+    dlr=((4, 32, 256), BF16),
+    drr=((8, 8, 1024), F32),
+    dlater=((256, 256), F32),
+    datt=((256, 256), BF16),
+    dproj=((256, 1024), BF16),
+    dqkv=((256, 768), F32),
+    osend=((8, 4, 16, 256), BF16),
+    orecv=((8, 4, 16, 256), BF16),
+)
+PAYLOAD = payload_layout()[1]
+KEPT.update(
+    pay=((PAYLOAD, 128), BF16),
+    sum_a=((8, PAYLOAD // 8, 128), BF16),
+    sum_b=((PAYLOAD // 8, 128), BF16),
+    sum_c=((4, PAYLOAD // 32, 128), BF16),
+    sum_d=((PAYLOAD // 32, 128), BF16),
+)
+LAST_ONLY = ()
+LARGE = ("msa_out", "pair_out", "msa_grad", "pair_grad")
+FINISH = ("full", "vet", "w_up", "w_nd", "adj_v", "at", "adj_l")
+FINISH_KEPT = dict(
+    rows_f=((256, 128), F32), rows_g=((256, 128), F32), xyz=((128, 256), F32)
+)
+MIDDLE = dict(full=((PAYLOAD, 128), BF16))
+RESULTS = dict(
+    msa_out=((4, 64, 256), BF16),
+    pair_out=((32, 64, 128), BF16),
+    single_out=((32, 64), F32),
+    coords_out=((3, 32), F32),
+    msa_grad=((4, 64, 256), F32),
+    pair_grad=((32, 64, 128), F32),
+    single_grad=((32, 64), F32),
+    coords_grad=((3, 32), F32),
+    o_gg1=((1, 256), F32),
+    o_g_qkvg=((256, 1024), F32),
+    o_g_ao=((256, 256), F32),
+    o_gg2=((1, 256), F32),
+    o_g_oi=((64, 256), F32),
+    o_g_oo=((1024, 128), F32),
+    o_gg3=((1, 128), F32),
+    o_g_ti=((128, 640), F32),
+    o_gg4=((1, 128), F32),
+    o_g_to=((128, 128), F32),
+    o_gg5=((1, 128), F32),
+    o_g_ii=((128, 640), F32),
+    o_gg6=((1, 128), F32),
+    o_g_io=((128, 128), F32),
+    o_g_nd=((64, 128), F32),
+    o_g_ed=((64, 128), F32),
+    o_g_ds=((1, 64), F32),
+    o_g_ms=((64, 64), F32),
+    o_g_sl=((1, 64), F32),
+    o_g_up=((64, 64), F32),
+)
+
+STEPS = (
+    (p_pack, 0),
+    (p_spread, 1),
+    (p_attention, 0),
+    (p_outer_exchange, 1),
+    (p_outer, 0),
+    (p_entry1, 0),
+    (p_tri1, 2),
+    (p_middle, 0),
+    (p_tri2, 2),
+    (p_turn, 0),
+    (p_back2, 2),
+    (p_between, 0),
+    (p_back1, 2),
+    (p_pair_end, 0),
+    (p_outer_back, 0),
+    (p_outer_return, 1),
+    (p_attention_back, 0),
+    (p_collect, 1),
+    (p_sum_pack, 0),
+    (p_sum, 4),
+)
+
+
+def first_kernel(n_seq, n_res, names, exchanges, *refs):
+    R = SimpleNamespace(**dict(zip(names, refs)))
+    sems = refs[len(names) :]
+    D = SimpleNamespace(s=lax.axis_index("seq"), r=lax.axis_index("res"), ns=n_seq, nr=n_res)
+    barrier = pltpu.get_barrier_semaphore()
+
+    @pl.loop(1, n_seq * n_res)
+    def _(t):
+        pl.semaphore_signal(barrier, inc=1, device_id=all_peers(D, t), device_id_type=MESH)
+
+    used = 0
+    for step, count in STEPS:
+        if count:
+            if not used:
+                pl.semaphore_wait(barrier, n_seq * n_res - 1)
+            step(R, D, sems[2 * used : 2 * used + 2 * count])
+            used += count
+        else:
+            step(R, D)
+
+
+def last_kernel(n_seq, n_res, names, *refs):
+    R = SimpleNamespace(**dict(zip(names, refs)))
+    D = SimpleNamespace(s=lax.axis_index("seq"), r=lax.axis_index("res"), ns=n_seq, nr=n_res)
+    p_finish(R, D)
+
+
+ARGS = dict(
+    x=(4, 64, 256),
+    pe=(32, 64, 128),
+    vet=(256, 64),
+    at=(3, 256),
+    fl=(32,),
+    ca=(32, 64),
+    g1=(256,),
+    w_qkvg=(256, 1024),
+    w_ao=(256, 256),
+    g2=(256,),
+    w_oit=(256, 64),
+    w_oo=(1024, 128),
+    g3=(128,),
+    w_ti=(128, 640),
+    g4=(128,),
+    w_to=(128, 128),
+    g5=(128,),
+    w_ii=(128, 640),
+    g6=(128,),
+    w_io=(128, 128),
+    w_nd=(64, 128),
+    w_edt=(128, 64),
+    w_ds=(64,),
+    w_ms=(64, 64),
+    w_sl=(64,),
+    w_up=(64, 64),
+    adj_a=(4, 64, 256),
+    adj_c=(32, 64, 128),
+    adj_v=(32, 64),
+    adj_l=(3, 32),
+)
+
+
+def fits(n_seq, n_res, args):
+    shapes = tuple(tuple(arg.shape) for arg in args)
+    return (n_seq, n_res) == (8, 4) and shapes == tuple(ARGS.values())
+
+
+def fast_shards(n_seq, n_res, *args):
+    env = dict(zip(ARGS, args))
+    for name, value in tuple(env.items()):
+        if value.ndim == 1:
+            env[name] = value.reshape(1, -1)
+    env.update(vet=env["vet"].T, w_oit=env["w_oit"].T, w_edt=env["w_edt"].T)
+    space = pl.BlockSpec(memory_space=pltpu.VMEM)
+    exchanges = sum(count for _, count in STEPS)
+    slots = n_seq * n_res
+
+    def shapes(table):
+        return [jax.ShapeDtypeStruct(*entry) for entry in table.values()]
+
+    large = {name: RESULTS[name] for name in LARGE}
+    middle = dict(**large, **MIDDLE)
+    inputs = [name for name in env if name not in LAST_ONLY]
+    values = pl.pallas_call(
+        functools.partial(first_kernel, n_seq, n_res, (*inputs, *middle, *KEPT), exchanges),
+        out_shape=shapes(middle),
+        in_specs=[space] * len(inputs),
+        out_specs=[space] * len(middle),
+        scratch_shapes=[pltpu.VMEM(*entry) for entry in KEPT.values()]
+        + [pltpu.SemaphoreType.DMA((slots,))] * (2 * exchanges),
+        compiler_params=pltpu.CompilerParams(
+            vmem_limit_bytes=60 * 2**20, collective_id=0, has_side_effects=True
+        ),
+    )(*[env[name] for name in inputs])
+    env.update(zip(middle, values))
+    small = {name: entry for name, entry in RESULTS.items() if name not in large}
+    inputs = [*FINISH]
+    values = pl.pallas_call(
+        functools.partial(last_kernel, n_seq, n_res, (*inputs, *small, *FINISH_KEPT)),
+        out_shape=shapes(small),
+        in_specs=[space] * len(inputs),
+        out_specs=[space] * len(small),
+        scratch_shapes=[pltpu.VMEM(*entry) for entry in FINISH_KEPT.values()],
+        compiler_params=pltpu.CompilerParams(vmem_limit_bytes=60 * 2**20),
+    )(*[env[name] for name in inputs])
+    env.update(zip(small, values))
+    results = [env[name] for name in RESULTS]
+    for index, value in enumerate(results):
+        if value.shape[0] == 1:
+            results[index] = value.reshape(-1)
+    for index in (12, 23):
+        results[index] = results[index].T
+    return tuple(results)
+
+
 def solution(mesh):
+    n_seq, n_res = mesh.shape["seq"], mesh.shape["res"]
+
+    def body(*args):
+        if fits(n_seq, n_res, args):
+            return fast_shards(n_seq, n_res, *args)
+        return shards(*args)
+
     return jax.shard_map(
-        shards,
+        body,
         mesh=mesh,
         in_specs=(
             P("seq", "res", None),

time: 1370 us -> 363 us (0.26)
  waiting for transfers between devices: 802 us -> 0 us
  Pallas kernels: 0 us -> 359 us
  local copies, waits for them, and re-layouts: 246 us -> 3.14 us
  matrix products: 219 us -> 0 us
  other arithmetic: 75.2 us -> 0 us
  between operations: 16.4 us -> 0.74 us
    pallas_call x0 -> x2, Pallas kernels: none -> 359 us  [the longest x1 356 us: fast_shards(): pl.pallas_call(functools.partial(first_kernel, n_seq, n_res, (*inputs, *m...]
    psum x4 -> x0, waiting for transfers between devices: 303 us -> none  [the longest x1 130 us: sum_flat(): summed = lax.psum(flat, ('seq', 'res'))]
    all_gather x6 -> x0, waiting for transfers between devices: 256 us -> none  [the longest x2 88.5 us: gather_rows(): return lax.all_gather(value, 'seq', axis=0, tiled=True)]
    reduce_scatter x6 -> x0, waiting for transfers between devices: 243 us -> none  [the longest x3 200 us: owners_sum(): return lax.psum_scatter(value, 'seq', scatter_dimension=0, tiled=True)]
    dot_general x59 -> x0, matrix products: 219 us -> none  [the longest x1 28.6 us: shards(): jnp.einsum('lhqk,qlhd->klhd', d_scores_b, query4, preferred_element_type=...]
    reshape x23 -> x0, local copies, waits for them, and re-layouts: 43.3 us -> none  [the longest x6 7 us: sum_flat(): flat = jnp.concatenate([jnp.ravel(member) for member in parts])]
    unnamed x347 -> x12, local copies, waits for them, and re-layouts: 43.8 us -> 3.14 us
    concatenate x1 -> x0, local copies, waits for them, and re-layouts: 35.9 us -> none  [sum_flat(): flat = jnp.concatenate([jnp.ravel(member) for member in parts])]
  transfers between devices with their start and end apart: 17 -> 0, of which waited for: 14 -> 0; matrix products, arithmetic and copies ran while one was open for 18% -> 0% of each run, Pallas kernels for 0% -> 0%
where the time goes in v1:
time: 363 us
  Pallas kernels  359 us (99%)
    pallas_call x1, Pallas kernels, fast_shards(): pl.pallas_call(functools.partial(first_kernel, n_seq, n_res, (*inputs, *m...  356 us

profile of v1, /device:TPU:1, one launch (start us, length us, event | category | flops | bytes accessed | tf_op | source)
XLA Modules:
  0.0 363.1 jit_solution(10919688371244328859)
XLA Ops:
  0.7 355.6 %shard_map.501 = (bf16[4,64,256]{2,1,0:T(8,128)(2,1)}, bf16[32,64,128]{2,1,0:T(8,128)(2,1)}, f32[4,64,256]{2,1,0:T(8,128)}, f32[32,64,128]{2,1,0:T(8,128)}, bf16[6144,128]{1,0:T(8,128)(2,1)}) custom-call(bf16[4,64,256]{2,1,0:T(8,128)(2,1)} %refs_0_.1, bf16[32,64,128]{2,1,0:T(8,128)(2,1)} %refs_1_.1, f32[64,256]{1,0:T(8,128)} %bitcast.22, f32[3,256]{1,0:T(4,128)} %refs_5_.3, ...), custom_call_target="tpu_custom_call" | custom-call | tf_op jit(solution)/shard_map/pallas_call | solution.py:1680
  356.3 0.0 copy-start.3
  356.3 0.0 copy-start.1
  356.3 0.0 copy-start.2
  356.3 0.0 copy-start
  356.3 3.6 %shard_map.502 = (f32[32,64]{1,0:T(8,128)}, f32[3,32]{1,0:T(4,128)}, f32[32,64]{1,0:T(8,128)}, f32[3,32]{1,0:T(4,128)}, f32[1,256]{1,0:T(1,128)}, /*index=5*/f32...) custom-call(bf16[6144,128]{1,0:T(8,128)(2,1)} %get-tuple-element.59., ...), custom_call_target="tpu_custom_call" | custom-call | tf_op jit(solution)/shard_map/pallas_call | solution.py:1694
  360.0 0.0 copy-done.3
  360.0 0.7 copy.62
  360.7 0.0 copy-done.1
  360.7 0.8 copy.63
  361.5 0.0 copy-done.2
  361.5 0.7 copy.64
  362.2 0.0 copy-done
  362.2 1.0 copy.65
Async XLA Ops:
  356.3 3.7 %copy-start.3 = (bf16[4,64,256]{2,1,0:T(8,128)(2,1)S(1)}, bf16[4,64,256]{2,1,0:T(8,128)(2,1)}, u32[]{:S(2)}) copy-start(bf16[4,64,256]{2,1,0:T(8,128)(2,1)} %get-tuple-element.114) | copy-start | bytes 393220
  356.3 4.3 %copy-start.1 = (bf16[32,64,128]{2,1,0:T(8,128)(2,1)S(1)}, bf16[32,64,128]{2,1,0:T(8,128)(2,1)}, u32[]{:S(2)}) copy-start(bf16[32,64,128]{2,1,0:T(8,128)(2,1)} %get-tuple-element.115) | copy-start | bytes 1572868
  356.3 5.1 %copy-start.2 = (f32[4,64,256]{2,1,0:T(8,128)S(1)}, f32[4,64,256]{2,1,0:T(8,128)}, u32[]{:S(2)}) copy-start(f32[4,64,256]{2,1,0:T(8,128)} %get-tuple-element.118) | copy-start | bytes 786436
  356.3 5.8 %copy-start = (f32[32,64,128]{2,1,0:T(8,128)S(1)}, f32[32,64,128]{2,1,0:T(8,128)}, u32[]{:S(2)}) copy-start(f32[32,64,128]{2,1,0:T(8,128)} %get-tuple-element.119) | copy-start | bytes 3145732

commit v2 on v1

--- a/solution.py
+++ b/solution.py
@@ -568,55 +568,72 @@
         copy(t).wait()
 
 
-def swap_all(R, D, src, dst, sems):
+def start_all(D, src, dst, first, size):
     n = D.ns * D.nr
     me = D.s * D.nr + D.r
+    rows = pl.ds(first, size)
     copy = swap(
         D,
-        lambda i: src.at[i],
-        lambda i: dst.at[i],
-        sems,
+        lambda i: src.at[i, rows],
+        lambda i: dst.at[i, rows],
+        D.take(),
         n,
         all_peers,
         lambda ps, pr: ps * D.nr + pr,
         me,
     )
-    dst[me] = src[me]
-    swap_wait(copy, n)
-
-
-def p_pack(R, D):
-    for q in range(4):
-        rows = R.x[q].astype(F32)
-        adjoint = R.adj_a[q].astype(F32)
+    dst[me, rows, :] = src[me, rows, :]
+    return lambda: swap_wait(copy, n)
+
+
+def start_seq(D, src_at, dst_at):
+    copy = swap(D, src_at, dst_at, D.take(), D.ns, seq_peers, lambda ps, pr: ps, D.s)
+    return lambda: swap_wait(copy, D.ns)
+
+
+def start_res(D, src_at, dst_at):
+    copy = swap(D, src_at, dst_at, D.take(), D.nr, res_peers, lambda ps, pr: pr, D.r)
+    return lambda: swap_wait(copy, D.nr)
+
+
+def pack_columns(value, send):
+    for q in range(2):
+        first = value[2 * q].astype(F32)
+        second = value[2 * q + 1].astype(F32)
         for d in range(8):
-            both = jnp.concatenate([rows[8 * d : 8 * d + 8], adjoint[8 * d : 8 * d + 8]], 0)
-            R.xsend[d, q] = both.astype(BF16)
-
-
-def p_spread(R, D, sems):
-    copy = swap(
-        D,
-        lambda i: R.xsend.at[i],
-        lambda i: R.xrecv.at[i],
-        sems,
-        D.ns,
-        seq_peers,
-        lambda ps, pr: ps,
-        D.s,
-    )
-    R.xrecv[D.s] = R.xsend[D.s]
-    swap_wait(copy, D.ns)
+            at = slice(8 * d, 8 * d + 8)
+            send[d, q] = jnp.concatenate([first[at], second[at]], 0).astype(BF16)
+
+
+def start_columns(D, send, recv):
+    recv[D.s] = send[D.s]
+    return start_seq(D, lambda i: send.at[i], lambda i: recv.at[i])
+
+
+def unpack_columns(R, recv, target):
     for d in range(8):
-        for q in range(4):
-            both = R.xrecv[d, q].astype(F32)
-            rows = pl.ds(4 * d + q, 8, stride=32)
-            for half, stages in ((0, (R.sp0, R.sp2)), (1, (R.sp1, R.sp3))):
-                lanes = slice(LANES * half, LANES * half + LANES)
-                stages[0][rows, :] = both[:8, lanes]
-                stages[1][rows, :] = both[8:, lanes]
-    R.xc[...] = jnp.concatenate([R.sp0[...], R.sp1[...]], 1)
-    R.ac[...] = jnp.concatenate([R.sp2[...], R.sp3[...]], 1)
+        for q in range(2):
+            both = recv[d, q].astype(F32)
+            for k in range(2):
+                rows = pl.ds(4 * d + 2 * q + k, 8, stride=32)
+                R.sp0[rows, :] = both[8 * k : 8 * k + 8, :LANES]
+                R.sp1[rows, :] = both[8 * k : 8 * k + 8, LANES:]
+    target[...] = jnp.concatenate([R.sp0[...], R.sp1[...]], 1)
+
+
+def p_spread(R, D):
+    pack_columns(R.x, R.xsend)
+    D.ready()
+    wait = start_columns(D, R.xsend, R.xrecv)
+    pack_columns(R.adj_a, R.asend)
+    R.wait_adjoint = start_columns(D, R.asend, R.arecv)
+    R.w1t[...] = R.w_ti[...].astype(F32).T.astype(BF16)
+    R.w2t[...] = R.w_ii[...].astype(F32).T.astype(BF16)
+    R.wo1t[...] = R.w_to[...].astype(F32).T.astype(BF16)
+    R.wo2t[...] = R.w_io[...].astype(F32).T.astype(BF16)
+    stage_outer_weight(R)
+    wait()
+    unpack_columns(R, R.xrecv, R.xc)
 
 
 def flag_column(flags):
@@ -643,7 +660,7 @@
     R.gl[...] = projected[:, 768:]
     R.att[...] = jnp.zeros((256, 256), F32)
 
-    @pl.loop(0, 8)
+    @pl.loop(0, 8, unroll=4)
     def _(head):
         probs = head_probs(R.qkv[:, 256:512], R.qkv[:, :256], flag_rows, head).astype(BF16)
         lanes = iota((1, 256), 1) // 32
@@ -663,7 +680,8 @@
     R.rsend[...] = dot_nn(hot_bf16(iota((8, 256), 0) == iota((8, 256), 1) // 32), rows)
 
 
-def p_outer_exchange(R, D, sems):
+def p_outer_exchange(R, D):
+    sems = D.take()
     owner = 2 * D.r + D.s // 4
     slot = D.s % 4
 
@@ -725,11 +743,11 @@
 
 
 def stage_outer_weight(R):
-    R.st0[0:1024, :] = R.w_oo[...].astype(F32)
+    R.wst[...] = R.w_oo[...].astype(F32)
 
 
 def outer_weight(R, d):
-    return R.st0[pl.ds(d, 32, stride=32), :].astype(BF16)
+    return R.wst[pl.ds(d, 32, stride=32), :].astype(BF16)
 
 
 def count_of(R):
@@ -737,28 +755,30 @@
 
 
 def p_outer(R, D):
-    stage_outer_weight(R)
     for q in range(4):
         wide = jnp.concatenate([R.lall[q].astype(F32), jnp.zeros((96, 256), F32)], 0)
         R.l2[256 * q : 256 * q + 256, :] = wide.T[:, :32].astype(BF16)
-
-    @pl.loop(0, 32)
-    def _(d):
-        part = dot_nn(R.l2[...], outer_weight(R, d)).astype(BF16)
-        at = pl.ds(pl.multiple_of(32 * d, 32), 32)
-        for i in range(32):
-            R.zb[i, at, :] = part[32 * i : 32 * i + 32]
+        R.lt[:, 256 * q : 256 * q + 256] = R.lall[q]
+
+    @pl.loop(0, 8)
+    def _(e):
+        weights = jnp.concatenate([outer_weight(R, 4 * e + u) for u in range(4)], 1)
+        part = dot_nn(R.l2[...], weights).astype(BF16)
+        for u in range(4):
+            at = pl.ds(pl.multiple_of(32 * (4 * e + u), 32), 32)
+            for i in range(32):
+                R.zb[i, at, :] = part[32 * i : 32 * i + 32, LANES * u : LANES * u + LANES]
 
     inverse = 1.0 / count_of(R)
-
-    @pl.loop(0, 16)
+    right = R.rall[...].astype(BF16)
+
+    @pl.loop(0, 16, unroll=4)
     def _(m):
-        right = R.rall[...].astype(BF16)
-        halves = []
-        for h in range(2):
-            i = 16 * h + m
-            halves.append(dot_nn(right, R.zb[i]) * inverse + R.pe[i].astype(F32))
-        R.pair1[:, pl.ds(pl.multiple_of(m * LANES, LANES), LANES)] = jnp.concatenate(halves, 0).T
+        both = dot_nn(right, jnp.concatenate([R.zb[m], R.zb[16 + m]], 1)) * inverse
+        rows = [
+            both[:, LANES * h : LANES * h + LANES] + R.pe[16 * h + m].astype(F32) for h in range(2)
+        ]
+        R.pair1[:, pl.ds(pl.multiple_of(m * LANES, LANES), LANES)] = jnp.concatenate(rows, 0).T
 
 
 def entry_chunk(R, pair, gain, w_t, nb, j):
@@ -771,41 +791,41 @@
 
 
 def pack_both(R, send):
-    @pl.loop(0, 32)
+    @pl.loop(0, 32, unroll=4)
     def _(d):
         at = pl.ds(pl.multiple_of(64 * d, 64), 64)
-        send[d, 0:64, :] = R.st0[at, :].astype(BF16)
-        send[d, 64:128, :] = R.st1[at, :].astype(BF16)
+        first = R.st0[at, :].astype(BF16)
+        second = R.st1[at, :].astype(BF16)
+        for c in range(4):
+            send[d, 32 * c : 32 * c + 16, :] = first[16 * c : 16 * c + 16]
+            send[d, 32 * c + 16 : 32 * c + 32, :] = second[16 * c : 16 * c + 16]
 
 
 def p_entry1(R, D):
-    R.w1t[...] = R.w_ti[...].astype(F32).T.astype(BF16)
     gain = column(R.g3[...])
 
-    @pl.loop(0, 8)
+    @pl.loop(0, 8, unroll=4)
     def _(j):
         entry_chunk(R, R.pair1[:, chunk_at(j)], gain, R.w1t, R.nb3, j)
 
     pack_both(R, R.lrs)
 
 
-def gather_mats(recv, mats, first, rows, at):
-    @pl.loop(0, 8)
+def gather_mat(recv, off, mats, at):
+    @pl.loop(0, 8, unroll=4)
     def _(s):
         top = pl.ds(pl.multiple_of(32 * s, 32), 16)
         low = pl.ds(pl.multiple_of(32 * s + 16, 16), 16)
-        for c in range(4):
-            off = first + 16 * c
-            for p in range(2):
-                a = recv[4 * s + 2 * p, off : off + 16, :]
-                b = recv[4 * s + 2 * p + 1, off : off + 16, :]
-                lanes = slice(LANES * p, LANES * p + LANES)
-                mats[at + c, top, lanes] = jnp.concatenate([a[:, :64], b[:, :64]], 1)
-                mats[at + c, low, lanes] = jnp.concatenate([a[:, 64:], b[:, 64:]], 1)
+        for p in range(2):
+            a = recv[4 * s + 2 * p, off : off + 16, :]
+            b = recv[4 * s + 2 * p + 1, off : off + 16, :]
+            lanes = slice(LANES * p, LANES * p + LANES)
+            mats[at, top, lanes] = jnp.concatenate([a[:, :64], b[:, :64]], 1)
+            mats[at, low, lanes] = jnp.concatenate([a[:, 64:], b[:, 64:]], 1)
 
 
 def scatter_mat(mat, send, off):
-    @pl.loop(0, 8)
+    @pl.loop(0, 8, unroll=4)
     def _(s):
         for p in range(2):
             lanes = slice(LANES * p, LANES * p + LANES)
@@ -815,50 +835,69 @@
             send[4 * s + 2 * p + 1, off : off + 16, :] = jnp.concatenate([a[:, 64:], b[:, 64:]], 1)
 
 
-def tri_forward(R, mats, send, product):
-    for c in range(4):
-        R.tm[...] = product(mats[c], mats[4 + c]).astype(BF16)
-        scatter_mat(R.tm, send, 16 * c)
-
-
-def tri_backward(R, recv, mats, send, products):
-    gather_mats(recv, R.dm, 0, 64, 0)
-    for c in range(4):
-        for k in range(2):
-            R.tm[...] = products[k](mats[c], mats[4 + c], R.dm[c]).astype(BF16)
-            scatter_mat(R.tm, send, 64 * k + 16 * c)
-
-
-def p_tri1(R, D, sems):
-    swap_all(R, D, R.lrs, R.lr1r, sems[0:2])
-    gather_mats(R.lr1r, R.mats1, 0, 64, 0)
-    gather_mats(R.lr1r, R.mats1, 64, 64, 4)
-    tri_forward(R, R.mats1, R.ts, dot_nt)
-    swap_all(R, D, R.ts, R.t1r, sems[2:4])
+def tri_forward(R, D, recv, mats, back, product, meanwhile):
+    size = 4 // PARTS
+    waits = [start_all(D, R.lrs, recv, 32 * size * h, 32 * size) for h in range(PARTS)]
+    meanwhile(R, D)
+    later = []
+    for h in range(PARTS):
+        waits[h]()
+        for c in range(size * h, size * h + size):
+            gather_mat(recv, 32 * c, mats, c)
+            gather_mat(recv, 32 * c + 16, mats, 4 + c)
+            R.tm[c] = product(mats[c], mats[4 + c]).astype(BF16)
+            scatter_mat(R.tm.at[c], R.ts, 16 * c)
+        later.append(start_all(D, R.ts, back, 16 * size * h, 16 * size))
+    for wait in later:
+        wait()
+
+
+def tri_backward(R, D, recv, mats, back, products, meanwhile):
+    size = 4 // PARTS
+    waits = [start_all(D, R.ts, recv, 16 * size * h, 16 * size) for h in range(PARTS)]
+    meanwhile(R, D)
+    later = []
+    for h in range(PARTS):
+        waits[h]()
+        for c in range(size * h, size * h + size):
+            gather_mat(recv, 16 * c, R.dm, c)
+            for k in range(2):
+                R.tm[c] = products[k](mats[c], mats[4 + c], R.dm[c]).astype(BF16)
+                scatter_mat(R.tm.at[c], R.lrs, 32 * c + 16 * k)
+        later.append(start_all(D, R.lrs, back, 32 * size * h, 32 * size))
+    for wait in later:
+        wait()
+
+
+def nothing(R, D):
+    pass
+
+
+def p_tri1(R, D):
+    tri_forward(R, D, R.lr1r, R.mats1, R.t1r, dot_nt, p_still)
 
 
 def stage_single(recv, stage):
-    @pl.loop(0, 32)
+    @pl.loop(0, 32, unroll=4)
     def _(d):
         stage[pl.ds(pl.multiple_of(64 * d, 64), 64), :] = recv[d].astype(F32)
 
 
 def stage_both(recv, first, second):
-    @pl.loop(0, 32)
+    @pl.loop(0, 32, unroll=4)
     def _(d):
         at = pl.ds(pl.multiple_of(64 * d, 64), 64)
-        first[at, :] = recv[d, 0:64, :].astype(F32)
-        second[at, :] = recv[d, 64:128, :].astype(F32)
+        both = recv[d].astype(F32)
+        first[at, :] = jnp.concatenate([both[32 * c : 32 * c + 16] for c in range(4)], 0)
+        second[at, :] = jnp.concatenate([both[32 * c + 16 : 32 * c + 32] for c in range(4)], 0)
 
 
 def p_middle(R, D):
     stage_single(R.t1r, R.st2)
-    R.w2t[...] = R.w_ii[...].astype(F32).T.astype(BF16)
-    R.wo1t[...] = R.w_to[...].astype(F32).T.astype(BF16)
     gain4 = column(R.g4[...])
     gain5 = column(R.g5[...])
 
-    @pl.loop(0, 8)
+    @pl.loop(0, 8, unroll=4)
     def _(j):
         hat, _ = norm(lane_group(R.st2, j), 0)
         nb4 = (hat * gain4).astype(BF16)
@@ -872,40 +911,66 @@
     pack_both(R, R.lrs)
 
 
-def p_tri2(R, D, sems):
-    swap_all(R, D, R.lrs, R.lr2r, sems[0:2])
-    gather_mats(R.lr2r, R.mats2, 0, 64, 0)
-    gather_mats(R.lr2r, R.mats2, 64, 64, 4)
-    tri_forward(R, R.mats2, R.ts, dot_tn)
-    swap_all(R, D, R.ts, R.t2r, sems[2:4])
-
-
-def p_turn(R, D):
-    stage_single(R.t2r, R.st2)
-    R.wo2t[...] = R.w_io[...].astype(F32).T.astype(BF16)
-    gain6 = column(R.g6[...])
+def p_tri2(R, D):
+    tri_forward(R, D, R.lr2r, R.mats2, R.t2r, dot_tn, nothing)
+
+
+def chunk_rows(D, j):
+    lane = iota((1, CHUNK), 1)
+    local = 16 * ((lane % LANES) // 64) + 2 * j + lane // LANES
+    return local, hot_bf16(iota((256, CHUNK), 0) == 32 * D.s + local)
+
+
+def near_rows(D):
+    return hot_bf16(iota((256, CHUNK), 0) == 64 * D.r + iota((256, CHUNK), 1) % 64)
+
+
+def p_still(R, D):
     dist = column(R.w_ds[...])
-    turn_weight = column(R.w_sl[...])
     inv_k = 1.0 / R.ca.shape[1]
     R.at8[...] = jnp.zeros((8, 256), F32)
     R.at8[0:3, :] = R.at[...]
     R.la8[...] = jnp.zeros((8, 32), F32)
     R.la8[0:3, :] = R.adj_l[...]
-    node = dot_tn(R.vet[...].astype(BF16), R.w_nd[...])
-    R.nodet[...] = node.T
+    R.nodet[...] = dot_tn(R.vet[...].astype(BF16), R.w_nd[...]).T
     R.dmean[...] = dot_nt(R.w_up[...], R.adj_v[...].astype(BF16))
-    near = hot_bf16(iota((256, CHUNK), 0) == 64 * D.r + iota((256, CHUNK), 1) % 64)
+    near = near_rows(D)
     R.nbase[...] = pick_nn(R.nodet[64:, :], near, 2)
     R.cbase[...] = pick_nn(R.at8[...], near, 3)
-    for acc in (R.s_mean, R.s_own, R.s_other):
-        acc[...] = jnp.zeros(acc.shape, F32)
-    R.s_xyz[...] = jnp.zeros((16, 256), F32)
+    R.nb_f[...] = R.ca[...].astype(F32)
+
+    @pl.loop(0, 8, unroll=2)
+    def _(j):
+        here = chunk_at(j)
+        local, row = chunk_rows(D, j)
+        mine = hot_bf16(iota((32, CHUNK), 0) == local)
+        named = dot_tn(R.nb_f[...].astype(BF16), mine)
+        target = (64 * D.r + iota((1, CHUNK), 1) % 64).astype(F32)
+        mask = jnp.max(jnp.where(named == target, 1.0, 0.0), 0, keepdims=True) * inv_k
+        diff = pick_nn(R.at8[...], row, 3) - R.cbase[...]
+        square = 1.0 + jnp.sum(diff * diff, 0, keepdims=True)
+        radial = jnp.log(square)
+        R.geo[0:8, here] = diff
+        R.geo[8:16, here] = pick_nn(R.la8[...], mine, 3)
+        R.geo[16:17, here] = radial
+        R.geo[17:18, here] = mask
+        R.geo[18:19, here] = 2.0 / square
+        R.pre[0:64, here] = pick_nn(R.nodet[0:64, :], row, 2) + R.nbase[...] + radial * dist
+        R.pre[64:128, here] = pick_nn(R.dmean[...], mine, 2) * mask
+        for q in range(2):
+            m = 2 * j + q
+            both = jnp.concatenate([R.adj_c[m], R.adj_c[16 + m]], 0).astype(F32)
+            R.dpair[:, pl.ds(pl.multiple_of(m * LANES, LANES), LANES)] = both.T
+
+
+def p_turn(R, D):
+    stage_single(R.t2r, R.st2)
+    gain6 = column(R.g6[...])
+    dist = column(R.w_ds[...])
+    turn_weight = column(R.w_sl[...])
     R.a_g6[...] = jnp.zeros((128, CHUNK), F32)
-    R.a_dist[...] = jnp.zeros((64, CHUNK), F32)
-    R.a_coord[...] = jnp.zeros((64, CHUNK), F32)
-    R.nb_f[...] = R.ca[...].astype(F32)
-
-    @pl.loop(0, 8)
+
+    @pl.loop(0, 8, unroll=4)
     def _(j):
         here = chunk_at(j)
         hat, rstd = norm(lane_group(R.st2, j), 0)
@@ -916,18 +981,7 @@
         pair3 = R.pair2[:, here] + gate2 * update2
         po_b = pair3.astype(BF16)
         R.po[:, here] = po_b
-        lane = iota((1, CHUNK), 1)
-        local_row = 16 * ((lane % LANES) // 64) + 2 * j + lane // LANES
-        mine = hot_bf16(iota((32, CHUNK), 0) == local_row)
-        row = hot_bf16(iota((256, CHUNK), 0) == 32 * D.s + local_row)
-        named = dot_tn(R.nb_f[...].astype(BF16), mine)
-        target = (64 * D.r + lane % 64).astype(F32)
-        mask = jnp.max(jnp.where(named == target, 1.0, 0.0), 0, keepdims=True) * inv_k
-        diff = pick_nn(R.at8[...], row, 3) - R.cbase[...]
-        square = 1.0 + jnp.sum(diff * diff, 0, keepdims=True)
-        radial = jnp.log(square)
-        edge = dot_nn(R.w_edt[...], po_b)
-        pre = pick_nn(R.nodet[0:64, :], row, 2) + R.nbase[...] + edge + radial * dist
+        pre = R.pre[0:64, here] + dot_nn(R.w_edt[...], po_b)
         sig_pre = sigmoid(pre)
         hidden = (pre * sig_pre).astype(BF16)
         R.hid[:, here] = hidden
@@ -935,33 +989,23 @@
         sig_msg = sigmoid(msg)
         message = msg * sig_msg
         turn = jnp.tanh(jnp.sum(message * turn_weight, 0, keepdims=True))
-        R.s_mean[...] += pick_nt(message * mask, row, 2)
-        locadj = pick_nn(R.la8[...], mine, 3)
+        diff = R.geo[0:8, here]
+        locadj = R.geo[8:16, here]
+        mask = R.geo[17:18, here]
         d_turn = jnp.sum(locadj * diff, 0, keepdims=True) * mask * (1.0 - turn * turn)
-        d_message = pick_nn(R.dmean[...], mine, 2) * mask + turn_weight * d_turn
-        R.a_coord[...] += message * d_turn
+        d_message = R.pre[64:128, here] + turn_weight * d_turn
         d_msg = (d_message * sig_msg * (1.0 + msg * (1.0 - sig_msg))).astype(BF16)
         R.dmsg[:, here] = d_msg
         d_pre = dot_nn(R.w_ms[...], d_msg) * sig_pre * (1.0 + pre * (1.0 - sig_pre))
-        R.a_dist[...] += d_pre * radial
         d_edge = d_pre.astype(BF16)
         R.dedge[:, here] = d_edge
-        R.s_own[...] += pick_nt(d_pre, row, 2)
-        R.s_other[...] += pick_nt(d_pre, near, 2)
         d_radial = jnp.sum(d_pre * dist, 0, keepdims=True)
-        d_diff = (2.0 * d_radial / square) * diff + locadj * (turn * mask)
-        R.s_xyz[0:8, :] += pick_nt(diff * (turn * mask), row, 2)
-        R.s_xyz[8:16, :] += pick_nt(d_diff, row, 2) - pick_nt(d_diff, near, 2)
-        d_po = dot_tn(R.w_edt[...], d_edge)
-        adjoint = []
-        for q in range(2):
-            m = 2 * j + q
-            both = jnp.concatenate([R.adj_c[m], R.adj_c[16 + m]], 0).astype(F32)
-            adjoint.append(both.T)
-            out = pair3[:, q * LANES : (q + 1) * LANES].T.astype(BF16)
-            R.pair_out[m] = out[:64]
-            R.pair_out[16 + m] = out[64:]
-        d_pair3 = jnp.concatenate(adjoint, 1) + d_po
+        R.pre[0:64, here] = message
+        R.pre[64:128, here] = d_pre
+        R.geo[19:20, here] = turn * mask
+        R.geo[20:21, here] = d_turn
+        R.geo[24:32, here] = (d_radial * R.geo[18:19, here]) * diff + locadj * (turn * mask)
+        d_pair3 = R.dpair[:, here] + dot_tn(R.w_edt[...], d_edge)
         R.dpair[:, here] = d_pair3
         d_up = (d_pair3 * gate2).astype(BF16)
         R.dup2[:, here] = d_up
@@ -970,31 +1014,56 @@
         R.a_g6[...] += d_nb * hat
         lane_ungroup(R.st0, j, norm_back(d_nb, gain6, hat, rstd, 0))
 
+    pack_single(R, R.ts)
+
+
+def p_turn_grads(R, D):
     R.g_io[...] = dot_nt(R.nb6[...], R.dup2[...])
     R.g_ed[...] = dot_nt(R.dedge[...], R.po[...])
     R.g_ms[...] = dot_nt(R.hid[...], R.dmsg[...])
     R.gg6[...] = jnp.sum(R.a_g6[...], 1, keepdims=True)
-    R.g_ds[...] = jnp.sum(R.a_dist[...], 1, keepdims=True)
-    R.g_sl[...] = jnp.sum(R.a_coord[...], 1, keepdims=True)
-    pack_single(R, R.ts)
+    R.g_ds[...] = jnp.sum(R.pre[64:128, :] * R.geo[16:17, :], 1, keepdims=True)
+    R.g_sl[...] = jnp.sum(R.pre[0:64, :] * R.geo[20:21, :], 1, keepdims=True)
+    for acc in (R.s_mean, R.s_own, R.s_other):
+        acc[...] = jnp.zeros(acc.shape, F32)
+    R.s_xyz[...] = jnp.zeros((16, 256), F32)
+
+    @pl.loop(0, 8, unroll=2)
+    def _(j):
+        here = chunk_at(j)
+        _, row = chunk_rows(D, j)
+        near = near_rows(D)
+        d_pre = R.pre[64:128, here]
+        d_diff = R.geo[24:32, here]
+        R.s_mean[...] += pick_nt(R.pre[0:64, here] * R.geo[17:18, here], row, 2)
+        R.s_own[...] += pick_nt(d_pre, row, 2)
+        R.s_other[...] += pick_nt(d_pre, near, 2)
+        R.s_xyz[0:8, :] += pick_nt(R.geo[0:8, here] * R.geo[19:20, here], row, 2)
+        R.s_xyz[8:16, :] += pick_nt(d_diff, row, 2) - pick_nt(d_diff, near, 2)
+        for q in range(2):
+            m = 2 * j + q
+            at = pl.ds(pl.multiple_of(m * LANES, LANES), LANES)
+            out = R.po[:, at].astype(F32).T.astype(BF16)
+            R.pair_out[m] = out[:64]
+            R.pair_out[16 + m] = out[64:]
 
 
 def pack_single(R, send):
-    @pl.loop(0, 32)
+    @pl.loop(0, 32, unroll=4)
     def _(d):
         send[d] = R.st0[pl.ds(pl.multiple_of(64 * d, 64), 64), :].astype(BF16)
 
 
-def p_back2(R, D, sems):
-    swap_all(R, D, R.ts, R.dt2r, sems[0:2])
+def p_back2(R, D):
     tri_backward(
         R,
+        D,
         R.dt2r,
         R.mats2,
-        R.lrs,
+        R.dlr2r,
         (lambda a, b, d: dot_nt(b, d), lambda a, b, d: dot_nn(a, d)),
-    )
-    swap_all(R, D, R.lrs, R.dlr2r, sems[2:4])
+        p_turn_grads,
+    )
 
 
 def gates_back(R, d_tri, w_t, nb_here, j):
@@ -1018,7 +1087,7 @@
     R.a_g4[...] = jnp.zeros((128, CHUNK), F32)
     R.a_g5[...] = jnp.zeros((128, CHUNK), F32)
 
-    @pl.loop(0, 8)
+    @pl.loop(0, 8, unroll=4)
     def _(j):
         here = chunk_at(j)
         gates_back(R, R.dtri2, R.w2t, R.nb5[:, here], j)
@@ -1037,26 +1106,28 @@
         R.a_g4[...] += d_nb4 * hat4
         lane_ungroup(R.st3, j, norm_back(d_nb4, gain4, hat4, rstd4, 0))
 
+    @pl.loop(0, 32, unroll=4)
+    def _(d):
+        R.ts[d] = R.st3[pl.ds(pl.multiple_of(64 * d, 64), 64), :].astype(BF16)
+
+
+def p_between_grads(R, D):
     R.g_ii[...] = dot_nt(R.nb5[...], R.dtri2[...])
     R.g_to[...] = dot_nt(R.nb4[...], R.dup1[...])
     R.gg5[...] = jnp.sum(R.a_g5[...], 1, keepdims=True)
     R.gg4[...] = jnp.sum(R.a_g4[...], 1, keepdims=True)
 
-    @pl.loop(0, 32)
-    def _(d):
-        R.ts[d] = R.st3[pl.ds(pl.multiple_of(64 * d, 64), 64), :].astype(BF16)
-
-
-def p_back1(R, D, sems):
-    swap_all(R, D, R.ts, R.dt1r, sems[0:2])
+
+def p_back1(R, D):
     tri_backward(
         R,
+        D,
         R.dt1r,
         R.mats1,
-        R.lrs,
+        R.dlr1r,
         (lambda a, b, d: dot_nn(d, b), lambda a, b, d: dot_tn(d, a)),
-    )
-    swap_all(R, D, R.lrs, R.dlr1r, sems[2:4])
+        p_between_grads,
+    )
 
 
 def p_pair_end(R, D):
@@ -1065,7 +1136,7 @@
     R.a_g3[...] = jnp.zeros((128, CHUNK), F32)
     inverse = 1.0 / count_of(R)
 
-    @pl.loop(0, 8)
+    @pl.loop(0, 8, unroll=4)
     def _(j):
         here = chunk_at(j)
         gates_back(R, R.dtri1, R.w1t, R.nb3[:, here], j)
@@ -1087,37 +1158,40 @@
 
 
 def p_outer_back(R, D):
-    stage_outer_weight(R)
     R.rt[...] = R.rall[...].T.astype(BF16)
     R.dright[...] = jnp.zeros((64, 1024), F32)
     R.dleft[...] = jnp.zeros((32, 1024), F32)
-    for q in range(4):
-
-        @pl.loop(0, 8)
+
+    @pl.loop(0, 4)
+    def _(k):
+        grad = jnp.concatenate([R.dopm[8 * k + u] for u in range(8)], 1)
+        R.dright[...] += dot_nt(grad, jnp.concatenate([R.zb[8 * k + u] for u in range(8)], 1))
+
+    @pl.loop(0, 4)
+    def _(g):
+        right = R.rt[pl.ds(pl.multiple_of(256 * g, 256), 256), :]
+
+        @pl.loop(0, 16, unroll=16)
         def _(k):
-            i = 8 * q + k
-            grad = R.dopm[i]
-            R.yb[k] = dot_nn(R.rt[...], grad).astype(BF16)
-            R.dright[...] += dot_nt(grad, R.zb[i])
-
-        @pl.loop(0, 32)
-        def _(d):
-            at = pl.ds(pl.multiple_of(32 * d, 32), 32)
-            rows = R.yb[:, at, :].reshape(256, LANES)
-            lanes = slice(256 * q, 256 * q + 256)
-            R.dleft[:, lanes] += dot_nt(outer_weight(R, d), rows)
-            total = dot_nn(R.lall[q], rows)
-            here = pl.ds(d, 32, stride=32)
-            if q:
-                total += R.st1[here, :]
-            R.st1[here, :] = total
+            grad = jnp.concatenate([R.dopm[2 * k], R.dopm[2 * k + 1]], 1)
+            both = dot_nn(right, grad).astype(BF16)
+            R.yg[:, 2 * k] = both[:, :LANES].reshape(8, 32, LANES)
+            R.yg[:, 2 * k + 1] = both[:, LANES:].reshape(8, 32, LANES)
+
+        weights = jnp.concatenate([outer_weight(R, 8 * g + u) for u in range(8)], 1)
+        rows = jnp.concatenate([R.yg[u].reshape(1024, LANES) for u in range(8)], 1)
+        R.dleft[...] += dot_nt(weights, rows)
+        total = dot_nn(R.lt[...], rows)
+        for u in range(8):
+            R.st1[pl.ds(8 * g + u, 32, stride=32), :] = total[:, LANES * u : LANES * u + LANES]
 
     R.g_oo[...] = R.st1[0:1024, :]
     for q in range(4):
         R.dls[q] = R.dleft[:, 256 * q : 256 * q + 256].astype(BF16)
 
 
-def p_outer_return(R, D, sems):
+def p_outer_return(R, D):
+    sems = D.take()
     column_res = D.s // 2
     owner = 2 * D.r + D.s // 4
 
@@ -1171,6 +1245,7 @@
 
 
 def p_attention_back(R, D):
+    next(R.sum0)
     flag_rows = flag_column(R.fl[...].astype(F32))
     live = (flag_rows > 0).astype(F32)
     left = R.dlr[0].astype(F32)
@@ -1203,7 +1278,7 @@
     R.dproj[:, 768:] = (d_gated * R.att[...] * gate * (1.0 - gate)).astype(BF16)
     R.dqkv[...] = jnp.zeros((256, 768), F32)
 
-    @pl.loop(0, 8)
+    @pl.loop(0, 8, unroll=4)
     def _(head):
         lanes = iota((1, 256), 1) // 32
         mine = lanes == head
@@ -1226,45 +1301,43 @@
     d_normed = dot_nt(R.dproj[...], R.w_qkvg[...])
     R.gg1[...] = jnp.sum(d_normed * hat, 0, keepdims=True)
     R.dlater[...] += norm_back(d_normed, R.g1[...], hat, rstd, -1)
-
-    R.sp0[...] = R.msan[:, :LANES]
-    R.sp1[...] = R.msan[:, LANES:]
-    R.sp2[...] = R.dlater[:, :LANES]
-    R.sp3[...] = R.dlater[:, LANES:]
+    group_columns(R, R.dlater, R.gsend)
+
+
+def group_columns(R, value, send):
+    R.sp0[...] = value[:, :LANES]
+    R.sp1[...] = value[:, LANES:]
     for d in range(8):
-        for q in range(4):
-            rows = pl.ds(4 * d + q, 8, stride=32)
-            value = jnp.concatenate([R.sp0[rows, :], R.sp1[rows, :]], 1)
-            grad = jnp.concatenate([R.sp2[rows, :], R.sp3[rows, :]], 1)
-            R.osend[d, q] = jnp.concatenate([value, grad], 0).astype(BF16)
-
-
-def p_collect(R, D, sems):
-    copy = swap(
-        D,
-        lambda i: R.osend.at[i],
-        lambda i: R.orecv.at[i],
-        sems,
-        D.ns,
-        seq_peers,
-        lambda ps, pr: ps,
-        D.s,
-    )
-    R.orecv[D.s] = R.osend[D.s]
-    swap_wait(copy, D.ns)
-    for q in range(4):
-        blocks = [R.orecv[d, q].astype(F32) for d in range(8)]
-        R.msa_out[q] = jnp.concatenate([b[:8] for b in blocks], 0).astype(BF16)
-        R.msa_grad[q] = jnp.concatenate([b[8:] for b in blocks], 0)
-
-
-def payload_layout():
-    layout = []
-    start = 0
-    shapes = dict(
-        g_qkvg=(256, 1024),
-        g_ao=(256, 256),
-        g_oo=(1024, 128),
+        for q in range(2):
+            parts = []
+            for k in range(2):
+                rows = pl.ds(4 * d + 2 * q + k, 8, stride=32)
+                parts.append(jnp.concatenate([R.sp0[rows, :], R.sp1[rows, :]], 1))
+            send[d, q] = jnp.concatenate(parts, 0).astype(BF16)
+
+
+def ungroup_columns(recv, target):
+    for q in range(2):
+        blocks = [recv[d, q].astype(F32) for d in range(8)]
+        for k in range(2):
+            rows = jnp.concatenate([block[8 * k : 8 * k + 8] for block in blocks], 0)
+            target[2 * q + k] = rows.astype(target.dtype)
+
+
+def p_send_value(R, D):
+    group_columns(R, R.msan, R.osend)
+    R.wait_value = start_columns(D, R.osend, R.orecv)
+
+
+def p_take_value(R, D):
+    R.wait_value()
+    ungroup_columns(R.orecv, R.msa_out)
+    R.wait_adjoint()
+    unpack_columns(R, R.arecv, R.ac)
+
+
+SEGMENTS = (
+    dict(
         g_ti=(128, 640),
         g_ii=(128, 640),
         g_to=(128, 128),
@@ -1274,128 +1347,132 @@
         s_other=(64, 256),
         s_vadj=(64, 256),
         s_xyz=(16, 256),
-        g_oi=(64, 256),
         g_ed=(64, 128),
         g_ms=(64, 64),
-        small=(128, 128),
-    )
-    for name, (rows, cols) in shapes.items():
+        small0=(16, 128),
+    ),
+    dict(g_oo=(1024, 128)),
+    dict(g_qkvg=(256, 1024), g_ao=(256, 256), g_oi=(64, 256), small1=(16, 128)),
+)
+
+
+def segment_layout(index):
+    layout = []
+    start = 0
+    for name, (rows, cols) in SEGMENTS[index].items():
         for lane in range(0, cols, LANES):
             layout.append((name, start, rows, lane, min(LANES, cols - lane)))
             start += rows
     return layout, -(-start // 512) * 512
 
 
-def p_sum_pack(R, D):
-    rows = iota((32, 256), 0)
-    place = hot_bf16(iota((32, 256), 1) == 32 * D.s + rows)
+def pack_segment(R, index):
+    layout, total = segment_layout(index)
+    pay = R.pay[index]
+    for name, start, count, lane, width in layout:
+        value = getattr(R, name)[:, lane : lane + width]
+        pay[start : start + count, 0:width] = value.astype(BF16)
+    end = layout[-1][1] + layout[-1][2]
+    if end < total:
+        pay[end:total, :] = jnp.zeros((total - end, LANES), BF16)
+
+
+def rows_of(index, size):
+    return pl.ds(pl.multiple_of(index * size, size), size)
+
+
+def sum_segment(R, D, index):
+    pay, full = R.pay[index], R.full[index]
+    first, second, third, fourth = (table[index] for table in R.parts)
+    eighth = pay.shape[0] // 8
+    part = eighth // 4
+    pack_segment(R, index)
+    first[D.s] = pay[rows_of(D.s, eighth), :]
+    wait = start_seq(D, lambda i: pay.at[rows_of(i, eighth)], lambda i: first.at[i])
+    yield
+    wait()
+    total = first[0].astype(F32)
+    for k in range(1, 8):
+        total += first[k].astype(F32)
+    second[...] = total.astype(BF16)
+    third[D.r] = second[rows_of(D.r, part), :]
+    wait = start_res(D, lambda i: second.at[rows_of(i, part)], lambda i: third.at[i])
+    yield
+    wait()
+    total = third[0].astype(F32)
+    for k in range(1, 4):
+        total += third[k].astype(F32)
+    fourth[...] = total.astype(BF16)
+    mine = pl.ds(pl.multiple_of(D.s * eighth + D.r * part, part), part)
+    full[mine, :] = fourth[...]
+    wait = start_res(D, lambda i: fourth, lambda i: full.at[mine])
+    yield
+    wait()
+    wait = start_seq(
+        D, lambda i: full.at[rows_of(D.s, eighth)], lambda i: full.at[rows_of(i, eighth)]
+    )
+    yield
+    wait()
+
+
+def p_sum0(R, D):
+    place = hot_bf16(iota((32, 256), 1) == 32 * D.s + iota((32, 256), 0))
     first = jnp.where(D.r == 0, 1.0, 0.0)
     R.s_vadj[...] = dot_tn(R.adj_v[...].astype(BF16), place) * first
     R.small[...] = jnp.zeros((128, LANES), F32)
-    for k, name in enumerate(("gg3", "gg4", "gg5", "gg6", "g_ds", "g_sl")):
-        value = getattr(R, name)
+    for k, value in enumerate((R.gg3, R.gg4, R.gg5, R.gg6, R.g_ds, R.g_sl)):
         R.small[0 : value.shape[0], k : k + 1] = value[...]
-    for k, name in enumerate(("gg1", "gg2")):
-        value = getattr(R, name)
+    R.small0[...] = R.small[...].T[:16]
+    R.sum0 = sum_segment(R, D, 0)
+    next(R.sum0)
+
+
+def p_sum1(R, D):
+    R.sum1 = sum_segment(R, D, 1)
+    next(R.sum1)
+
+
+def p_sum2(R, D):
+    R.small1[...] = jnp.zeros((16, LANES), F32)
+    for k, value in enumerate((R.gg1, R.gg2)):
         for half in range(2):
-            R.small[:, 8 + 2 * k + half : 9 + 2 * k + half] = column(
-                value[:, LANES * half : LANES * half + LANES]
-            )
-    layout, total = payload_layout()
-    for name, start, count, lane, width in layout:
-        R.pay[start : start + count, 0:width] = getattr(R, name)[:, lane : lane + width].astype(
-            BF16
-        )
-    last = layout[-1]
-    end = last[1] + last[2]
-    if end < total:
-        R.pay[end:total, :] = jnp.zeros((total - end, LANES), BF16)
-
-
-def p_sum(R, D, sems):
-    eighth = R.pay.shape[0] // 8
-    part = eighth // 4
-
-    def rows(ref, index, size):
-        return ref.at[pl.ds(pl.multiple_of(index * size, size), size)]
-
-    copy = swap(
-        D,
-        lambda i: rows(R.pay, i, eighth),
-        lambda i: R.sum_a.at[i],
-        sems[0:2],
-        D.ns,
-        seq_peers,
-        lambda ps, pr: ps,
-        D.s,
-    )
-    swap_wait(copy, D.ns)
-    R.sum_a[D.s] = R.pay[pl.ds(pl.multiple_of(D.s * eighth, eighth), eighth), :]
-    total = R.sum_a[0].astype(F32)
-    for k in range(1, 8):
-        total += R.sum_a[k].astype(F32)
-    R.sum_b[...] = total.astype(BF16)
-    copy = swap(
-        D,
-        lambda i: rows(R.sum_b, i, part),
-        lambda i: R.sum_c.at[i],
-        sems[2:4],
-        D.nr,
-        res_peers,
-        lambda ps, pr: pr,
-        D.r,
-    )
-    swap_wait(copy, D.nr)
-    R.sum_c[D.r] = R.sum_b[pl.ds(pl.multiple_of(D.r * part, part), part), :]
-    total = R.sum_c[0].astype(F32)
-    for k in range(1, 4):
-        total += R.sum_c[k].astype(F32)
-    R.sum_d[...] = total.astype(BF16)
-    mine = pl.ds(pl.multiple_of(D.s * eighth + D.r * part, part), part)
-    R.full[mine, :] = R.sum_d[...]
-    copy = swap(
-        D,
-        lambda i: R.sum_d,
-        lambda i: R.full.at[mine],
-        sems[4:6],
-        D.nr,
-        res_peers,
-        lambda ps, pr: pr,
-        D.r,
-    )
-    swap_wait(copy, D.nr)
-    copy = swap(
-        D,
-        lambda i: rows(R.full, D.s, eighth),
-        lambda i: rows(R.full, i, eighth),
-        sems[6:8],
-        D.ns,
-        seq_peers,
-        lambda ps, pr: ps,
-        D.s,
-    )
-    swap_wait(copy, D.ns)
+            at = 2 * k + half
+            R.small1[at : at + 1, :] = value[:, LANES * half : LANES * half + LANES]
+    R.sum2 = sum_segment(R, D, 2)
+    next(R.sum2)
+
+
+def p_sums(R, D):
+    wait = start_columns(D, R.gsend, R.grecv)
+    sums = [R.sum0, R.sum1, R.sum2]
+    while sums:
+        sums = [each for each in sums if next(each, D) is not D]
+        if wait:
+            wait()
+            ungroup_columns(R.grecv, R.msa_grad)
+            wait = None
 
 
 def p_finish(R, D):
-    layout, _ = payload_layout()
     held = {}
-    for name, start, count, lane, width in layout:
-        value = R.full[start : start + count, 0:width].astype(F32)
-        if name.startswith("g_"):
-            getattr(R, "o_" + name)[:, lane : lane + width] = value
-        else:
-            held.setdefault(name, []).append(value)
+    for index in range(len(SEGMENTS)):
+        for name, start, count, lane, width in segment_layout(index)[0]:
+            value = R.full[index][start : start + count, 0:width].astype(F32)
+            if name.startswith("g_"):
+                getattr(R, "o_" + name)[:, lane : lane + width] = value
+            else:
+                held.setdefault(name, []).append(value)
     held = {name: jnp.concatenate(parts, 1) for name, parts in held.items()}
-    small = held["small"].T
-    for k, name in enumerate(("gg3", "gg4", "gg5", "gg6")):
-        getattr(R, "o_" + name)[...] = small[k : k + 1, :]
+    small = held["small0"]
+    for k, target in enumerate((R.o_gg3, R.o_gg4, R.o_gg5, R.o_gg6)):
+        target[...] = small[k : k + 1, :]
     R.o_g_ds[...] = small[4:5, :64]
     R.o_g_sl[...] = small[5:6, :64]
-    for k, name in enumerate(("gg1", "gg2")):
+    small = held["small1"]
+    for k, target in enumerate((R.o_gg1, R.o_gg2)):
         for half in range(2):
-            at = 8 + 2 * k + half
-            getattr(R, "o_" + name)[:, LANES * half : LANES * half + LANES] = small[at : at + 1]
+            at = 2 * k + half
+            target[:, LANES * half : LANES * half + LANES] = small[at : at + 1]
     mean_b = held["s_mean"].astype(BF16)
     R.o_g_up[...] = dot_nt(mean_b, held["s_vadj"].astype(BF16))
     d_node = jnp.concatenate([held["s_own"], held["s_other"]], 0).astype(BF16)
@@ -1418,14 +1495,26 @@
 
 
 KEPT = dict(
-    xsend=((8, 4, 16, 256), BF16),
-    xrecv=((8, 4, 16, 256), BF16),
+    xsend=((8, 2, 16, 256), BF16),
+    xrecv=((8, 2, 16, 256), BF16),
+    asend=((8, 2, 16, 256), BF16),
+    arecv=((8, 2, 16, 256), BF16),
+    osend=((8, 2, 16, 256), BF16),
+    orecv=((8, 2, 16, 256), BF16),
+    gsend=((8, 2, 16, 256), BF16),
+    grecv=((8, 2, 16, 256), BF16),
+    wst=((1024, 128), F32),
+    lt=((32, 1024), BF16),
+    yg=((8, 32, 32, 128), BF16),
+    tm=((4, 256, 256), BF16),
+    geo=((32, 2048), F32),
+    pre=((128, 2048), F32),
+    small0=((16, 128), F32),
+    small1=((16, 128), F32),
     xc=((256, 256), F32),
     ac=((256, 256), F32),
     sp0=((256, 128), F32),
     sp1=((256, 128), F32),
-    sp2=((256, 128), F32),
-    sp3=((256, 128), F32),
     qkv=((256, 768), BF16),
     gl=((256, 256), F32),
     att=((256, 256), F32),
@@ -1440,7 +1529,6 @@
     st3=((2048, 128), F32),
     l2=((1024, 32), BF16),
     zb=((32, 1024, 128), BF16),
-    yb=((8, 1024, 128), BF16),
     pair1=((128, 2048), F32),
     pair2=((128, 2048), F32),
     dpair=((128, 2048), F32),
@@ -1463,7 +1551,6 @@
     mats1=((8, 256, 256), BF16),
     mats2=((8, 256, 256), BF16),
     dm=((4, 256, 256), BF16),
-    tm=((256, 256), BF16),
     lrs=((32, 128, 128), BF16),
     lr1r=((32, 128, 128), BF16),
     lr2r=((32, 128, 128), BF16),
@@ -1490,8 +1577,6 @@
     a_g4=((128, 256), F32),
     a_g5=((128, 256), F32),
     a_g6=((128, 256), F32),
-    a_dist=((64, 256), F32),
-    a_coord=((64, 256), F32),
     gg3=((128, 1), F32),
     gg4=((128, 1), F32),
     gg5=((128, 1), F32),
@@ -1522,24 +1607,20 @@
     datt=((256, 256), BF16),
     dproj=((256, 1024), BF16),
     dqkv=((256, 768), F32),
-    osend=((8, 4, 16, 256), BF16),
-    orecv=((8, 4, 16, 256), BF16),
 )
-PAYLOAD = payload_layout()[1]
-KEPT.update(
-    pay=((PAYLOAD, 128), BF16),
-    sum_a=((8, PAYLOAD // 8, 128), BF16),
-    sum_b=((PAYLOAD // 8, 128), BF16),
-    sum_c=((4, PAYLOAD // 32, 128), BF16),
-    sum_d=((PAYLOAD // 32, 128), BF16),
+SIZES = [segment_layout(index)[1] for index in range(len(SEGMENTS))]
+PAYLOADS = [((size, 128), BF16) for size in SIZES]
+PARTIAL = (
+    [((8, size // 8, 128), BF16) for size in SIZES]
+    + [((size // 8, 128), BF16) for size in SIZES]
+    + [((4, size // 32, 128), BF16) for size in SIZES]
+    + [((size // 32, 128), BF16) for size in SIZES]
 )
-LAST_ONLY = ()
 LARGE = ("msa_out", "pair_out", "msa_grad", "pair_grad")
-FINISH = ("full", "vet", "w_up", "w_nd", "adj_v", "at", "adj_l")
+FINISH = ("vet", "w_up", "w_nd", "adj_v", "at", "adj_l")
 FINISH_KEPT = dict(
     rows_f=((256, 128), F32), rows_g=((256, 128), F32), xyz=((128, 256), F32)
 )
-MIDDLE = dict(full=((PAYLOAD, 128), BF16))
 RESULTS = dict(
     msa_out=((4, 64, 256), BF16),
     pair_out=((32, 64, 128), BF16),
@@ -1572,54 +1653,69 @@
 )
 
 STEPS = (
-    (p_pack, 0),
-    (p_spread, 1),
-    (p_attention, 0),
-    (p_outer_exchange, 1),
-    (p_outer, 0),
-    (p_entry1, 0),
-    (p_tri1, 2),
-    (p_middle, 0),
-    (p_tri2, 2),
-    (p_turn, 0),
-    (p_back2, 2),
-    (p_between, 0),
-    (p_back1, 2),
-    (p_pair_end, 0),
-    (p_outer_back, 0),
-    (p_outer_return, 1),
-    (p_attention_back, 0),
-    (p_collect, 1),
-    (p_sum_pack, 0),
-    (p_sum, 4),
+    p_spread,
+    p_attention,
+    p_outer_exchange,
+    p_send_value,
+    p_outer,
+    p_take_value,
+    p_entry1,
+    p_tri1,
+    p_middle,
+    p_tri2,
+    p_turn,
+    p_back2,
+    p_between,
+    p_back1,
+    p_pair_end,
+    p_sum0,
+    p_outer_back,
+    p_sum1,
+    p_outer_return,
+    p_attention_back,
+    p_sum2,
+    p_sums,
 )
-
-
-def first_kernel(n_seq, n_res, names, exchanges, *refs):
-    R = SimpleNamespace(**dict(zip(names, refs)))
-    sems = refs[len(names) :]
-    D = SimpleNamespace(s=lax.axis_index("seq"), r=lax.axis_index("res"), ns=n_seq, nr=n_res)
+EXCHANGES = 35
+PARTS = 2
+
+
+class Device:
+    def __init__(self, n_seq, n_res, sems):
+        self.s, self.r = lax.axis_index("seq"), lax.axis_index("res")
+        self.ns, self.nr = n_seq, n_res
+        self.sems = list(sems)
+
+    def take(self):
+        return self.sems.pop(0), self.sems.pop(0)
+
+    def ready(self):
+        pl.semaphore_wait(pltpu.get_barrier_semaphore(), self.ns * self.nr - 1)
+
+
+def first_kernel(n_seq, n_res, names, *refs):
+    refs = list(refs)
+    R = SimpleNamespace(**{name: refs.pop(0) for name in names})
+    R.full = [refs.pop(0) for _ in SIZES]
+    R.__dict__.update({name: refs.pop(0) for name in KEPT})
+    tables = [[refs.pop(0) for _ in SIZES] for _ in range(5)]
+    R.pay, R.parts = tables[0], tables[1:]
+    D = Device(n_seq, n_res, refs)
     barrier = pltpu.get_barrier_semaphore()
 
     @pl.loop(1, n_seq * n_res)
     def _(t):
         pl.semaphore_signal(barrier, inc=1, device_id=all_peers(D, t), device_id_type=MESH)
 
-    used = 0
-    for step, count in STEPS:
-        if count:
-            if not used:
-                pl.semaphore_wait(barrier, n_seq * n_res - 1)
-            step(R, D, sems[2 * used : 2 * used + 2 * count])
-            used += count
-        else:
-            step(R, D)
+    for step in STEPS:
+        step(R, D)
 
 
 def last_kernel(n_seq, n_res, names, *refs):
-    R = SimpleNamespace(**dict(zip(names, refs)))
-    D = SimpleNamespace(s=lax.axis_index("seq"), r=lax.axis_index("res"), ns=n_seq, nr=n_res)
-    p_finish(R, D)
+    refs = list(refs)
+    full = [refs.pop(0) for _ in SIZES]
+    R = SimpleNamespace(full=full, **dict(zip(names, refs)))
+    p_finish(R, Device(n_seq, n_res, ()))
 
 
 ARGS = dict(
@@ -1668,37 +1764,34 @@
             env[name] = value.reshape(1, -1)
     env.update(vet=env["vet"].T, w_oit=env["w_oit"].T, w_edt=env["w_edt"].T)
     space = pl.BlockSpec(memory_space=pltpu.VMEM)
-    exchanges = sum(count for _, count in STEPS)
     slots = n_seq * n_res
 
-    def shapes(table):
-        return [jax.ShapeDtypeStruct(*entry) for entry in table.values()]
+    def shapes(entries):
+        return [jax.ShapeDtypeStruct(*entry) for entry in entries]
 
     large = {name: RESULTS[name] for name in LARGE}
-    middle = dict(**large, **MIDDLE)
-    inputs = [name for name in env if name not in LAST_ONLY]
     values = pl.pallas_call(
-        functools.partial(first_kernel, n_seq, n_res, (*inputs, *middle, *KEPT), exchanges),
-        out_shape=shapes(middle),
-        in_specs=[space] * len(inputs),
-        out_specs=[space] * len(middle),
-        scratch_shapes=[pltpu.VMEM(*entry) for entry in KEPT.values()]
-        + [pltpu.SemaphoreType.DMA((slots,))] * (2 * exchanges),
+        functools.partial(first_kernel, n_seq, n_res, (*env, *large)),
+        out_shape=shapes((*large.values(), *PAYLOADS)),
+        in_specs=[space] * len(env),
+        out_specs=[space] * (len(large) + len(PAYLOADS)),
+        scratch_shapes=[pltpu.VMEM(*entry) for entry in (*KEPT.values(), *PAYLOADS, *PARTIAL)]
+        + [pltpu.SemaphoreType.DMA((slots,))] * (2 * EXCHANGES),
         compiler_params=pltpu.CompilerParams(
-            vmem_limit_bytes=60 * 2**20, collective_id=0, has_side_effects=True
+            vmem_limit_bytes=62 * 2**20, collective_id=0, has_side_effects=True
         ),
-    )(*[env[name] for name in inputs])
-    env.update(zip(middle, values))
+    )(*env.values())
+    full = values[len(large) :]
+    env.update(zip(large, values))
     small = {name: entry for name, entry in RESULTS.items() if name not in large}
-    inputs = [*FINISH]
     values = pl.pallas_call(
-        functools.partial(last_kernel, n_seq, n_res, (*inputs, *small, *FINISH_KEPT)),
-        out_shape=shapes(small),
-        in_specs=[space] * len(inputs),
+        functools.partial(last_kernel, n_seq, n_res, (*FINISH, *small, *FINISH_KEPT)),
+        out_shape=shapes(small.values()),
+        in_specs=[space] * (len(full) + len(FINISH)),
         out_specs=[space] * len(small),
         scratch_shapes=[pltpu.VMEM(*entry) for entry in FINISH_KEPT.values()],
         compiler_params=pltpu.CompilerParams(vmem_limit_bytes=60 * 2**20),
-    )(*[env[name] for name in inputs])
+    )(*full, *[env[name] for name in FINISH])
     env.update(zip(small, values))
     results = [env[name] for name in RESULTS]
     for index, value in enumerate(results):

time: 363 us -> 289 us (0.80)
  Pallas kernels: 359 us -> 285 us
    pallas_call x2, Pallas kernels: 359 us -> 285 us  [the longest x1 281 us: fast_shards(): pl.pallas_call(functools.partial(first_kernel, n_seq, n_res, (*env, *larg...]
where the time goes in v2:
time: 289 us
  Pallas kernels  285 us (99%)
  local copies, waits for them, and re-layouts  3.43 us (1%)
    pallas_call x1, Pallas kernels, fast_shards(): pl.pallas_call(functools.partial(first_kernel, n_seq, n_res, (*env, *larg...  281 us

profile of v2, /device:TPU:1, one launch (start us, length us, event | category | flops | bytes accessed | tf_op | source)
XLA Modules:
  0.0 289.0 jit_solution(14508826548076850387)
XLA Ops:
  0.7 281.3 %shard_map.501 = (bf16[4,64,256]{2,1,0:T(8,128)(2,1)}, bf16[32,64,128]{2,1,0:T(8,128)(2,1)}, f32[4,64,256]{2,1,0:T(8,128)}, f32[32,64,128]{2,1,0:T(8,128)}, bf16...) custom-call(bf16[4,64,256]{2,1,0:T(8,128)(2,1)} %refs_0_.1, ...), custom_call_target="tpu_custom_call" | custom-call | tf_op jit(solution)/shard_map/pallas_call | solution.py:1773
  282.0 0.0 copy-start.3
  282.0 0.0 copy-start.1
  282.0 3.6 %shard_map.502 = (f32[32,64]{1,0:T(8,128)}, f32[3,32]{1,0:T(4,128)}, f32[32,64]{1,0:T(8,128)}, f32[3,32]{1,0:T(4,128)}, f32[1,256]{1,0:T(1,128)}, /*index=5*/f32...) custom-call(bf16[2560,128]{1,0:T(8,128)(2,1)} %get-tuple-element.61., ...), custom_call_target="tpu_custom_call" | custom-call | tf_op jit(solution)/shard_map/pallas_call | solution.py:1787
  285.6 0.0 copy-start
  285.6 0.0 copy-done.3
  285.6 0.7 copy.62
  286.3 0.0 copy-done.1
  286.3 0.0 copy-start.2
  286.3 0.8 copy.63
  287.1 0.3 copy-done.2
  287.4 0.7 copy.64
  288.1 0.0 copy-done
  288.1 1.0 copy.65
Async XLA Ops:
  282.0 3.6 %copy-start.3 = (bf16[4,64,256]{2,1,0:T(8,128)(2,1)S(1)}, bf16[4,64,256]{2,1,0:T(8,128)(2,1)}, u32[]{:S(2)}) copy-start(bf16[4,64,256]{2,1,0:T(8,128)(2,1)} %get-tuple-element.118) | copy-start | bytes 393220
  282.0 4.3 %copy-start.1 = (bf16[32,64,128]{2,1,0:T(8,128)(2,1)S(1)}, bf16[32,64,128]{2,1,0:T(8,128)(2,1)}, u32[]{:S(2)}) copy-start(bf16[32,64,128]{2,1,0:T(8,128)(2,1)} %get-tuple-element.119) | copy-start | bytes 1572868
  285.6 2.5 copy-start
  286.3 1.1 copy-start.2

commit v3 on v2

--- a/solution.py
+++ b/solution.py
@@ -539,61 +539,56 @@
     return D.s, lax.rem(D.r + t, D.nr)
 
 
-def remote(src, dst, sems, slot, peer):
+def remote(src, dst, send, recv, peer):
     return pltpu.make_async_remote_copy(
         src_ref=src,
         dst_ref=dst,
-        send_sem=sems[0].at[slot],
-        recv_sem=sems[1].at[slot],
+        send_sem=send,
+        recv_sem=recv,
         device_id=peer,
         device_id_type=MESH,
     )
 
 
-def swap(D, src_at, dst_at, sems, count, peers, index, me):
-    def copy(t):
-        peer = peers(D, t)
-        return remote(src_at(index(*peer)), dst_at(me), sems, t, peer)
+def swap(D, src_at, dst_at, count, peers, index, me, like):
+    send, recv = D.take()
 
     @pl.loop(1, count)
     def _(t):
-        copy(t).start()
-
-    return copy
-
-
-def swap_wait(copy, count):
-    @pl.loop(1, count)
-    def _(t):
-        copy(t).wait()
+        peer = peers(D, t)
+        remote(src_at(index(*peer)), dst_at(me), send, recv, peer).start()
+
+    def wait():
+        done = remote(like, like, send, recv, peers(D, 1))
+        done.wait_send()
+        done.wait_recv()
+
+    return wait
 
 
 def start_all(D, src, dst, first, size):
     n = D.ns * D.nr
     me = D.s * D.nr + D.r
     rows = pl.ds(first, size)
-    copy = swap(
+    dst[me, rows, :] = src[me, rows, :]
+    return swap(
         D,
         lambda i: src.at[i, rows],
         lambda i: dst.at[i, rows],
-        D.take(),
         n,
         all_peers,
         lambda ps, pr: ps * D.nr + pr,
         me,
-    )
-    dst[me, rows, :] = src[me, rows, :]
-    return lambda: swap_wait(copy, n)
-
-
-def start_seq(D, src_at, dst_at):
-    copy = swap(D, src_at, dst_at, D.take(), D.ns, seq_peers, lambda ps, pr: ps, D.s)
-    return lambda: swap_wait(copy, D.ns)
-
-
-def start_res(D, src_at, dst_at):
-    copy = swap(D, src_at, dst_at, D.take(), D.nr, res_peers, lambda ps, pr: pr, D.r)
-    return lambda: swap_wait(copy, D.nr)
+        dst.at[pl.ds(0, n - 1), rows],
+    )
+
+
+def start_seq(D, src_at, dst_at, like):
+    return swap(D, src_at, dst_at, D.ns, seq_peers, lambda ps, pr: ps, D.s, like)
+
+
+def start_res(D, src_at, dst_at, like):
+    return swap(D, src_at, dst_at, D.nr, res_peers, lambda ps, pr: pr, D.r, like)
 
 
 def pack_columns(value, send):
@@ -607,7 +602,7 @@
 
 def start_columns(D, send, recv):
     recv[D.s] = send[D.s]
-    return start_seq(D, lambda i: send.at[i], lambda i: recv.at[i])
+    return start_seq(D, lambda i: send.at[i], lambda i: recv.at[i], recv.at[pl.ds(0, D.ns - 1)])
 
 
 def unpack_columns(R, recv, target):
@@ -625,8 +620,10 @@
     pack_columns(R.x, R.xsend)
     D.ready()
     wait = start_columns(D, R.xsend, R.xrecv)
+    R.arrived("adj_a")
     pack_columns(R.adj_a, R.asend)
     R.wait_adjoint = start_columns(D, R.asend, R.arecv)
+    R.arrived("w_ti", "w_ii", "w_oo", "w_qkvg", "w_ao", "pe", "adj_c")
     R.w1t[...] = R.w_ti[...].astype(F32).T.astype(BF16)
     R.w2t[...] = R.w_ii[...].astype(F32).T.astype(BF16)
     R.wo1t[...] = R.w_to[...].astype(F32).T.astype(BF16)
@@ -681,26 +678,20 @@
 
 
 def p_outer_exchange(R, D):
-    sems = D.take()
+    send, recv = R.out_send, R.out_recv
+    D.all_ready()
     owner = 2 * D.r + D.s // 4
     slot = D.s % 4
 
-    def left(k):
-        return remote(R.lsend, R.lall.at[slot], sems, k, (owner, k))
+    def left(k, to):
+        return remote(R.lsend, R.lall.at[to], send.at[k], recv.at[to], (owner, k))
 
     for k in range(4):
         mine = (owner == D.s) & (D.r == k)
 
         @pl.when(jnp.logical_not(mine))
         def _():
-            pltpu.make_async_remote_copy(
-                src_ref=R.lsend,
-                dst_ref=R.lall.at[slot],
-                send_sem=sems[0].at[k],
-                recv_sem=sems[1].at[slot],
-                device_id=(owner, k),
-                device_id_type=MESH,
-            ).start()
+            left(k, slot).start()
 
         @pl.when(mine)
         def _():
@@ -709,7 +700,7 @@
     here = pl.ds(pl.multiple_of(8 * D.s, 8), 8)
 
     def right(t):
-        return remote(R.rsend, R.rall.at[here], sems, 4 + t, seq_peers(D, t))
+        return remote(R.rsend, R.rall.at[here], send.at[4 + t], recv.at[4 + t], seq_peers(D, t))
 
     @pl.loop(1, 8)
     def _(t):
@@ -720,22 +711,14 @@
     for k in range(4):
         mine = (owner == D.s) & (D.r == k)
         theirs = (4 * (D.s % 2) + k == D.s) & (D.s // 2 == D.r)
-        token = pltpu.make_async_remote_copy(
-            src_ref=R.lsend,
-            dst_ref=R.lall.at[k],
-            send_sem=sems[0].at[k],
-            recv_sem=sems[1].at[k],
-            device_id=(owner, k),
-            device_id_type=MESH,
-        )
 
         @pl.when(jnp.logical_not(mine))
         def _():
-            token.wait_send()
+            left(k, k).wait_send()
 
         @pl.when(jnp.logical_not(theirs))
         def _():
-            token.wait_recv()
+            left(k, k).wait_recv()
 
     @pl.loop(1, 8)
     def _(t):
@@ -1047,6 +1030,8 @@
             R.pair_out[m] = out[:64]
             R.pair_out[16 + m] = out[64:]
 
+    R.leave("pair_out")
+
 
 def pack_single(R, send):
     @pl.loop(0, 32, unroll=4)
@@ -1153,6 +1138,10 @@
             R.dopm[m] = small[:64]
             R.dopm[16 + m] = small[64:]
 
+    R.leave("pair_grad")
+
+
+def p_pair_grads(R, D):
     R.g_ti[...] = dot_nt(R.nb3[...], R.dtri1[...])
     R.gg3[...] = jnp.sum(R.a_g3[...], 1, keepdims=True)
 
@@ -1175,35 +1164,38 @@
         def _(k):
             grad = jnp.concatenate([R.dopm[2 * k], R.dopm[2 * k + 1]], 1)
             both = dot_nn(right, grad).astype(BF16)
-            R.yg[:, 2 * k] = both[:, :LANES].reshape(8, 32, LANES)
-            R.yg[:, 2 * k + 1] = both[:, LANES:].reshape(8, 32, LANES)
+            for h in range(2):
+                at = pl.ds(pl.multiple_of(64 * k + 32 * h, 32), 32)
+                for u in range(8):
+                    block = both[32 * u : 32 * u + 32, LANES * h : LANES * h + LANES]
+                    R.zb[8 * g + u, at, :] = block
 
         weights = jnp.concatenate([outer_weight(R, 8 * g + u) for u in range(8)], 1)
-        rows = jnp.concatenate([R.yg[u].reshape(1024, LANES) for u in range(8)], 1)
-        R.dleft[...] += dot_nt(weights, rows)
+        R.dleft[...] += dot_nt(weights, jnp.concatenate([R.zb[8 * g + u] for u in range(8)], 1))
+
+    for q in range(4):
+        R.dls[q] = R.dleft[:, 256 * q : 256 * q + 256].astype(BF16)
+
+
+def p_outer_grads(R, D):
+    @pl.loop(0, 4)
+    def _(g):
+        rows = jnp.concatenate([R.zb[8 * g + u] for u in range(8)], 1)
         total = dot_nn(R.lt[...], rows)
         for u in range(8):
             R.st1[pl.ds(8 * g + u, 32, stride=32), :] = total[:, LANES * u : LANES * u + LANES]
 
     R.g_oo[...] = R.st1[0:1024, :]
-    for q in range(4):
-        R.dls[q] = R.dleft[:, 256 * q : 256 * q + 256].astype(BF16)
 
 
 def p_outer_return(R, D):
-    sems = D.take()
+    send, recv = R.back_send, R.back_recv
     column_res = D.s // 2
     owner = 2 * D.r + D.s // 4
 
     def left(q, slot):
-        return pltpu.make_async_remote_copy(
-            src_ref=R.dls.at[q],
-            dst_ref=R.dlr.at[slot],
-            send_sem=sems[0].at[q],
-            recv_sem=sems[1].at[slot],
-            device_id=(4 * (D.s % 2) + q, column_res),
-            device_id_type=MESH,
-        )
+        peer = (4 * (D.s % 2) + q, column_res)
+        return remote(R.dls.at[q], R.dlr.at[slot], send.at[q], recv.at[slot], peer)
 
     for q in range(4):
         mine = (4 * (D.s % 2) + q == D.s) & (column_res == D.r)
@@ -1219,13 +1211,17 @@
     def right(t):
         peer = seq_peers(D, t)
         at = pl.ds(pl.multiple_of(8 * peer[0], 8), 8)
-        return remote(R.dright.at[at], R.drr.at[D.s], sems, 4 + t, peer)
+        return remote(R.dright.at[at], R.drr.at[D.s], send.at[4 + t], recv.at[4 + t], peer)
 
     @pl.loop(1, 8)
     def _(t):
         right(t).start()
 
     R.drr[D.s] = R.dright[pl.ds(pl.multiple_of(8 * D.s, 8), 8), :]
+    p_pair_grads(R, D)
+    p_sum0(R, D)
+    p_outer_grads(R, D)
+    p_sum1(R, D)
 
     for q in range(4):
         mine = (4 * (D.s % 2) + q == D.s) & (column_res == D.r)
@@ -1245,7 +1241,6 @@
 
 
 def p_attention_back(R, D):
-    next(R.sum0)
     flag_rows = flag_column(R.fl[...].astype(F32))
     live = (flag_rows > 0).astype(F32)
     left = R.dlr[0].astype(F32)
@@ -1332,6 +1327,7 @@
 def p_take_value(R, D):
     R.wait_value()
     ungroup_columns(R.orecv, R.msa_out)
+    R.leave("msa_out")
     R.wait_adjoint()
     unpack_columns(R, R.arecv, R.ac)
 
@@ -1388,7 +1384,10 @@
     part = eighth // 4
     pack_segment(R, index)
     first[D.s] = pay[rows_of(D.s, eighth), :]
-    wait = start_seq(D, lambda i: pay.at[rows_of(i, eighth)], lambda i: first.at[i])
+    most = pl.ds(0, eighth * (D.ns - 1))
+    wait = start_seq(
+        D, lambda i: pay.at[rows_of(i, eighth)], lambda i: first.at[i], pay.at[most]
+    )
     yield
     wait()
     total = first[0].astype(F32)
@@ -1396,7 +1395,10 @@
         total += first[k].astype(F32)
     second[...] = total.astype(BF16)
     third[D.r] = second[rows_of(D.r, part), :]
-    wait = start_res(D, lambda i: second.at[rows_of(i, part)], lambda i: third.at[i])
+    some = pl.ds(0, part * (D.nr - 1))
+    wait = start_res(
+        D, lambda i: second.at[rows_of(i, part)], lambda i: third.at[i], second.at[some]
+    )
     yield
     wait()
     total = third[0].astype(F32)
@@ -1405,14 +1407,18 @@
     fourth[...] = total.astype(BF16)
     mine = pl.ds(pl.multiple_of(D.s * eighth + D.r * part, part), part)
     full[mine, :] = fourth[...]
-    wait = start_res(D, lambda i: fourth, lambda i: full.at[mine])
+    wait = start_res(D, lambda i: fourth, lambda i: full.at[mine], full.at[some])
     yield
     wait()
     wait = start_seq(
-        D, lambda i: full.at[rows_of(D.s, eighth)], lambda i: full.at[rows_of(i, eighth)]
+        D,
+        lambda i: full.at[rows_of(D.s, eighth)],
+        lambda i: full.at[rows_of(i, eighth)],
+        full.at[most],
     )
     yield
     wait()
+    R.leave(index)
 
 
 def p_sum0(R, D):
@@ -1450,29 +1456,38 @@
         if wait:
             wait()
             ungroup_columns(R.grecv, R.msa_grad)
+            R.leave("msa_grad")
             wait = None
 
 
+def unpack_segment(R, index):
+    held = {}
+    for name, start, count, lane, width in segment_layout(index)[0]:
+        value = R.full[index][start : start + count, 0:width].astype(F32)
+        if name.startswith("g_"):
+            getattr(R, "o_" + name)[:, lane : lane + width] = value
+        else:
+            held.setdefault(name, []).append(value)
+    return {name: jnp.concatenate(parts, 1) for name, parts in held.items()}
+
+
+def p_finish_first(R, D):
+    unpack_segment(R, 1)
+    held = unpack_segment(R, 2)
+    small = held["small1"]
+    for k, target in enumerate((R.o_gg1, R.o_gg2)):
+        for half in range(2):
+            at = 2 * k + half
+            target[:, LANES * half : LANES * half + LANES] = small[at : at + 1]
+
+
 def p_finish(R, D):
-    held = {}
-    for index in range(len(SEGMENTS)):
-        for name, start, count, lane, width in segment_layout(index)[0]:
-            value = R.full[index][start : start + count, 0:width].astype(F32)
-            if name.startswith("g_"):
-                getattr(R, "o_" + name)[:, lane : lane + width] = value
-            else:
-                held.setdefault(name, []).append(value)
-    held = {name: jnp.concatenate(parts, 1) for name, parts in held.items()}
+    held = unpack_segment(R, 0)
     small = held["small0"]
     for k, target in enumerate((R.o_gg3, R.o_gg4, R.o_gg5, R.o_gg6)):
         target[...] = small[k : k + 1, :]
     R.o_g_ds[...] = small[4:5, :64]
     R.o_g_sl[...] = small[5:6, :64]
-    small = held["small1"]
-    for k, target in enumerate((R.o_gg1, R.o_gg2)):
-        for half in range(2):
-            at = 2 * k + half
-            target[:, LANES * half : LANES * half + LANES] = small[at : at + 1]
     mean_b = held["s_mean"].astype(BF16)
     R.o_g_up[...] = dot_nt(mean_b, held["s_vadj"].astype(BF16))
     d_node = jnp.concatenate([held["s_own"], held["s_other"]], 0).astype(BF16)
@@ -1505,7 +1520,6 @@
     grecv=((8, 2, 16, 256), BF16),
     wst=((1024, 128), F32),
     lt=((32, 1024), BF16),
-    yg=((8, 32, 32, 128), BF16),
     tm=((4, 256, 256), BF16),
     geo=((32, 2048), F32),
     pre=((128, 2048), F32),
@@ -1617,6 +1631,7 @@
     + [((size // 32, 128), BF16) for size in SIZES]
 )
 LARGE = ("msa_out", "pair_out", "msa_grad", "pair_grad")
+MOVED_IN = ("adj_a", "w_qkvg", "w_ao", "w_oo", "w_ti", "w_ii", "pe", "adj_c")
 FINISH = ("vet", "w_up", "w_nd", "adj_v", "at", "adj_l")
 FINISH_KEPT = dict(
     rows_f=((256, 128), F32), rows_g=((256, 128), F32), xyz=((128, 256), F32)
@@ -1668,54 +1683,105 @@
     p_between,
     p_back1,
     p_pair_end,
-    p_sum0,
     p_outer_back,
-    p_sum1,
     p_outer_return,
     p_attention_back,
     p_sum2,
     p_sums,
 )
-EXCHANGES = 35
-PARTS = 2
+PARTS = 4
+EXCHANGES = 16 + 8 * PARTS
 
 
 class Device:
-    def __init__(self, n_seq, n_res, sems):
+    def __init__(self, n_seq, n_res, sems, rows_in):
         self.s, self.r = lax.axis_index("seq"), lax.axis_index("res")
         self.ns, self.nr = n_seq, n_res
-        self.sems = list(sems)
+        self.sems = sems
+        self.rows_in = rows_in
+        self.used = 0
 
     def take(self):
-        return self.sems.pop(0), self.sems.pop(0)
+        self.used += 2
+        assert self.used <= 2 * EXCHANGES
+        return self.sems.at[self.used - 2], self.sems.at[self.used - 1]
 
     def ready(self):
-        pl.semaphore_wait(pltpu.get_barrier_semaphore(), self.ns * self.nr - 1)
+        pl.semaphore_wait(pltpu.get_barrier_semaphore(), self.ns + self.nr - 2)
+
+        @pl.loop(1, self.nr)
+        def _(t):
+            pl.semaphore_signal(self.rows_in, inc=1, device_id=res_peers(self, t), device_id_type=MESH)
+
+    def all_ready(self):
+        pl.semaphore_wait(self.rows_in, self.nr - 1)
 
 
 def first_kernel(n_seq, n_res, names, *refs):
     refs = list(refs)
-    R = SimpleNamespace(**{name: refs.pop(0) for name in names})
-    R.full = [refs.pop(0) for _ in SIZES]
-    R.__dict__.update({name: refs.pop(0) for name in KEPT})
-    tables = [[refs.pop(0) for _ in SIZES] for _ in range(5)]
-    R.pay, R.parts = tables[0], tables[1:]
-    D = Device(n_seq, n_res, refs)
+    far = {name: refs.pop(0) for name in names}
+    far_full = [refs.pop(0) for _ in SIZES]
+    R = SimpleNamespace(**far)
+    R.__dict__.update({name: refs.pop(0) for name in (*KEPT, *MOVED_IN, *LARGE)})
+    tables = [[refs.pop(0) for _ in SIZES] for _ in range(6)]
+    R.full, R.pay, R.parts = tables[0], tables[1], tables[2:]
+    R.out_send, R.out_recv, R.back_send, R.back_recv, R.move = refs[2:]
+    D = Device(n_seq, n_res, refs[0], refs[1])
     barrier = pltpu.get_barrier_semaphore()
 
-    @pl.loop(1, n_seq * n_res)
-    def _(t):
-        pl.semaphore_signal(barrier, inc=1, device_id=all_peers(D, t), device_id_type=MESH)
-
+    for peers, count in ((seq_peers, n_seq), (res_peers, n_res)):
+
+        @pl.loop(1, count)
+        def _(t):
+            pl.semaphore_signal(barrier, inc=1, device_id=peers(D, t), device_id_type=MESH)
+
+    moves = {}
+    for name in MOVED_IN:
+        moves[name] = pltpu.make_async_copy(far[name], getattr(R, name), R.move.at[len(moves)])
+        moves[name].start()
+    R.arrived = lambda *wanted: [moves.pop(name).wait() for name in wanted]
+    base = len(moves)
+    out = []
+
+    def leave(name):
+        if name in far:
+            source, target, at = getattr(R, name), far[name], LARGE.index(name)
+        else:
+            source, target, at = R.full[name], far_full[name], len(LARGE) + name
+        out.append(pltpu.make_async_copy(source, target, R.move.at[base + at]))
+        out[-1].start()
+
+    R.leave = leave
     for step in STEPS:
         step(R, D)
+    for copy in out:
+        copy.wait()
 
 
 def last_kernel(n_seq, n_res, names, *refs):
     refs = list(refs)
     full = [refs.pop(0) for _ in SIZES]
-    R = SimpleNamespace(full=full, **dict(zip(names, refs)))
-    p_finish(R, Device(n_seq, n_res, ()))
+    near = [refs.pop(0) for _ in LARGE]
+    R = SimpleNamespace(**{name: refs.pop(0) for name in names[: len(FINISH)]}, full=full)
+    away = [refs.pop(0) for _ in LARGE]
+    *refs, sems = refs
+    held = refs[-len(LARGE) :]
+    R.__dict__.update(zip(names[len(FINISH) :], refs))
+
+    def move(index, source, target):
+        copy = pltpu.make_async_copy(source, target, sems.at[index])
+        copy.start()
+        return copy
+
+    coming = [move(k, near[k], held[k]) for k in range(len(LARGE))]
+    D = Device(n_seq, n_res, None, None)
+    p_finish_first(R, D)
+    for copy in coming:
+        copy.wait()
+    going = [move(len(LARGE) + k, held[k], away[k]) for k in range(len(LARGE))]
+    p_finish(R, D)
+    for copy in going:
+        copy.wait()
 
 
 ARGS = dict(
@@ -1764,19 +1830,24 @@
             env[name] = value.reshape(1, -1)
     env.update(vet=env["vet"].T, w_oit=env["w_oit"].T, w_edt=env["w_edt"].T)
     space = pl.BlockSpec(memory_space=pltpu.VMEM)
-    slots = n_seq * n_res
 
     def shapes(entries):
         return [jax.ShapeDtypeStruct(*entry) for entry in entries]
 
     large = {name: RESULTS[name] for name in LARGE}
+    anywhere = pl.BlockSpec(memory_space=pl.ANY)
+    held = [(ARGS[name], BF16) for name in MOVED_IN] + [RESULTS[name] for name in LARGE]
     values = pl.pallas_call(
         functools.partial(first_kernel, n_seq, n_res, (*env, *large)),
         out_shape=shapes((*large.values(), *PAYLOADS)),
-        in_specs=[space] * len(env),
-        out_specs=[space] * (len(large) + len(PAYLOADS)),
-        scratch_shapes=[pltpu.VMEM(*entry) for entry in (*KEPT.values(), *PAYLOADS, *PARTIAL)]
-        + [pltpu.SemaphoreType.DMA((slots,))] * (2 * EXCHANGES),
+        in_specs=[anywhere if name in MOVED_IN else space for name in env],
+        out_specs=[anywhere] * (len(large) + len(PAYLOADS)),
+        scratch_shapes=[
+            pltpu.VMEM(*entry) for entry in (*KEPT.values(), *held, *PAYLOADS, *PAYLOADS, *PARTIAL)
+        ]
+        + [pltpu.SemaphoreType.DMA((2 * EXCHANGES,)), pltpu.SemaphoreType.REGULAR]
+        + [pltpu.SemaphoreType.DMA((12,))] * 4
+        + [pltpu.SemaphoreType.DMA((len(MOVED_IN) + len(LARGE) + len(SIZES),))],
         compiler_params=pltpu.CompilerParams(
             vmem_limit_bytes=62 * 2**20, collective_id=0, has_side_effects=True
         ),
@@ -1786,13 +1857,15 @@
     small = {name: entry for name, entry in RESULTS.items() if name not in large}
     values = pl.pallas_call(
         functools.partial(last_kernel, n_seq, n_res, (*FINISH, *small, *FINISH_KEPT)),
-        out_shape=shapes(small.values()),
-        in_specs=[space] * (len(full) + len(FINISH)),
-        out_specs=[space] * len(small),
-        scratch_shapes=[pltpu.VMEM(*entry) for entry in FINISH_KEPT.values()],
+        out_shape=shapes((*large.values(), *small.values())),
+        in_specs=[space] * len(full) + [anywhere] * len(LARGE) + [space] * len(FINISH),
+        out_specs=[anywhere] * len(LARGE) + [space] * len(small),
+        scratch_shapes=[pltpu.VMEM(*entry) for entry in FINISH_KEPT.values()]
+        + [pltpu.VMEM(*RESULTS[name]) for name in LARGE]
+        + [pltpu.SemaphoreType.DMA((2 * len(LARGE),))],
         compiler_params=pltpu.CompilerParams(vmem_limit_bytes=60 * 2**20),
-    )(*full, *[env[name] for name in FINISH])
-    env.update(zip(small, values))
+    )(*full, *[env[name] for name in LARGE], *[env[name] for name in FINISH])
+    env.update(zip((*large, *small), values))
     results = [env[name] for name in RESULTS]
     for index, value in enumerate(results):
         if value.shape[0] == 1:

time: 289 us -> 264 us (0.913)
  Pallas kernels: 285 us -> 263 us
  local copies, waits for them, and re-layouts: 3.43 us -> 0 us
    pallas_call x1, Pallas kernels: 281 us -> 257 us  [fast_shards(): pl.pallas_call(functools.partial(first_kernel, n_seq, n_res, (*env, *larg...]
    unnamed x12 -> x0, local copies, waits for them, and re-layouts: 3.43 us -> none
where the time goes in v3:
time: 264 us
  Pallas kernels  263 us (100%)
    pallas_call x1, Pallas kernels, fast_shards(): pl.pallas_call(functools.partial(first_kernel, n_seq, n_res, (*env, *larg...  257 us
    pallas_call x1, Pallas kernels, fast_shards(): pl.pallas_call(functools.partial(last_kernel, n_seq, n_res, (*FINISH, *sm...  6.04 us

profile of v3, /device:TPU:1, one launch (start us, length us, event | category | flops | bytes accessed | tf_op | source)
XLA Modules:
  0.0 263.7 jit_solution(8339554082255982588)
XLA Ops:
  0.7 256.8 %shard_map.501 = (bf16[4,64,256]{2,1,0:T(8,128)(2,1)}, bf16[32,64,128]{2,1,0:T(8,128)(2,1)}, f32[4,64,256]{2,1,0:T(8,128)}, f32[32,64,128]{2,1,0:T(8,128)}, bf16...) custom-call(bf16[4,64,256]{2,1,0:T(8,128)(2,1)} %refs_0_.1, ...), custom_call_target="tpu_custom_call" | custom-call | tf_op jit(solution)/shard_map/pallas_call | solution.py:1840
  257.5 6.0 %shard_map.502 = (bf16[4,64,256]{2,1,0:T(8,128)(2,1)}, bf16[32,64,128]{2,1,0:T(8,128)(2,1)}, f32[4,64,256]{2,1,0:T(8,128)}, f32[32,64,128]{2,1,0:T(8,128)}, f32[...) custom-call(bf16[2560,128]{1,0:T(8,128)(2,1)} %get-tuple-element.63., ...), custom_call_target="tpu_custom_call" | custom-call | tf_op jit(solution)/shard_map/pallas_call | solution.py:1858

commit v4 on v3

--- a/solution.py
+++ b/solution.py
@@ -528,7 +528,7 @@
 
 
 def all_peers(D, t):
-    return lax.rem(D.s + t // D.nr, D.ns), lax.rem(D.r + t % D.nr, D.nr)
+    return lax.rem(D.s + t % D.ns, D.ns), lax.rem(D.r + t // D.ns, D.nr)
 
 
 def seq_peers(D, t):
@@ -752,16 +752,82 @@
             for i in range(32):
                 R.zb[i, at, :] = part[32 * i : 32 * i + 32, LANES * u : LANES * u + LANES]
 
+
+def outer_rows(R, half):
     inverse = 1.0 / count_of(R)
     right = R.rall[...].astype(BF16)
 
-    @pl.loop(0, 16, unroll=4)
+    @pl.loop(8 * half, 8 * half + 8, unroll=4)
     def _(m):
         both = dot_nn(right, jnp.concatenate([R.zb[m], R.zb[16 + m]], 1)) * inverse
         rows = [
             both[:, LANES * h : LANES * h + LANES] + R.pe[16 * h + m].astype(F32) for h in range(2)
         ]
         R.pair1[:, pl.ds(pl.multiple_of(m * LANES, LANES), LANES)] = jnp.concatenate(rows, 0).T
+
+
+def pack_both(R, half):
+    @pl.loop(0, 32, unroll=4)
+    def _(d):
+        for pair in range(2):
+            for k, stage in ((0, R.st0), (1, R.st1)):
+                rows = tile_rows(stage, 64 * d + 32 * pair + 8 * half)
+                first = 64 * half + 32 * pair + 16 * k
+                R.lrs[d, first : first + 16, :] = rows.astype(BF16)
+
+
+def pack_single(R, stage, half):
+    @pl.loop(0, 32, unroll=4)
+    def _(d):
+        for pair in range(2):
+            first = 32 * half + 16 * pair
+            rows = tile_rows(stage, 64 * d + 32 * pair + 8 * half)
+            R.ts[d, first : first + 16, :] = rows.astype(BF16)
+
+
+def tile_rows(stage, start):
+    start = pl.multiple_of(start, 8)
+    return jnp.concatenate([stage[pl.ds(start, 8), :], stage[pl.ds(start + 16, 8), :]], 0)
+
+
+def untile(stage, start, rows):
+    start = pl.multiple_of(start, 8)
+    stage[pl.ds(start, 8), :] = rows[:8]
+    stage[pl.ds(start + 16, 8), :] = rows[8:]
+
+
+def stage_single(recv, stage, half):
+    @pl.loop(0, 32, unroll=4)
+    def _(d):
+        for pair in range(2):
+            first = 32 * half + 16 * pair
+            rows = recv[d, first : first + 16, :].astype(F32)
+            untile(stage, 64 * d + 32 * pair + 8 * half, rows)
+
+
+def stage_both(R, recv, half):
+    @pl.loop(0, 32, unroll=4)
+    def _(d):
+        for pair in range(2):
+            for k, stage in ((0, R.st0), (1, R.st1)):
+                first = 64 * half + 32 * pair + 16 * k
+                rows = recv[d, first : first + 16, :].astype(F32)
+                untile(stage, 64 * d + 32 * pair + 8 * half, rows)
+
+
+def send_part(D, src, dst, table, half, pair):
+    size = src.shape[1] // 4
+    table[half, pair] = start_all(D, src, dst, size * (2 * half + pair), size)
+
+
+def send_half(D, src, dst, table, half):
+    for pair in range(2):
+        send_part(D, src, dst, table, half, pair)
+
+
+def wait_half(table, half):
+    for pair in range(2):
+        table[half, pair]()
 
 
 def entry_chunk(R, pair, gain, w_t, nb, j):
@@ -773,129 +839,123 @@
         lane_ungroup(stage, j, sigmoid(linear[128:]) * linear[:128])
 
 
-def pack_both(R, send):
-    @pl.loop(0, 32, unroll=4)
-    def _(d):
-        at = pl.ds(pl.multiple_of(64 * d, 64), 64)
-        first = R.st0[at, :].astype(BF16)
-        second = R.st1[at, :].astype(BF16)
-        for c in range(4):
-            send[d, 32 * c : 32 * c + 16, :] = first[16 * c : 16 * c + 16]
-            send[d, 32 * c + 16 : 32 * c + 32, :] = second[16 * c : 16 * c + 16]
-
-
 def p_entry1(R, D):
     gain = column(R.g3[...])
-
-    @pl.loop(0, 8, unroll=4)
-    def _(j):
-        entry_chunk(R, R.pair1[:, chunk_at(j)], gain, R.w1t, R.nb3, j)
-
-    pack_both(R, R.lrs)
-
-
-def gather_mat(recv, off, mats, at):
+    for half in range(2):
+        outer_rows(R, half)
+
+        @pl.loop(4 * half, 4 * half + 4, unroll=4)
+        def _(j):
+            entry_chunk(R, R.pair1[:, chunk_at(j)], gain, R.w1t, R.nb3, j)
+
+        pack_both(R, half)
+        send_half(D, R.lrs, R.lr1r, R.waits, half)
+
+
+def gather_pair(recv, pair, k, mats, at):
+    size = recv.shape[1] // 4
+
     @pl.loop(0, 8, unroll=4)
     def _(s):
         top = pl.ds(pl.multiple_of(32 * s, 32), 16)
         low = pl.ds(pl.multiple_of(32 * s + 16, 16), 16)
         for p in range(2):
-            a = recv[4 * s + 2 * p, off : off + 16, :]
-            b = recv[4 * s + 2 * p + 1, off : off + 16, :]
+            tiles = []
+            for q in range(2):
+                halves = []
+                for half in range(2):
+                    first = size * (2 * half + pair) + 16 * k
+                    block = recv[4 * s + 2 * p + q, first : first + 16, :]
+                    halves.append(block.astype(F32))
+                tiles.append(halves)
             lanes = slice(LANES * p, LANES * p + LANES)
-            mats[at, top, lanes] = jnp.concatenate([a[:, :64], b[:, :64]], 1)
-            mats[at, low, lanes] = jnp.concatenate([a[:, 64:], b[:, 64:]], 1)
-
-
-def scatter_mat(mat, send, off):
+            for c in range(2):
+                rows = slice(8 * c, 8 * c + 8)
+                a, b = (jnp.concatenate([h[rows] for h in halves], 0) for halves in tiles)
+                mats[at + c, top, lanes] = jnp.concatenate([a[:, :64], b[:, :64]], 1).astype(BF16)
+                mats[at + c, low, lanes] = jnp.concatenate([a[:, 64:], b[:, 64:]], 1).astype(BF16)
+
+
+def scatter_pair(mats, send, pair, k):
+    size = send.shape[1] // 4
+
     @pl.loop(0, 8, unroll=4)
     def _(s):
         for p in range(2):
             lanes = slice(LANES * p, LANES * p + LANES)
-            a = mat[pl.ds(pl.multiple_of(32 * s, 32), 16), lanes]
-            b = mat[pl.ds(pl.multiple_of(32 * s + 16, 16), 16), lanes]
-            send[4 * s + 2 * p, off : off + 16, :] = jnp.concatenate([a[:, :64], b[:, :64]], 1)
-            send[4 * s + 2 * p + 1, off : off + 16, :] = jnp.concatenate([a[:, 64:], b[:, 64:]], 1)
+            tiles = [[], []]
+            for c in range(2):
+                a = mats[c, pl.ds(pl.multiple_of(32 * s, 32), 16), lanes]
+                b = mats[c, pl.ds(pl.multiple_of(32 * s + 16, 16), 16), lanes]
+                tiles[0].append(jnp.concatenate([a[:, :64], b[:, :64]], 1))
+                tiles[1].append(jnp.concatenate([a[:, 64:], b[:, 64:]], 1))
+            for q in range(2):
+                for half in range(2):
+                    first = size * (2 * half + pair) + 16 * k
+                    rows = slice(8 * half, 8 * half + 8)
+                    block = jnp.concatenate([tile[rows] for tile in tiles[q]], 0)
+                    send[4 * s + 2 * p + q, first : first + 16, :] = block.astype(BF16)
 
 
 def tri_forward(R, D, recv, mats, back, product, meanwhile):
-    size = 4 // PARTS
-    waits = [start_all(D, R.lrs, recv, 32 * size * h, 32 * size) for h in range(PARTS)]
     meanwhile(R, D)
-    later = []
-    for h in range(PARTS):
-        waits[h]()
-        for c in range(size * h, size * h + size):
-            gather_mat(recv, 32 * c, mats, c)
-            gather_mat(recv, 32 * c + 16, mats, 4 + c)
-            R.tm[c] = product(mats[c], mats[4 + c]).astype(BF16)
-            scatter_mat(R.tm.at[c], R.ts, 16 * c)
-        later.append(start_all(D, R.ts, back, 16 * size * h, 16 * size))
-    for wait in later:
-        wait()
+    for pair in range(2):
+        R.waits[0, pair]()
+        R.waits[1, pair]()
+        gather_pair(recv, pair, 0, mats, 2 * pair)
+        gather_pair(recv, pair, 1, mats, 4 + 2 * pair)
+        for c in range(2):
+            R.tm[c] = product(mats[2 * pair + c], mats[4 + 2 * pair + c])
+        scatter_pair(R.tm, R.ts, pair, 0)
+        send_part(D, R.ts, back, R.later, 0, pair)
+    for pair in range(2):
+        send_part(D, R.ts, back, R.later, 1, pair)
 
 
 def tri_backward(R, D, recv, mats, back, products, meanwhile):
-    size = 4 // PARTS
-    waits = [start_all(D, R.ts, recv, 16 * size * h, 16 * size) for h in range(PARTS)]
     meanwhile(R, D)
-    later = []
-    for h in range(PARTS):
-        waits[h]()
-        for c in range(size * h, size * h + size):
-            gather_mat(recv, 16 * c, R.dm, c)
-            for k in range(2):
-                R.tm[c] = products[k](mats[c], mats[4 + c], R.dm[c]).astype(BF16)
-                scatter_mat(R.tm.at[c], R.lrs, 32 * c + 16 * k)
-        later.append(start_all(D, R.lrs, back, 32 * size * h, 32 * size))
-    for wait in later:
-        wait()
-
-
-def nothing(R, D):
-    pass
+    for pair in range(2):
+        R.waits[0, pair]()
+        R.waits[1, pair]()
+        gather_pair(recv, pair, 0, R.dm, 0)
+        for k in range(2):
+            for c in range(2):
+                at = 2 * pair + c
+                R.tm[c] = products[k](mats[at], mats[4 + at], R.dm[c])
+            scatter_pair(R.tm, R.lrs, pair, k)
+        send_part(D, R.lrs, back, R.later, 0, pair)
+    for pair in range(2):
+        send_part(D, R.lrs, back, R.later, 1, pair)
 
 
 def p_tri1(R, D):
     tri_forward(R, D, R.lr1r, R.mats1, R.t1r, dot_nt, p_still)
 
 
-def stage_single(recv, stage):
-    @pl.loop(0, 32, unroll=4)
-    def _(d):
-        stage[pl.ds(pl.multiple_of(64 * d, 64), 64), :] = recv[d].astype(F32)
-
-
-def stage_both(recv, first, second):
-    @pl.loop(0, 32, unroll=4)
-    def _(d):
-        at = pl.ds(pl.multiple_of(64 * d, 64), 64)
-        both = recv[d].astype(F32)
-        first[at, :] = jnp.concatenate([both[32 * c : 32 * c + 16] for c in range(4)], 0)
-        second[at, :] = jnp.concatenate([both[32 * c + 16 : 32 * c + 32] for c in range(4)], 0)
-
-
 def p_middle(R, D):
-    stage_single(R.t1r, R.st2)
     gain4 = column(R.g4[...])
     gain5 = column(R.g5[...])
-
-    @pl.loop(0, 8, unroll=4)
-    def _(j):
-        hat, _ = norm(lane_group(R.st2, j), 0)
-        nb4 = (hat * gain4).astype(BF16)
-        R.nb4[:, chunk_at(j)] = nb4
-        update = dot_nn(R.wo1t[...], nb4)
-        gate = sigmoid(dot_nn(R.w1t[512:, :], R.nb3[:, chunk_at(j)]))
-        pair2 = R.pair1[:, chunk_at(j)] + gate * update
-        R.pair2[:, chunk_at(j)] = pair2
-        entry_chunk(R, pair2, gain5, R.w2t, R.nb5, j)
-
-    pack_both(R, R.lrs)
+    for half in range(2):
+        wait_half(R.later, half)
+        stage_single(R.t1r, R.st2, half)
+
+        @pl.loop(4 * half, 4 * half + 4, unroll=4)
+        def _(j):
+            hat, _ = norm(lane_group(R.st2, j), 0)
+            nb4 = (hat * gain4).astype(BF16)
+            R.nb4[:, chunk_at(j)] = nb4
+            update = dot_nn(R.wo1t[...], nb4)
+            gate = sigmoid(dot_nn(R.w1t[512:, :], R.nb3[:, chunk_at(j)]))
+            pair2 = R.pair1[:, chunk_at(j)] + gate * update
+            R.pair2[:, chunk_at(j)] = pair2
+            entry_chunk(R, pair2, gain5, R.w2t, R.nb5, j)
+
+        pack_both(R, half)
+        send_half(D, R.lrs, R.lr2r, R.waits, half)
 
 
 def p_tri2(R, D):
-    tri_forward(R, D, R.lr2r, R.mats2, R.t2r, dot_tn, nothing)
+    tri_forward(R, D, R.lr2r, R.mats2, R.t2r, dot_tn, p_values)
 
 
 def chunk_rows(D, j):
@@ -947,14 +1007,12 @@
 
 
 def p_turn(R, D):
-    stage_single(R.t2r, R.st2)
     gain6 = column(R.g6[...])
     dist = column(R.w_ds[...])
     turn_weight = column(R.w_sl[...])
     R.a_g6[...] = jnp.zeros((128, CHUNK), F32)
 
-    @pl.loop(0, 8, unroll=4)
-    def _(j):
+    def chunk(j):
         here = chunk_at(j)
         hat, rstd = norm(lane_group(R.st2, j), 0)
         nb6 = (hat * gain6).astype(BF16)
@@ -997,7 +1055,12 @@
         R.a_g6[...] += d_nb * hat
         lane_ungroup(R.st0, j, norm_back(d_nb, gain6, hat, rstd, 0))
 
-    pack_single(R, R.ts)
+    for half in range(2):
+        wait_half(R.later, half)
+        stage_single(R.t2r, R.st2, half)
+        pl.loop(4 * half, 4 * half + 4, unroll=4)(chunk)
+        pack_single(R, R.st0, half)
+        send_half(D, R.ts, R.dt2r, R.waits, half)
 
 
 def p_turn_grads(R, D):
@@ -1033,10 +1096,11 @@
     R.leave("pair_out")
 
 
-def pack_single(R, send):
-    @pl.loop(0, 32, unroll=4)
-    def _(d):
-        send[d] = R.st0[pl.ds(pl.multiple_of(64 * d, 64), 64), :].astype(BF16)
+def p_turn_rest(R, D):
+    p_turn_grads(R, D)
+    p_sum0(R, D)
+    for half in range(2):
+        stage_single(R.t1r, R.st2, half)
 
 
 def p_back2(R, D):
@@ -1047,7 +1111,7 @@
         R.mats2,
         R.dlr2r,
         (lambda a, b, d: dot_nt(b, d), lambda a, b, d: dot_nn(a, d)),
-        p_turn_grads,
+        p_turn_rest,
     )
 
 
@@ -1065,15 +1129,13 @@
 
 
 def p_between(R, D):
-    stage_both(R.dlr2r, R.st0, R.st1)
-    stage_single(R.t1r, R.st2)
     gain4 = column(R.g4[...])
     gain5 = column(R.g5[...])
     R.a_g4[...] = jnp.zeros((128, CHUNK), F32)
     R.a_g5[...] = jnp.zeros((128, CHUNK), F32)
-
-    @pl.loop(0, 8, unroll=4)
-    def _(j):
+    next(R.sum0)
+
+    def chunk(j):
         here = chunk_at(j)
         gates_back(R, R.dtri2, R.w2t, R.nb5[:, here], j)
         d_nb5 = dot_nn(R.w_ii[...], R.dtri2[:, here])
@@ -1091,9 +1153,12 @@
         R.a_g4[...] += d_nb4 * hat4
         lane_ungroup(R.st3, j, norm_back(d_nb4, gain4, hat4, rstd4, 0))
 
-    @pl.loop(0, 32, unroll=4)
-    def _(d):
-        R.ts[d] = R.st3[pl.ds(pl.multiple_of(64 * d, 64), 64), :].astype(BF16)
+    for half in range(2):
+        wait_half(R.later, half)
+        stage_both(R, R.dlr2r, half)
+        pl.loop(4 * half, 4 * half + 4, unroll=4)(chunk)
+        pack_single(R, R.st3, half)
+        send_half(D, R.ts, R.dt1r, R.waits, half)
 
 
 def p_between_grads(R, D):
@@ -1101,6 +1166,8 @@
     R.g_to[...] = dot_nt(R.nb4[...], R.dup1[...])
     R.gg5[...] = jnp.sum(R.a_g5[...], 1, keepdims=True)
     R.gg4[...] = jnp.sum(R.a_g4[...], 1, keepdims=True)
+    p_sum1(R, D)
+    next(R.sum0)
 
 
 def p_back1(R, D):
@@ -1116,13 +1183,13 @@
 
 
 def p_pair_end(R, D):
-    stage_both(R.dlr1r, R.st0, R.st1)
+    next(R.sum0)
+    next(R.sum1)
     gain3 = column(R.g3[...])
     R.a_g3[...] = jnp.zeros((128, CHUNK), F32)
     inverse = 1.0 / count_of(R)
 
-    @pl.loop(0, 8, unroll=4)
-    def _(j):
+    def chunk(j):
         here = chunk_at(j)
         gates_back(R, R.dtri1, R.w1t, R.nb3[:, here], j)
         d_nb3 = dot_nn(R.w_ti[...], R.dtri1[:, here])
@@ -1138,6 +1205,10 @@
             R.dopm[m] = small[:64]
             R.dopm[16 + m] = small[64:]
 
+    for half in range(2):
+        wait_half(R.later, half)
+        stage_both(R, R.dlr1r, half)
+        pl.loop(4 * half, 4 * half + 4, unroll=4)(chunk)
     R.leave("pair_grad")
 
 
@@ -1219,9 +1290,10 @@
 
     R.drr[D.s] = R.dright[pl.ds(pl.multiple_of(8 * D.s, 8), 8), :]
     p_pair_grads(R, D)
-    p_sum0(R, D)
     p_outer_grads(R, D)
-    p_sum1(R, D)
+    p_sum2(R, D)
+    next(R.sum0, D)
+    next(R.sum1)
 
     for q in range(4):
         mine = (4 * (D.s % 2) + q == D.s) & (column_res == D.r)
@@ -1271,7 +1343,12 @@
     d_gated = dot_nt(d_exit, R.w_ao[...])
     R.datt[...] = (d_gated * gate).astype(BF16)
     R.dproj[:, 768:] = (d_gated * R.att[...] * gate * (1.0 - gate)).astype(BF16)
+    hat, rstd = norm(R.xc[...], -1)
+    R.normed[...] = (hat * R.g1[...]).astype(BF16)
+    R.c_gate[...] = dot_tn(R.normed[...], R.dproj[:, 768:])
+    p_sum3(R, D)
     R.dqkv[...] = jnp.zeros((256, 768), F32)
+    next(R.sum2)
 
     @pl.loop(0, 8, unroll=4)
     def _(head):
@@ -1290,11 +1367,9 @@
         R.dqkv[:, 512:768] += jnp.where(mine, dot_nn(probs.astype(BF16), d_att), 0.0)
 
     R.dproj[:, :768] = R.dqkv[...].astype(BF16)
+    R.c_qkv[...] = dot_tn(R.normed[...], R.dproj[:, :768])
+    d_normed = dot_nt(R.dproj[...], R.w_qkvg[...])
     hat, rstd = norm(R.xc[...], -1)
-    normed = (hat * R.g1[...]).astype(BF16)
-    R.g_qkvg[...] = dot_tn(normed, R.dproj[...])
-    d_normed = dot_nt(R.dproj[...], R.w_qkvg[...])
-    R.gg1[...] = jnp.sum(d_normed * hat, 0, keepdims=True)
     R.dlater[...] += norm_back(d_normed, R.g1[...], hat, rstd, -1)
     group_columns(R, R.dlater, R.gsend)
 
@@ -1324,7 +1399,8 @@
     R.wait_value = start_columns(D, R.osend, R.orecv)
 
 
-def p_take_value(R, D):
+def p_values(R, D):
+    p_send_value(R, D)
     R.wait_value()
     ungroup_columns(R.orecv, R.msa_out)
     R.leave("msa_out")
@@ -1334,9 +1410,6 @@
 
 SEGMENTS = (
     dict(
-        g_ti=(128, 640),
-        g_ii=(128, 640),
-        g_to=(128, 128),
         g_io=(128, 128),
         s_mean=(64, 256),
         s_own=(64, 256),
@@ -1347,8 +1420,10 @@
         g_ms=(64, 64),
         small0=(16, 128),
     ),
-    dict(g_oo=(1024, 128)),
-    dict(g_qkvg=(256, 1024), g_ao=(256, 256), g_oi=(64, 256), small1=(16, 128)),
+    dict(g_ii=(128, 640), g_to=(128, 128), small1=(16, 128)),
+    dict(g_ti=(128, 640), g_oo=(1024, 128), small2=(16, 128)),
+    dict(g_ao=(256, 256), c_gate=(256, 256), g_oi=(64, 256), small3=(16, 128)),
+    dict(c_qkv=(256, 768)),
 )
 
 
@@ -1425,39 +1500,58 @@
     place = hot_bf16(iota((32, 256), 1) == 32 * D.s + iota((32, 256), 0))
     first = jnp.where(D.r == 0, 1.0, 0.0)
     R.s_vadj[...] = dot_tn(R.adj_v[...].astype(BF16), place) * first
-    R.small[...] = jnp.zeros((128, LANES), F32)
-    for k, value in enumerate((R.gg3, R.gg4, R.gg5, R.gg6, R.g_ds, R.g_sl)):
-        R.small[0 : value.shape[0], k : k + 1] = value[...]
-    R.small0[...] = R.small[...].T[:16]
+    small_rows(R, R.small0, (R.gg6, R.g_ds, R.g_sl))
     R.sum0 = sum_segment(R, D, 0)
     next(R.sum0)
 
 
+def small_rows(R, target, values):
+    R.small[...] = jnp.zeros((128, LANES), F32)
+    for k, value in enumerate(values):
+        R.small[0 : value.shape[0], k : k + 1] = value[...]
+    target[...] = R.small[...].T[:16]
+
+
 def p_sum1(R, D):
+    small_rows(R, R.small1, (R.gg5, R.gg4))
     R.sum1 = sum_segment(R, D, 1)
     next(R.sum1)
 
 
 def p_sum2(R, D):
-    R.small1[...] = jnp.zeros((16, LANES), F32)
-    for k, value in enumerate((R.gg1, R.gg2)):
-        for half in range(2):
-            at = 2 * k + half
-            R.small1[at : at + 1, :] = value[:, LANES * half : LANES * half + LANES]
+    small_rows(R, R.small2, (R.gg3,))
     R.sum2 = sum_segment(R, D, 2)
     next(R.sum2)
 
 
+def p_sum3(R, D):
+    R.small3[...] = jnp.zeros((16, LANES), F32)
+    for half in range(2):
+        R.small3[half : half + 1, :] = R.gg2[:, LANES * half : LANES * half + LANES]
+    R.sum3 = sum_segment(R, D, 3)
+    next(R.sum3)
+
+
 def p_sums(R, D):
+    R.sum4 = sum_segment(R, D, 4)
+    next(R.sum4)
     wait = start_columns(D, R.gsend, R.grecv)
-    sums = [R.sum0, R.sum1, R.sum2]
-    while sums:
-        sums = [each for each in sums if next(each, D) is not D]
-        if wait:
-            wait()
-            ungroup_columns(R.grecv, R.msa_grad)
-            R.leave("msa_grad")
-            wait = None
+    next(R.sum1)
+    next(R.sum2)
+    next(R.sum3)
+    next(R.sum1, D)
+    next(R.sum2)
+    next(R.sum3)
+    wait()
+    ungroup_columns(R.grecv, R.msa_grad)
+    R.leave("msa_grad")
+    next(R.sum4)
+    next(R.sum2, D)
+    next(R.sum3)
+    next(R.sum4)
+    next(R.sum3, D)
+    next(R.sum4)
+    next(R.sum4, D)
 
 
 def unpack_segment(R, index):
@@ -1471,23 +1565,35 @@
     return {name: jnp.concatenate(parts, 1) for name, parts in held.items()}
 
 
-def p_finish_first(R, D):
-    unpack_segment(R, 1)
-    held = unpack_segment(R, 2)
-    small = held["small1"]
-    for k, target in enumerate((R.o_gg1, R.o_gg2)):
-        for half in range(2):
-            at = 2 * k + half
-            target[:, LANES * half : LANES * half + LANES] = small[at : at + 1]
-
-
 def p_finish(R, D):
+    R.arrived(1)
+    small = unpack_segment(R, 1)["small1"]
+    R.o_gg5[...] = small[0:1]
+    R.o_gg4[...] = small[1:2]
+    R.leave(R.o_g_ii)
+    R.arrived(2)
+    R.o_gg3[...] = unpack_segment(R, 2)["small2"][0:1]
+    R.leave(R.o_g_ti, R.o_g_oo)
+    R.arrived(3)
+    held = unpack_segment(R, 3)
+    R.leave(R.o_g_ao)
+    for half in range(2):
+        R.o_gg2[:, LANES * half : LANES * half + LANES] = held["small3"][half : half + 1]
+    R.o_g_qkvg[:, 768:] = held["c_gate"]
+    R.arrived(4)
+    R.o_g_qkvg[:, :768] = unpack_segment(R, 4)["c_qkv"]
+    R.leave(R.o_g_qkvg)
+    R.pass_on()
+    R.arrived(5)
+    total = jnp.sum(R.w_far[...].astype(F32) * R.o_g_qkvg[...], 1, keepdims=True)
+    eye = iota((256, 256), 0) == iota((256, 256), 1)
+    R.o_gg1[...] = jnp.sum(jnp.where(eye, total, 0.0), 0, keepdims=True) / R.g1[...]
+    R.arrived(0)
     held = unpack_segment(R, 0)
     small = held["small0"]
-    for k, target in enumerate((R.o_gg3, R.o_gg4, R.o_gg5, R.o_gg6)):
-        target[...] = small[k : k + 1, :]
-    R.o_g_ds[...] = small[4:5, :64]
-    R.o_g_sl[...] = small[5:6, :64]
+    R.o_gg6[...] = small[0:1]
+    R.o_g_ds[...] = small[1:2, :64]
+    R.o_g_sl[...] = small[2:3, :64]
     mean_b = held["s_mean"].astype(BF16)
     R.o_g_up[...] = dot_nt(mean_b, held["s_vadj"].astype(BF16))
     d_node = jnp.concatenate([held["s_own"], held["s_other"]], 0).astype(BF16)
@@ -1520,11 +1626,13 @@
     grecv=((8, 2, 16, 256), BF16),
     wst=((1024, 128), F32),
     lt=((32, 1024), BF16),
-    tm=((4, 256, 256), BF16),
+    tm=((2, 256, 256), F32),
     geo=((32, 2048), F32),
     pre=((128, 2048), F32),
     small0=((16, 128), F32),
     small1=((16, 128), F32),
+    small2=((16, 128), F32),
+    small3=((16, 128), F32),
     xc=((256, 256), F32),
     ac=((256, 256), F32),
     sp0=((256, 128), F32),
@@ -1564,7 +1672,7 @@
     dtri2=((640, 2048), BF16),
     mats1=((8, 256, 256), BF16),
     mats2=((8, 256, 256), BF16),
-    dm=((4, 256, 256), BF16),
+    dm=((2, 256, 256), BF16),
     lrs=((32, 128, 128), BF16),
     lr1r=((32, 128, 128), BF16),
     lr2r=((32, 128, 128), BF16),
@@ -1595,7 +1703,6 @@
     gg4=((128, 1), F32),
     gg5=((128, 1), F32),
     gg6=((128, 1), F32),
-    gg1=((1, 256), F32),
     gg2=((1, 256), F32),
     g_ds=((64, 1), F32),
     g_sl=((64, 1), F32),
@@ -1608,7 +1715,9 @@
     g_oo=((1024, 128), F32),
     g_oi=((64, 256), F32),
     g_ao=((256, 256), F32),
-    g_qkvg=((256, 1024), F32),
+    c_gate=((256, 256), F32),
+    c_qkv=((256, 768), F32),
+    normed=((256, 256), BF16),
     small=((128, 128), F32),
     dopm=((32, 64, 128), BF16),
     rt=((1024, 64), BF16),
@@ -1632,7 +1741,8 @@
 )
 LARGE = ("msa_out", "pair_out", "msa_grad", "pair_grad")
 MOVED_IN = ("adj_a", "w_qkvg", "w_ao", "w_oo", "w_ti", "w_ii", "pe", "adj_c")
-FINISH = ("vet", "w_up", "w_nd", "adj_v", "at", "adj_l")
+BIG = ("o_g_ii", "o_g_ti", "o_g_oo", "o_g_ao", "o_g_qkvg")
+FINISH = ("g1", "vet", "w_up", "w_nd", "adj_v", "at", "adj_l")
 FINISH_KEPT = dict(
     rows_f=((256, 128), F32), rows_g=((256, 128), F32), xyz=((128, 256), F32)
 )
@@ -1671,9 +1781,7 @@
     p_spread,
     p_attention,
     p_outer_exchange,
-    p_send_value,
     p_outer,
-    p_take_value,
     p_entry1,
     p_tri1,
     p_middle,
@@ -1686,11 +1794,9 @@
     p_outer_back,
     p_outer_return,
     p_attention_back,
-    p_sum2,
     p_sums,
 )
-PARTS = 4
-EXCHANGES = 16 + 8 * PARTS
+EXCHANGES = 56
 
 
 class Device:
@@ -1725,6 +1831,7 @@
     R.__dict__.update({name: refs.pop(0) for name in (*KEPT, *MOVED_IN, *LARGE)})
     tables = [[refs.pop(0) for _ in SIZES] for _ in range(6)]
     R.full, R.pay, R.parts = tables[0], tables[1], tables[2:]
+    R.waits, R.later = {}, {}
     R.out_send, R.out_recv, R.back_send, R.back_recv, R.move = refs[2:]
     D = Device(n_seq, n_res, refs[0], refs[1])
     barrier = pltpu.get_barrier_semaphore()
@@ -1760,26 +1867,44 @@
 
 def last_kernel(n_seq, n_res, names, *refs):
     refs = list(refs)
-    full = [refs.pop(0) for _ in SIZES]
-    near = [refs.pop(0) for _ in LARGE]
-    R = SimpleNamespace(**{name: refs.pop(0) for name in names[: len(FINISH)]}, full=full)
-    away = [refs.pop(0) for _ in LARGE]
-    *refs, sems = refs
-    held = refs[-len(LARGE) :]
-    R.__dict__.update(zip(names[len(FINISH) :], refs))
-
-    def move(index, source, target):
-        copy = pltpu.make_async_copy(source, target, sems.at[index])
+
+    def some(wanted):
+        return {name: refs.pop(0) for name in wanted}
+
+    far_in = [refs.pop(0) for _ in range(len(SIZES) + 1)]
+    far_large = some(LARGE)
+    R = SimpleNamespace(**some(FINISH))
+    away = some((*LARGE, *BIG))
+    R.__dict__.update(some(names))
+    R.__dict__.update(some((*FINISH_KEPT, *LARGE, *BIG)))
+    near_in = [refs.pop(0) for _ in far_in]
+    (sems,) = refs
+    R.full, R.w_far = near_in[:-1], near_in[-1]
+    used = []
+
+    def move(source, target):
+        copy = pltpu.make_async_copy(source, target, sems.at[len(used)])
         copy.start()
+        used.append(copy)
         return copy
 
-    coming = [move(k, near[k], held[k]) for k in range(len(LARGE))]
-    D = Device(n_seq, n_res, None, None)
-    p_finish_first(R, D)
-    for copy in coming:
-        copy.wait()
-    going = [move(len(LARGE) + k, held[k], away[k]) for k in range(len(LARGE))]
-    p_finish(R, D)
+    order = (1, 2, 3, 4, 5, 0)
+    coming = {k: move(far_in[k], near_in[k]) for k in order}
+    passing = [(name, move(far_large[name], getattr(R, name))) for name in LARGE]
+    going = []
+
+    def leave(*values):
+        for name in BIG:
+            if any(getattr(R, name) is value for value in values):
+                going.append(move(getattr(R, name), away[name]))
+
+    def pass_on():
+        for name, copy in passing:
+            copy.wait()
+            going.append(move(getattr(R, name), away[name]))
+
+    R.arrived, R.leave, R.pass_on = lambda k: coming[k].wait(), leave, pass_on
+    p_finish(R, Device(n_seq, n_res, None, None))
     for copy in going:
         copy.wait()
 
@@ -1854,18 +1979,21 @@
     )(*env.values())
     full = values[len(large) :]
     env.update(zip(large, values))
-    small = {name: entry for name, entry in RESULTS.items() if name not in large}
+    apart = {name: RESULTS[name] for name in (*LARGE, *BIG)}
+    small = {name: entry for name, entry in RESULTS.items() if name not in apart}
+    brought = [*PAYLOADS, (ARGS["w_qkvg"], BF16)]
     values = pl.pallas_call(
-        functools.partial(last_kernel, n_seq, n_res, (*FINISH, *small, *FINISH_KEPT)),
-        out_shape=shapes((*large.values(), *small.values())),
-        in_specs=[space] * len(full) + [anywhere] * len(LARGE) + [space] * len(FINISH),
-        out_specs=[anywhere] * len(LARGE) + [space] * len(small),
-        scratch_shapes=[pltpu.VMEM(*entry) for entry in FINISH_KEPT.values()]
-        + [pltpu.VMEM(*RESULTS[name]) for name in LARGE]
-        + [pltpu.SemaphoreType.DMA((2 * len(LARGE),))],
+        functools.partial(last_kernel, n_seq, n_res, tuple(small)),
+        out_shape=shapes((*apart.values(), *small.values())),
+        in_specs=[anywhere] * (len(brought) + len(LARGE)) + [space] * len(FINISH),
+        out_specs=[anywhere] * len(apart) + [space] * len(small),
+        scratch_shapes=[
+            pltpu.VMEM(*entry) for entry in (*FINISH_KEPT.values(), *apart.values(), *brought)
+        ]
+        + [pltpu.SemaphoreType.DMA((len(brought) + len(apart) + len(LARGE),))],
         compiler_params=pltpu.CompilerParams(vmem_limit_bytes=60 * 2**20),
-    )(*full, *[env[name] for name in LARGE], *[env[name] for name in FINISH])
-    env.update(zip((*large, *small), values))
+    )(*full, env["w_qkvg"], *[env[name] for name in LARGE], *[env[name] for name in FINISH])
+    env.update(zip((*apart, *small), values))
     results = [env[name] for name in RESULTS]
     for index, value in enumerate(results):
         if value.shape[0] == 1:

time: 264 us -> 239 us (0.905)
  Pallas kernels: 263 us -> 238 us
    pallas_call x1, Pallas kernels: 257 us -> 232 us  [fast_shards(): pl.pallas_call(functools.partial(first_kernel, n_seq, n_res, (*env, *larg...]
where the time goes in v4:
time: 239 us
  Pallas kernels  238 us (100%)
    pallas_call x1, Pallas kernels, fast_shards(): pl.pallas_call(functools.partial(first_kernel, n_seq, n_res, (*env, *larg...  232 us
    pallas_call x1, Pallas kernels, fast_shards(): pl.pallas_call(functools.partial(last_kernel, n_seq, n_res, tuple(small))...  5.82 us

profile of v4, /device:TPU:1, one launch (start us, length us, event | category | flops | bytes accessed | tf_op | source)
XLA Modules:
  0.0 238.8 jit_solution(11375676063668743728)
XLA Ops:
  0.7 232.1 %shard_map.501 = (bf16[4,64,256]{2,1,0:T(8,128)(2,1)}, bf16[32,64,128]{2,1,0:T(8,128)(2,1)}, f32[4,64,256]{2,1,0:T(8,128)}, f32[32,64,128]{2,1,0:T(8,128)}, bf16...) custom-call(bf16[4,64,256]{2,1,0:T(8,128)(2,1)} %refs_0_.1, ...), custom_call_target="tpu_custom_call" | custom-call | tf_op jit(solution)/shard_map/pallas_call | solution.py:1965
  232.8 5.8 %shard_map.502 = (bf16[4,64,256]{2,1,0:T(8,128)(2,1)}, bf16[32,64,128]{2,1,0:T(8,128)(2,1)}, f32[4,64,256]{2,1,0:T(8,128)}, f32[32,64,128]{2,1,0:T(8,128)}, f32[...) custom-call(bf16[1024,128]{1,0:T(8,128)(2,1)} %get-tuple-element.65., ...), custom_call_target="tpu_custom_call" | custom-call | tf_op jit(solution)/shard_map/pallas_call | solution.py:1985

commit v5 on v4

--- a/solution.py
+++ b/solution.py
@@ -539,6 +539,14 @@
     return D.s, lax.rem(D.r + t, D.nr)
 
 
+def sibling(D, t):
+    return D.s + 1 - 2 * (D.s % 2), D.r
+
+
+def chip_peers(D, t):
+    return lax.rem(D.s + 2 * t, D.ns), D.r
+
+
 def remote(src, dst, send, recv, peer):
     return pltpu.make_async_remote_copy(
         src_ref=src,
@@ -914,6 +922,7 @@
 
 def tri_backward(R, D, recv, mats, back, products, meanwhile):
     meanwhile(R, D)
+    advance(R, D)
     for pair in range(2):
         R.waits[0, pair]()
         R.waits[1, pair]()
@@ -924,8 +933,11 @@
                 R.tm[c] = products[k](mats[at], mats[4 + at], R.dm[c])
             scatter_pair(R.tm, R.lrs, pair, k)
         send_part(D, R.lrs, back, R.later, 0, pair)
+        if not pair:
+            advance(R, D)
     for pair in range(2):
         send_part(D, R.lrs, back, R.later, 1, pair)
+    advance(R, D)
 
 
 def p_tri1(R, D):
@@ -1133,7 +1145,6 @@
     gain5 = column(R.g5[...])
     R.a_g4[...] = jnp.zeros((128, CHUNK), F32)
     R.a_g5[...] = jnp.zeros((128, CHUNK), F32)
-    next(R.sum0)
 
     def chunk(j):
         here = chunk_at(j)
@@ -1167,7 +1178,6 @@
     R.gg5[...] = jnp.sum(R.a_g5[...], 1, keepdims=True)
     R.gg4[...] = jnp.sum(R.a_g4[...], 1, keepdims=True)
     p_sum1(R, D)
-    next(R.sum0)
 
 
 def p_back1(R, D):
@@ -1183,8 +1193,6 @@
 
 
 def p_pair_end(R, D):
-    next(R.sum0)
-    next(R.sum1)
     gain3 = column(R.g3[...])
     R.a_g3[...] = jnp.zeros((128, CHUNK), F32)
     inverse = 1.0 / count_of(R)
@@ -1209,6 +1217,8 @@
         wait_half(R.later, half)
         stage_both(R, R.dlr1r, half)
         pl.loop(4 * half, 4 * half + 4, unroll=4)(chunk)
+        if not half:
+            advance(R, D)
     R.leave("pair_grad")
 
 
@@ -1291,9 +1301,8 @@
     R.drr[D.s] = R.dright[pl.ds(pl.multiple_of(8 * D.s, 8), 8), :]
     p_pair_grads(R, D)
     p_outer_grads(R, D)
+    advance(R, D)
     p_sum2(R, D)
-    next(R.sum0, D)
-    next(R.sum1)
 
     for q in range(4):
         mine = (4 * (D.s % 2) + q == D.s) & (column_res == D.r)
@@ -1346,9 +1355,9 @@
     hat, rstd = norm(R.xc[...], -1)
     R.normed[...] = (hat * R.g1[...]).astype(BF16)
     R.c_gate[...] = dot_tn(R.normed[...], R.dproj[:, 768:])
+    advance(R, D)
     p_sum3(R, D)
     R.dqkv[...] = jnp.zeros((256, 768), F32)
-    next(R.sum2)
 
     @pl.loop(0, 8, unroll=4)
     def _(head):
@@ -1454,25 +1463,29 @@
 
 def sum_segment(R, D, index):
     pay, full = R.pay[index], R.full[index]
-    first, second, third, fourth = (table[index] for table in R.parts)
-    eighth = pay.shape[0] // 8
+    first, second, third, fourth, fifth, sixth = (table[index] for table in R.parts)
+    half = pay.shape[0] // 2
+    eighth = half // 4
     part = eighth // 4
+    core, chip = D.s % 2, D.s // 2
+    place = core * 4 + chip
     pack_segment(R, index)
-    first[D.s] = pay[rows_of(D.s, eighth), :]
-    most = pl.ds(0, eighth * (D.ns - 1))
-    wait = start_seq(
-        D, lambda i: pay.at[rows_of(i, eighth)], lambda i: first.at[i], pay.at[most]
-    )
+    theirs = pay.at[rows_of(1 - core, half)]
+    wait = swap(D, lambda i: theirs, lambda i: first, 2, sibling, lambda ps, pr: 0, 0, first)
     yield
     wait()
-    total = first[0].astype(F32)
-    for k in range(1, 8):
-        total += first[k].astype(F32)
+    total = pay[rows_of(core, half), :].astype(F32) + first[...].astype(F32)
     second[...] = total.astype(BF16)
-    third[D.r] = second[rows_of(D.r, part), :]
-    some = pl.ds(0, part * (D.nr - 1))
-    wait = start_res(
-        D, lambda i: second.at[rows_of(i, part)], lambda i: third.at[i], second.at[some]
+    third[chip] = second[rows_of(chip, eighth), :]
+    wait = swap(
+        D,
+        lambda i: second.at[rows_of(i, eighth)],
+        lambda i: third.at[i],
+        4,
+        chip_peers,
+        lambda ps, pr: ps // 2,
+        chip,
+        second.at[pl.ds(0, 3 * eighth)],
     )
     yield
     wait()
@@ -1480,20 +1493,42 @@
     for k in range(1, 4):
         total += third[k].astype(F32)
     fourth[...] = total.astype(BF16)
-    mine = pl.ds(pl.multiple_of(D.s * eighth + D.r * part, part), part)
-    full[mine, :] = fourth[...]
-    wait = start_res(D, lambda i: fourth, lambda i: full.at[mine], full.at[some])
+    fifth[D.r] = fourth[rows_of(D.r, part), :]
+    some = pl.ds(0, part * (D.nr - 1))
+    wait = start_res(
+        D, lambda i: fourth.at[rows_of(i, part)], lambda i: fifth.at[i], fourth.at[some]
+    )
     yield
     wait()
-    wait = start_seq(
-        D,
-        lambda i: full.at[rows_of(D.s, eighth)],
-        lambda i: full.at[rows_of(i, eighth)],
-        full.at[most],
-    )
+    total = fifth[0].astype(F32)
+    for k in range(1, 4):
+        total += fifth[k].astype(F32)
+    sixth[...] = total.astype(BF16)
+    mine = pl.ds(pl.multiple_of(place * eighth + D.r * part, part), part)
+    full[mine, :] = sixth[...]
+    wait = start_res(D, lambda i: sixth, lambda i: full.at[mine], full.at[some])
+    yield
+    wait()
+    mine = full.at[rows_of(place, eighth)]
+    most = full.at[pl.ds(0, 3 * eighth)]
+    wait = swap(D, lambda i: mine, lambda i: mine, 4, chip_peers, lambda ps, pr: 0, 0, most)
+    yield
+    wait()
+    mine = full.at[rows_of(core, half)]
+    wait = swap(D, lambda i: mine, lambda i: mine, 2, sibling, lambda ps, pr: 0, 0, first)
     yield
     wait()
     R.leave(index)
+
+
+def advance(R, D):
+    R.chains = [chain for chain in R.chains if next(chain, D) is not D]
+
+
+def begin(R, D, index):
+    chain = sum_segment(R, D, index)
+    next(chain)
+    R.chains.append(chain)
 
 
 def p_sum0(R, D):
@@ -1501,8 +1536,7 @@
     first = jnp.where(D.r == 0, 1.0, 0.0)
     R.s_vadj[...] = dot_tn(R.adj_v[...].astype(BF16), place) * first
     small_rows(R, R.small0, (R.gg6, R.g_ds, R.g_sl))
-    R.sum0 = sum_segment(R, D, 0)
-    next(R.sum0)
+    begin(R, D, 0)
 
 
 def small_rows(R, target, values):
@@ -1514,44 +1548,31 @@
 
 def p_sum1(R, D):
     small_rows(R, R.small1, (R.gg5, R.gg4))
-    R.sum1 = sum_segment(R, D, 1)
-    next(R.sum1)
+    begin(R, D, 1)
 
 
 def p_sum2(R, D):
     small_rows(R, R.small2, (R.gg3,))
-    R.sum2 = sum_segment(R, D, 2)
-    next(R.sum2)
+    begin(R, D, 2)
 
 
 def p_sum3(R, D):
     R.small3[...] = jnp.zeros((16, LANES), F32)
     for half in range(2):
         R.small3[half : half + 1, :] = R.gg2[:, LANES * half : LANES * half + LANES]
-    R.sum3 = sum_segment(R, D, 3)
-    next(R.sum3)
+    begin(R, D, 3)
 
 
 def p_sums(R, D):
-    R.sum4 = sum_segment(R, D, 4)
-    next(R.sum4)
     wait = start_columns(D, R.gsend, R.grecv)
-    next(R.sum1)
-    next(R.sum2)
-    next(R.sum3)
-    next(R.sum1, D)
-    next(R.sum2)
-    next(R.sum3)
+    advance(R, D)
+    begin(R, D, 4)
+    advance(R, D)
     wait()
     ungroup_columns(R.grecv, R.msa_grad)
     R.leave("msa_grad")
-    next(R.sum4)
-    next(R.sum2, D)
-    next(R.sum3)
-    next(R.sum4)
-    next(R.sum3, D)
-    next(R.sum4)
-    next(R.sum4, D)
+    while R.chains:
+        advance(R, D)
 
 
 def unpack_segment(R, index):
@@ -1734,7 +1755,9 @@
 SIZES = [segment_layout(index)[1] for index in range(len(SEGMENTS))]
 PAYLOADS = [((size, 128), BF16) for size in SIZES]
 PARTIAL = (
-    [((8, size // 8, 128), BF16) for size in SIZES]
+    [((size // 2, 128), BF16) for size in SIZES]
+    + [((size // 2, 128), BF16) for size in SIZES]
+    + [((4, size // 8, 128), BF16) for size in SIZES]
     + [((size // 8, 128), BF16) for size in SIZES]
     + [((4, size // 32, 128), BF16) for size in SIZES]
     + [((size // 32, 128), BF16) for size in SIZES]
@@ -1796,7 +1819,7 @@
     p_attention_back,
     p_sums,
 )
-EXCHANGES = 56
+EXCHANGES = 66
 
 
 class Device:
@@ -1829,9 +1852,9 @@
     far_full = [refs.pop(0) for _ in SIZES]
     R = SimpleNamespace(**far)
     R.__dict__.update({name: refs.pop(0) for name in (*KEPT, *MOVED_IN, *LARGE)})
-    tables = [[refs.pop(0) for _ in SIZES] for _ in range(6)]
+    tables = [[refs.pop(0) for _ in SIZES] for _ in range(8)]
     R.full, R.pay, R.parts = tables[0], tables[1], tables[2:]
-    R.waits, R.later = {}, {}
+    R.waits, R.later, R.chains = {}, {}, []
     R.out_send, R.out_recv, R.back_send, R.back_recv, R.move = refs[2:]
     D = Device(n_seq, n_res, refs[0], refs[1])
     barrier = pltpu.get_barrier_semaphore()

time: 239 us -> 232 us (0.971)
  Pallas kernels: 238 us -> 231 us
    pallas_call x1, Pallas kernels: 232 us -> 225 us  [fast_shards(): pl.pallas_call(functools.partial(first_kernel, n_seq, n_res, (*env, *larg...]
where the time goes in v5:
time: 232 us; the launch traced here: 231 us
  Pallas kernels  231 us (100%)
    pallas_call x1, Pallas kernels, fast_shards(): pl.pallas_call(functools.partial(first_kernel, n_seq, n_res, (*env, *larg...  225 us
    pallas_call x1, Pallas kernels, fast_shards(): pl.pallas_call(functools.partial(last_kernel, n_seq, n_res, tuple(small))...  5.82 us

profile of v5, /device:TPU:1, one launch (start us, length us, event | category | flops | bytes accessed | tf_op | source)
XLA Modules:
  0.0 231.4 jit_solution(9949679436984932083)
XLA Ops:
  0.7 224.7 %shard_map.501 = (bf16[4,64,256]{2,1,0:T(8,128)(2,1)}, bf16[32,64,128]{2,1,0:T(8,128)(2,1)}, f32[4,64,256]{2,1,0:T(8,128)}, f32[32,64,128]{2,1,0:T(8,128)}, bf16...) custom-call(bf16[4,64,256]{2,1,0:T(8,128)(2,1)} %refs_0_.1, ...), custom_call_target="tpu_custom_call" | custom-call | tf_op jit(solution)/shard_map/pallas_call | solution.py:1988
  225.4 5.8 %shard_map.502 = (bf16[4,64,256]{2,1,0:T(8,128)(2,1)}, bf16[32,64,128]{2,1,0:T(8,128)(2,1)}, f32[4,64,256]{2,1,0:T(8,128)}, f32[32,64,128]{2,1,0:T(8,128)}, f32[...) custom-call(bf16[1024,128]{1,0:T(8,128)(2,1)} %get-tuple-element.65., ...), custom_call_target="tpu_custom_call" | custom-call | tf_op jit(solution)/shard_map/pallas_call | solution.py:2008

commit v6 on v5

--- a/solution.py
+++ b/solution.py
@@ -751,14 +751,21 @@
         R.l2[256 * q : 256 * q + 256, :] = wide.T[:, :32].astype(BF16)
         R.lt[:, 256 * q : 256 * q + 256] = R.lall[q]
 
-    @pl.loop(0, 8)
+
+def outer_left(R, half):
+    left = jnp.concatenate(
+        [R.l2[256 * (2 * h + half) : 256 * (2 * h + half) + 256, :] for h in range(2)], 0
+    )
+
+    @pl.loop(0, 8, unroll=2)
     def _(e):
         weights = jnp.concatenate([outer_weight(R, 4 * e + u) for u in range(4)], 1)
-        part = dot_nn(R.l2[...], weights).astype(BF16)
+        part = dot_nn(left, weights).astype(BF16)
         for u in range(4):
             at = pl.ds(pl.multiple_of(32 * (4 * e + u), 32), 32)
-            for i in range(32):
-                R.zb[i, at, :] = part[32 * i : 32 * i + 32, LANES * u : LANES * u + LANES]
+            for i in range(16):
+                row = 16 * (i // 8) + 8 * half + i % 8
+                R.zb[row, at, :] = part[32 * i : 32 * i + 32, LANES * u : LANES * u + LANES]
 
 
 def outer_rows(R, half):
@@ -850,6 +857,7 @@
 def p_entry1(R, D):
     gain = column(R.g3[...])
     for half in range(2):
+        outer_left(R, half)
         outer_rows(R, half)
 
         @pl.loop(4 * half, 4 * half + 4, unroll=4)
@@ -1219,6 +1227,9 @@
         pl.loop(4 * half, 4 * half + 4, unroll=4)(chunk)
         if not half:
             advance(R, D)
+            R.rt[...] = R.rall[...].T.astype(BF16)
+            R.dright[...] = jnp.zeros((64, 1024), F32)
+            outer_right_back(R, 0)
     R.leave("pair_grad")
 
 
@@ -1227,15 +1238,23 @@
     R.gg3[...] = jnp.sum(R.a_g3[...], 1, keepdims=True)
 
 
+def outer_right_back(R, half):
+    @pl.loop(0, 2)
+    def _(h):
+        first = 16 * h + 8 * half
+        grad = jnp.concatenate([R.dopm[first + u] for u in range(8)], 1)
+        R.dright[...] += dot_nt(grad, jnp.concatenate([R.zb[first + u] for u in range(8)], 1))
+
+
 def p_outer_back(R, D):
-    R.rt[...] = R.rall[...].T.astype(BF16)
-    R.dright[...] = jnp.zeros((64, 1024), F32)
+    outer_right_back(R, 1)
+
+    @pl.loop(1, 8)
+    def _(t):
+        right_return(R, D, t).start()
+
+    R.drr[D.s] = R.dright[pl.ds(pl.multiple_of(8 * D.s, 8), 8), :]
     R.dleft[...] = jnp.zeros((32, 1024), F32)
-
-    @pl.loop(0, 4)
-    def _(k):
-        grad = jnp.concatenate([R.dopm[8 * k + u] for u in range(8)], 1)
-        R.dright[...] += dot_nt(grad, jnp.concatenate([R.zb[8 * k + u] for u in range(8)], 1))
 
     @pl.loop(0, 4)
     def _(g):
@@ -1258,6 +1277,13 @@
         R.dls[q] = R.dleft[:, 256 * q : 256 * q + 256].astype(BF16)
 
 
+def right_return(R, D, t):
+    peer = seq_peers(D, t)
+    at = pl.ds(pl.multiple_of(8 * peer[0], 8), 8)
+    sems = R.back_send.at[4 + t], R.back_recv.at[4 + t]
+    return remote(R.dright.at[at], R.drr.at[D.s], *sems, peer)
+
+
 def p_outer_grads(R, D):
     @pl.loop(0, 4)
     def _(g):
@@ -1289,16 +1315,6 @@
         def _():
             R.dlr[D.r] = R.dls[q]
 
-    def right(t):
-        peer = seq_peers(D, t)
-        at = pl.ds(pl.multiple_of(8 * peer[0], 8), 8)
-        return remote(R.dright.at[at], R.drr.at[D.s], send.at[4 + t], recv.at[4 + t], peer)
-
-    @pl.loop(1, 8)
-    def _(t):
-        right(t).start()
-
-    R.drr[D.s] = R.dright[pl.ds(pl.multiple_of(8 * D.s, 8), 8), :]
     p_pair_grads(R, D)
     p_outer_grads(R, D)
     advance(R, D)
@@ -1318,7 +1334,7 @@
 
     @pl.loop(1, 8)
     def _(t):
-        right(t).wait()
+        right_return(R, D, t).wait()
 
 
 def p_attention_back(R, D):
@@ -1377,6 +1393,7 @@
 
     R.dproj[:, :768] = R.dqkv[...].astype(BF16)
     R.c_qkv[...] = dot_tn(R.normed[...], R.dproj[:, :768])
+    begin(R, D, 4)
     d_normed = dot_nt(R.dproj[...], R.w_qkvg[...])
     hat, rstd = norm(R.xc[...], -1)
     R.dlater[...] += norm_back(d_normed, R.g1[...], hat, rstd, -1)
@@ -1566,7 +1583,6 @@
 def p_sums(R, D):
     wait = start_columns(D, R.gsend, R.grecv)
     advance(R, D)
-    begin(R, D, 4)
     advance(R, D)
     wait()
     ungroup_columns(R.grecv, R.msa_grad)

time: 232 us -> 225 us (0.970)
  Pallas kernels: 231 us -> 223 us
    pallas_call x1, Pallas kernels: 225 us -> 218 us  [fast_shards(): pl.pallas_call(functools.partial(first_kernel, n_seq, n_res, (*env, *larg...]
where the time goes in v6:
time: 225 us; the launch traced here: 224 us
  Pallas kernels  223 us (99%)
    pallas_call x1, Pallas kernels, fast_shards(): pl.pallas_call(functools.partial(first_kernel, n_seq, n_res, (*env, *larg...  218 us
    pallas_call x1, Pallas kernels, fast_shards(): pl.pallas_call(functools.partial(last_kernel, n_seq, n_res, tuple(small))...  5.82 us

profile of v6, /device:TPU:1, one launch (start us, length us, event | category | flops | bytes accessed | tf_op | source)
XLA Modules:
  0.0 224.3 jit_solution(6741507728695682616)
XLA Ops:
  0.7 217.6 %shard_map.501 = (bf16[4,64,256]{2,1,0:T(8,128)(2,1)}, bf16[32,64,128]{2,1,0:T(8,128)(2,1)}, f32[4,64,256]{2,1,0:T(8,128)}, f32[32,64,128]{2,1,0:T(8,128)}, bf16...) custom-call(bf16[4,64,256]{2,1,0:T(8,128)(2,1)} %refs_0_.1, ...), custom_call_target="tpu_custom_call" | custom-call | tf_op jit(solution)/shard_map/pallas_call | solution.py:2004
  218.3 5.8 %shard_map.502 = (bf16[4,64,256]{2,1,0:T(8,128)(2,1)}, bf16[32,64,128]{2,1,0:T(8,128)(2,1)}, f32[4,64,256]{2,1,0:T(8,128)}, f32[32,64,128]{2,1,0:T(8,128)}, f32[...) custom-call(bf16[1024,128]{1,0:T(8,128)(2,1)} %get-tuple-element.65., ...), custom_call_target="tpu_custom_call" | custom-call | tf_op jit(solution)/shard_map/pallas_call | solution.py:2024
